TPU v7x, 32 devices: a whole 2x2x4 slice. The times are simulated.
32 devices in a mesh: wide: 8 (over y, x, core), narrow: 4 (over z).
Axes of the slice: x: 2, y: 2, z: 4, core: 2. Of those that a mesh axis runs over, the one named last changes fastest.
Arguments:
- tokens: bfloat16 [4096, 2048], P(('wide', 'narrow')), may hold values from -6 to 6
- out_grad: bfloat16 [4096, 2048], P(('wide', 'narrow')), may hold values from -6 to 6
- routes: int32 [4096, 4], P(('wide', 'narrow')), may hold values from 0 to 31, all different within a row; in each aligned block of 128 rows (0 to 127, 128 to 255, ...) at most 32 rows name the same one
- route_gates: float32 [4096, 4], P(('wide', 'narrow')), may hold values from 0.05 to 0.4
- expert_weights: bfloat16 [2048, 32, 2304], P('narrow', 'wide'), may hold values from -0.21875 to 0.21875
Outputs:
- layer_output: bfloat16 [4096, 2048], P(('wide', 'narrow'))
- token_grad: bfloat16 [4096, 2048], P(('wide', 'narrow'))
- gate_grad: float32 [4096, 4], P(('wide', 'narrow'))
- weight_grad: bfloat16 [2048, 32, 2304], P('narrow', 'wide')
Inputs may be any that keep to these rules, and one draw needn't show every extreme that they name: `routes`: each row names 4 different experts. Among the 128 tokens of one device no expert is named by more than 32 of them, and in every draw some device's tokens name some expert exactly 32 times.
All inputs are finite; a program needn't handle non-finite values.
Results may differ from a plain program's by a relative error of at most 0.0064.
Values may be sent and summed in bfloat16 or wider, within the bound.
No kernel may reach another device: no remote copies, remote signals or barrier semaphores. Data moves between devices by JAX's collectives and lax.ppermute only.
A program may use at most 192 MiB of HBM per device.

v0:
```python
import functools

import jax
import jax.numpy as jnp
from jax import lax
from jax.experimental import pallas as pl
from jax.experimental.pallas import tpu as pltpu
from jax.sharding import PartitionSpec as P

F32 = jnp.float32
BF16 = jnp.bfloat16
VMEM_LIMIT = 50 * 1024 * 1024
META = 128
PIECES = 4


def dot(a, b, dims):
    return lax.dot_general(a, b, (dims, ((), ())), preferred_element_type=F32)


def params():
    return pltpu.CompilerParams(vmem_limit_bytes=VMEM_LIMIT)


def whole(shape):
    return pl.BlockSpec(shape, lambda *_: (0,) * len(shape))


def after(x, *others):
    return lax.optimization_barrier((x, others))[0]


def shift(x, k):
    n = lax.axis_size("narrow")
    return lax.ppermute(x, "narrow", [(i, (i + k) % n) for i in range(n)])


def shift_pieces(x, k, pieces, first=()):
    rows = x.shape[0] // pieces
    moved, latest = [], first
    for i in range(pieces):
        moved.append(shift(after(x[i * rows : (i + 1) * rows], *latest), k))
        latest = moved[-1:]
    return jnp.concatenate(moved)


def shift_chain(blocks, sign, order, first=()):
    moved, latest = list(blocks), first
    for k in order:
        moved[k] = shift(after(blocks[k], *latest), sign * k)
        latest = [moved[k]]
    return moved


def hop(x, up, sources):
    step = 1 if up else -1
    return lax.ppermute(x, "narrow", [(i, i + step) for i in sources])


def reduce_chain(parts):
    n = len(parts)
    up = down = None
    for step in range(1, n):
        up_send, down_send = parts[step], parts[n - step]
        if up is not None:
            up_send = (up_send.astype(F32) + up.astype(F32)).astype(BF16)
            down_send = (down_send.astype(F32) + down.astype(F32)).astype(BF16)
        up = hop(up_send, True, range(step))
        down = hop(down_send, False, range(n - step, n))
    total = parts[0].astype(F32) + up.astype(F32) + down.astype(F32)
    return total.astype(BF16)


def mixing(level, n, depth):
    row = lax.broadcasted_iota(jnp.int32, (n * depth, n * depth), 0)
    column = lax.broadcasted_iota(jnp.int32, (n * depth, n * depth), 1)
    same = (row // n == column % depth) & (row % n == lax.rem(level + column // depth, n))
    return jnp.where(same, 1.0, 0.0).astype(BF16)


def split_kernel(n, level_ref, shard_ref, *out_refs):
    depth, _, columns = shard_ref.shape
    part = out_refs[0].shape[1]
    shard = shard_ref[...].reshape(depth * n, columns)
    apart = dot(mixing(level_ref[0], n, depth), shard, ((0,), (0,))).astype(BF16)
    for k in range(n):
        out_refs[k][...] = apart[k * depth : (k + 1) * depth, :part]
        out_refs[n + k][...] = apart[k * depth : (k + 1) * depth, part:]


def split_shard(level, shard, part):
    rows, n, columns = shard.shape
    depth = min(rows, 256 // n)
    rest = columns - part
    outs = pl.pallas_call(
        functools.partial(split_kernel, n),
        out_shape=[jax.ShapeDtypeStruct((rows, part), BF16)] * n
        + [jax.ShapeDtypeStruct((rows, rest), BF16)] * n,
        grid_spec=pltpu.PrefetchScalarGridSpec(
            num_scalar_prefetch=1,
            grid=(rows // depth,),
            in_specs=[pl.BlockSpec((depth, n, columns), lambda i, level: (i, 0, 0))],
            out_specs=[pl.BlockSpec((depth, part), lambda i, level: (i, 0))] * n
            + [pl.BlockSpec((depth, rest), lambda i, level: (i, 0))] * n,
        ),
        compiler_params=params(),
    )(level, shard)
    return outs[:n], outs[n:]


def join_kernel(n, level_ref, *refs):
    out_ref = refs[-1]
    depth, _, columns = out_ref.shape
    apart = jnp.concatenate([ref[...] for ref in refs[:n]], axis=0)
    mixed = dot(mixing(level_ref[0], n, depth), apart, ((1,), (0,)))
    out_ref[...] = mixed.astype(BF16).reshape(depth, n, columns)


def join_shard(level, blocks, columns, place, shard=None):
    n = len(blocks)
    rows, part = blocks[0].shape
    depth = min(rows, 256 // n)
    more = [] if shard is None else [shard]
    return pl.pallas_call(
        functools.partial(join_kernel, n),
        out_shape=jax.ShapeDtypeStruct((rows, n, columns), BF16),
        grid_spec=pltpu.PrefetchScalarGridSpec(
            num_scalar_prefetch=1,
            grid=(rows // depth,),
            in_specs=[pl.BlockSpec((depth, part), lambda i, level: (i, 0))] * n
            + [pl.BlockSpec(memory_space=pl.ANY)] * len(more),
            out_specs=pl.BlockSpec((depth, n, part), lambda i, level: (i, 0, place)),
        ),
        input_output_aliases={1 + n: 0} if more else {},
        compiler_params=params(),
    )(level, *blocks, *more)


def arrived(refs, n, d):
    return refs[0][...] if d == 0 else refs[d][...] + refs[n - 1 + n - d][...]


def slots_of(level, n, groups, chosen, capacity, meta):
    tokens = meta.shape[0]
    lines = jnp.transpose(meta.astype(F32))
    expert = lax.broadcasted_iota(jnp.int32, (groups, tokens), 0) * n + level
    expert = expert.astype(F32)
    named = [lines[k : k + 1] == expert for k in range(chosen)]
    gates = [
        lines[chosen + k : chosen + k + 1]
        + lines[2 * chosen + k : 2 * chosen + k + 1]
        + lines[3 * chosen + k : 3 * chosen + k + 1]
        for k in range(chosen)
    ]
    one = sum(jnp.where(x, 1.0, 0.0) for x in named)
    row = lax.broadcasted_iota(jnp.int32, (tokens, tokens), 0)
    column = lax.broadcasted_iota(jnp.int32, (tokens, tokens), 1)
    earlier = jnp.where(row < column, 1.0, 0.0).astype(BF16)
    rank = dot(one.astype(BF16), earlier, ((1,), (0,)))
    rank = jnp.where(one > 0.5, rank, -1.0).astype(jnp.int32)
    slot = lax.broadcasted_iota(jnp.int32, (groups, capacity, tokens), 1)
    return named, gates, rank[:, None, :] == slot


def gates_of(named, gates):
    return sum(jnp.where(name, gate, 0.0) for name, gate in zip(named, gates))


def dispatch_kernel(n, chosen, gated, level_ref, *refs):
    count = 2 * n - 1
    metas, blocks, out_ref = refs[:count], refs[count : 2 * count], refs[2 * count]
    groups, _, capacity, width = out_ref.shape
    for d in range(n):
        meta, x = arrived(metas, n, d), arrived(blocks, n, d)
        named, gates, taken = slots_of(level_ref[0], n, groups, chosen, capacity, meta)
        tokens = x.shape[0]
        matrix = jnp.where(taken, 1.0, 0.0).astype(BF16).reshape(groups * capacity, tokens)
        rows = dot(matrix, x, ((1,), (0,)))
        if gated:
            weight = jnp.where(taken, gates_of(named, gates)[:, None, :], 0.0)
            weight = jnp.sum(weight, axis=2, keepdims=True)
            rows = rows * weight.reshape(groups * capacity, 1)
        out_ref[:, d] = rows.astype(BF16).reshape(groups, capacity, width)


def rolled(n, tokens, width):
    return pl.BlockSpec((tokens, width), lambda k, level: (0, lax.rem(level[0] - k + n, n)))


def meta_spec(tokens, model):
    return pl.BlockSpec((tokens, META), lambda k, level: (0, model // META))


def dispatch(level, metas, *, blocks, groups, capacity, chosen, gated):
    n = (len(blocks) + 1) // 2
    tokens, model = blocks[0].shape[0], metas[0].shape[1] - META
    width = model // n
    return pl.pallas_call(
        functools.partial(dispatch_kernel, n, chosen, gated),
        out_shape=jax.ShapeDtypeStruct((groups, n, capacity, model), BF16),
        grid_spec=pltpu.PrefetchScalarGridSpec(
            num_scalar_prefetch=1,
            grid=(n,),
            in_specs=[meta_spec(tokens, model)] * len(metas)
            + [rolled(n, tokens, width)] * len(blocks),
            out_specs=pl.BlockSpec((groups, n, capacity, width), lambda k, level: (0, 0, 0, k)),
        ),
        compiler_params=params(),
    )(level, *metas, *blocks)


def combine_out_kernel(n, chosen, level_ref, *refs):
    count = 2 * n - 1
    metas, grads, back_ref = refs[:count], refs[count : 2 * count], refs[2 * count]
    out_refs, dots_ref = refs[2 * count + 1 : -1], refs[-1]
    groups, _, capacity, width = back_ref.shape
    for d in range(n):
        meta, grad = arrived(metas, n, d), arrived(grads, n, d)
        named, gates, taken = slots_of(level_ref[0], n, groups, chosen, capacity, meta)
        tokens = grad.shape[0]
        weight = jnp.where(taken, gates_of(named, gates)[:, None, :], 0.0)
        weight = weight.reshape(groups * capacity, tokens)
        high = weight.astype(BF16)
        low = (weight - high.astype(F32)).astype(BF16)
        rows = back_ref[:, d].reshape(groups * capacity, width)
        total = dot(high, rows, ((0,), (0,))) + dot(low, rows, ((0,), (0,)))
        out_refs[d][...] = total.astype(BF16)
        pairs = dot(rows, grad, ((1,), (1,))).reshape(groups, capacity, tokens)
        pairs = jnp.sum(jnp.where(taken, pairs, 0.0), axis=1)
        part = jnp.concatenate(
            [jnp.sum(jnp.where(name, pairs, 0.0), axis=0, keepdims=True) for name in named]
        )

        @pl.when(pl.program_id(0) == 0)
        def _():
            dots_ref[d] = part

        @pl.when(pl.program_id(0) > 0)
        def _():
            dots_ref[d] += part


def combine_grad_kernel(n, chosen, level_ref, *refs):
    count = 2 * n - 1
    metas, back_ref, out_refs = refs[:count], refs[count], refs[count + 1 :]
    groups, _, capacity, width = back_ref.shape
    for d in range(n):
        meta = arrived(metas, n, d)
        _, _, taken = slots_of(level_ref[0], n, groups, chosen, capacity, meta)
        matrix = jnp.where(taken, 1.0, 0.0).astype(BF16)
        matrix = matrix.reshape(groups * capacity, meta.shape[0])
        rows = back_ref[:, d].reshape(groups * capacity, width)
        out_refs[d][...] = dot(matrix, rows, ((0,), (0,))).astype(BF16)


def combine(level, metas, back, chosen, grads=None):
    groups, n, capacity, model = back.shape
    tokens = metas[0].shape[0]
    width = model // n
    x_spec = rolled(n, tokens, width)
    back_spec = pl.BlockSpec((groups, n, capacity, width), lambda k, level: (0, 0, 0, k))
    out_shape = [jax.ShapeDtypeStruct((tokens, model), BF16)] * n
    out_specs = [x_spec] * n
    in_specs = [meta_spec(tokens, model)] * len(metas)
    if grads is None:
        kernel, extra = combine_grad_kernel, []
    else:
        kernel, extra = combine_out_kernel, grads
        in_specs = in_specs + [x_spec] * len(grads)
        out_shape = out_shape + [jax.ShapeDtypeStruct((n, chosen, tokens), F32)]
        out_specs = out_specs + [whole((n, chosen, tokens))]
    return pl.pallas_call(
        functools.partial(kernel, n, chosen),
        out_shape=out_shape,
        grid_spec=pltpu.PrefetchScalarGridSpec(
            num_scalar_prefetch=1,
            grid=(n,),
            in_specs=in_specs + [back_spec],
            out_specs=out_specs,
        ),
        compiler_params=params(),
    )(level, *metas, *extra, back)


def hidden_kernel(count, *refs):
    rows_ref, weights, outs = refs[0], refs[1 : 1 + count], refs[1 + count :]
    hidden_ref, active_ref, slope_ref = outs
    width = weights[0].shape[0]
    units = hidden_ref.shape[1]
    pre = sum(
        dot(rows_ref[:, k * width : (k + 1) * width], weights[k][...], ((1,), (0,)))
        for k in range(count)
    )
    gate, up = pre[:, :units], pre[:, units:]
    sigmoid = jax.nn.sigmoid(gate)
    active = gate * sigmoid
    hidden_ref[...] = (active * up).astype(BF16)
    active_ref[...] = active
    slope_ref[...] = up * (sigmoid * (1.0 + gate * (1.0 - sigmoid)))


def hidden_pass(rows, weights, tile):
    slots, model = rows.shape
    units = weights[0].shape[1] // 2
    out_spec = pl.BlockSpec((tile, units), lambda i: (i, 0))
    return pl.pallas_call(
        functools.partial(hidden_kernel, len(weights)),
        out_shape=(
            jax.ShapeDtypeStruct((slots, units), BF16),
            jax.ShapeDtypeStruct((slots, units), F32),
            jax.ShapeDtypeStruct((slots, units), F32),
        ),
        grid=(slots // tile,),
        in_specs=[pl.BlockSpec((tile, model), lambda i: (i, 0))]
        + [whole(w.shape) for w in weights],
        out_specs=(out_spec, out_spec, out_spec),
        compiler_params=params(),
    )(rows, *weights)


def down_kernel(count, *refs):
    hidden_ref, cotangent_ref, active_ref, slope_ref = refs[:4]
    weights = refs[4 : 4 + count]
    out_ref, both_ref = refs[4 + count :]
    width = weights[0].shape[0]
    hidden = hidden_ref[...]
    units = hidden.shape[1]
    grad = None
    for k in range(count):
        weight = weights[k][...]
        out_ref[:, k * width : (k + 1) * width] = dot(hidden, weight, ((1,), (1,))).astype(BF16)
        part = dot(cotangent_ref[:, k * width : (k + 1) * width], weight, ((1,), (0,)))
        grad = part if grad is None else grad + part
    both_ref[:, :units] = (grad * slope_ref[...]).astype(BF16)
    both_ref[:, units:] = (grad * active_ref[...]).astype(BF16)


def down_pass(hidden, cotangent, active, slope, weights, tile):
    slots, model = cotangent.shape
    units = hidden.shape[1]
    unit_spec = pl.BlockSpec((tile, units), lambda i: (i, 0))
    model_spec = pl.BlockSpec((tile, model), lambda i: (i, 0))
    return pl.pallas_call(
        functools.partial(down_kernel, len(weights)),
        out_shape=(
            jax.ShapeDtypeStruct((slots, model), BF16),
            jax.ShapeDtypeStruct((slots, 2 * units), BF16),
        ),
        grid=(slots // tile,),
        in_specs=[unit_spec, model_spec, unit_spec, unit_spec]
        + [whole(w.shape) for w in weights],
        out_specs=(model_spec, pl.BlockSpec((tile, 2 * units), lambda i: (i, 0))),
        compiler_params=params(),
    )(hidden, cotangent, active, slope, *weights)


def row_grad_kernel(count, *refs):
    both_ref, weights, out_ref = refs[0], refs[1 : 1 + count], refs[1 + count]
    width = weights[0].shape[0]
    for k in range(count):
        out_ref[:, k * width : (k + 1) * width] = dot(
            both_ref[...], weights[k][...], ((1,), (1,))
        ).astype(BF16)


def row_grad_pass(both, weights, tile):
    slots, units = both.shape
    model = len(weights) * weights[0].shape[0]
    return pl.pallas_call(
        functools.partial(row_grad_kernel, len(weights)),
        out_shape=jax.ShapeDtypeStruct((slots, model), BF16),
        grid=(slots // tile,),
        in_specs=[pl.BlockSpec((tile, units), lambda i: (i, 0))]
        + [whole(w.shape) for w in weights],
        out_specs=pl.BlockSpec((tile, model), lambda i: (i, 0)),
        compiler_params=params(),
    )(both, *weights)


def weight_grad_kernel(rows_ref, parts_ref, out_ref):
    out_ref[...] = dot(rows_ref[...], parts_ref[...], ((0,), (0,))).astype(BF16)


def weight_grad(rows, parts, k, width):
    slots, columns = parts.shape
    tile = columns // 2 if columns % 256 == 0 else columns
    return pl.pallas_call(
        weight_grad_kernel,
        out_shape=jax.ShapeDtypeStruct((width, columns), BF16),
        grid=(columns // tile,),
        in_specs=[
            pl.BlockSpec((slots, width), lambda i: (0, k)),
            pl.BlockSpec((slots, tile), lambda i: (0, i)),
        ],
        out_specs=pl.BlockSpec((width, tile), lambda i: (0, i)),
        compiler_params=params(),
    )(rows, parts)


def on_device(tokens, out_grad, routes, route_gates, expert_weights):
    groups = lax.axis_size("wide")
    n = lax.axis_size("narrow")
    me = lax.axis_index("narrow")
    experts = groups * n
    token_count, model = tokens.shape
    chosen = routes.shape[1]
    capacity = 2 * chosen * token_count // experts
    slots = experts * capacity
    width = model // n
    units = expert_weights.shape[2] // 3
    level = me.astype(jnp.int32).reshape(1)
    tile = min(256, slots)

    high = route_gates.astype(BF16)
    rest = route_gates - high.astype(F32)
    middle = rest.astype(BF16)
    low = (rest - middle.astype(F32)).astype(BF16)
    pad = jnp.zeros((token_count, META - 4 * chosen), BF16)
    sent = jnp.concatenate([tokens, routes.astype(BF16), high, middle, low, pad], axis=1)
    in_blocks, down_blocks = split_shard(level, expert_weights, 2 * units)
    middle, others = n // 2, [k for k in range(1, n) if k != n // 2]

    def swap(x):
        return lax.all_to_all(x, "wide", split_axis=0, concat_axis=0, tiled=True)

    def as_slots(x):
        return x.reshape(groups, n, capacity, model)

    w_in = [in_blocks[0]] + [None] * (n - 1)
    token_up, token_down = [sent], [sent]
    stage = list(in_blocks)
    for step in range(1, n):
        up, down = token_up[-1], token_down[-1]
        if step > 1:
            up, down = after((up, down), *stage)
            k = others[step - 2]
            w_in[k] = shift(after(in_blocks[k], token_up[-1], token_down[-1], *stage), k)
            stage = [w_in[k]]
        token_up.append(hop(up, True, range(step - 1, n - 1)))
        token_down.append(hop(down, False, range(1, n - step + 1)))
    token_blocks = token_up + token_down[1:]
    stage = stage + [token_up[-1], token_down[-1]]

    place = functools.partial(
        dispatch, level, groups=groups, capacity=capacity, chosen=chosen
    )
    sent_rows = place(after(token_blocks, *stage), blocks=token_blocks, gated=False)
    w_in[middle] = shift_pieces(in_blocks[middle], middle, PIECES, stage)
    start = after(out_grad, *stage)
    grad_up, grad_down = [start], [start]
    for step in range(1, n):
        grad_up.append(hop(grad_up[-1], True, range(step - 1, n - 1)))
        grad_down.append(hop(grad_down[-1], False, range(1, n - step + 1)))
    grad_blocks = grad_up + grad_down[1:]
    rows_in = swap(sent_rows).reshape(slots, model)
    stage = [w_in[middle], grad_up[-1], grad_down[-1]]

    w_down = shift_chain(down_blocks, 1, others + [middle], stage)
    sent_grads = place(after(token_blocks, *stage), blocks=grad_blocks, gated=True)
    cotangent = swap(sent_grads).reshape(slots, model)
    hidden, active, slope = hidden_pass(rows_in, w_in, tile)
    down_grads = [weight_grad(cotangent, hidden, k, width) for k in range(n)]
    stage = w_down + down_grads

    hidden = after(hidden, *stage)
    down_grads = shift_chain(down_grads, -1, others + [middle], stage)
    expert_out, both = down_pass(hidden, cotangent, active, slope, w_down, tile)
    in_grads = [weight_grad(rows_in, both, k, width) for k in range(n)]
    both = after(both, *in_grads)
    row_grad = row_grad_pass(both, w_in, tile)
    back_out = swap(as_slots(expert_out))
    stage = down_grads + [back_out, row_grad]
    columns = 3 * units
    shard = join_shard(level, down_grads, columns, 2)

    in_grads[middle] = shift_pieces(in_grads[middle], -middle, PIECES, stage)
    back_grad = swap(as_slots(after(row_grad, *stage)))
    back_out = after(back_out, *stage)
    *out_parts, dots = combine(level, token_blocks, back_out, chosen, grad_blocks)
    layer_output = reduce_chain(out_parts)
    stage = [in_grads[middle], layer_output, back_grad]
    for k in others:
        in_grads[k] = shift_pieces(in_grads[k], -k, PIECES // 2, stage)
        stage = [in_grads[k]]
    grad_parts = combine(level, token_blocks, after(back_grad, shard, layer_output), chosen)
    token_grad = reduce_chain(grad_parts)
    gate_grad = dots[0] + sum(shift(dots[d], -d) for d in range(1, n))

    shard = join_shard(level, in_grads, columns, 0, shard)
    return (layer_output, token_grad, gate_grad.T, shard)


def solution(mesh):
    return jax.shard_map(
        on_device,
        mesh=mesh,
        in_specs=(
            P(("wide", "narrow"), None),
            P(("wide", "narrow"), None),
            P(("wide", "narrow"), None),
            P(("wide", "narrow"), None),
            P("narrow", "wide", None),
        ),
        out_specs=(
            P(("wide", "narrow"), None),
            P(("wide", "narrow"), None),
            P(("wide", "narrow"), None),
            P("narrow", "wide", None),
        ),
        check_vma=False,
    )
```

profile of v0, /device:TPU:0, one launch (start us, length us, event | category | flops | bytes accessed | tf_op | source)
XLA Modules:
  0.0 653.1 jit_solution(12201867603210960801)
XLA Ops:
  5.1 5.6 collective-permute-start
  10.7 10.1 %shard_map.84 = (bf16[512,1536]{1,0:T(8,128)(2,1)}, bf16[512,1536]{1,0:T(8,128)(2,1)}, bf16[512,1536]{1,0:T(8,128)(2,1)}, bf16[512,1536]{1,0:T(8,128)(2,1)}, bf1...) custom-call(s32[1]{0:T(128)} %bitcast.level_ref, ...), custom_call_target="tpu_custom_call" | custom-call | tf_op jit(solution)/shard_map/pallas_call | solution.py:95
  27.6 45.8 %collective-permute-done.3.refs_5_.refs_12_ = bf16[128,2176]{1,0:T(8,128)(2,1)S(1)} collective-permute-done((bf16[128,2176]{1,0:T(8,128)(2,1)S(1)}, bf16[128,2176]{1,0:T(8,128)(2,1)S(1)}, u32[]{:S(2)}, u32[]{:S(2)}) %collective-permute-start.3) | collective-permute-done | bytes 557088 | tf_op jit(solution)/shard_map/ppermute | solution.py:57
  76.4 45.4 %collective-permute-done.6.refs_6_.refs_13_ = bf16[128,2176]{1,0:T(8,128)(2,1)S(1)} collective-permute-done((bf16[128,2176]{1,0:T(8,128)(2,1)S(1)}, bf16[128,2176]{1,0:T(8,128)(2,1)S(1)}, u32[]{:S(2)}, u32[]{:S(2)}) %collective-permute-start.6) | collective-permute-done | bytes 557088 | tf_op jit(solution)/shard_map/ppermute | solution.py:57
  121.8 5.9 shard_map.85
  142.1 13.7 %collective-permute-done.14 = bf16[128,1536]{1,0:T(8,128)(2,1)S(1)} collective-permute-done((bf16[128,1536]{1,0:T(8,128)(2,1)S(1)}, bf16[128,1536]{1,0:T(8,128)(2,1)S(1)}, u32[]{:S(2)}, u32[]{:S(2)}) %collective-permute-start.14) | collective-permute-done | bytes 393248 | tf_op jit(solution)/shard_map/ppermute | solution.py:35
  162.6 21.3 %collective-permute-done.15 = bf16[128,1536]{1,0:T(8,128)(2,1)S(1)} collective-permute-done((bf16[128,1536]{1,0:T(8,128)(2,1)S(1)}, bf16[128,1536]{1,0:T(8,128)(2,1)S(1)}, u32[]{:S(2)}, u32[]{:S(2)}) %collective-permute-start.15) | collective-permute-done | bytes 393248 | tf_op jit(solution)/shard_map/ppermute | solution.py:35
  184.0 11.1 %collective-permute-done.12.refs_12_ = bf16[128,2048]{1,0:T(8,128)(2,1)S(1)} collective-permute-done((bf16[128,2048]{1,0:T(8,128)(2,1)S(1)}, bf16[128,2048]{1,0:T(8,128)(2,1)S(1)}, u32[]{:S(2)}, u32[]{:S(2)}) %collective-permute-start.12) | collective-permute-done | bytes 524320 | tf_op jit(solution)/shard_map/ppermute | solution.py:57
  197.1 15.0 %collective-permute-done.16 = bf16[128,1536]{1,0:T(8,128)(2,1)S(1)} collective-permute-done((bf16[128,1536]{1,0:T(8,128)(2,1)S(1)}, bf16[128,1536]{1,0:T(8,128)(2,1)S(1)}, u32[]{:S(2)}, u32[]{:S(2)}) %collective-permute-start.16) | collective-permute-done | bytes 393248 | tf_op jit(solution)/shard_map/ppermute | solution.py:35
  212.2 19.3 %collective-permute-done.17 = bf16[128,1536]{1,0:T(8,128)(2,1)S(1)} collective-permute-done((bf16[128,1536]{1,0:T(8,128)(2,1)S(1)}, bf16[128,1536]{1,0:T(8,128)(2,1)S(1)}, u32[]{:S(2)}, u32[]{:S(2)}) %collective-permute-start.17) | collective-permute-done | bytes 393248 | tf_op jit(solution)/shard_map/ppermute | solution.py:35
  232.8 6.7 %shard_map.87 = bf16[8,4,32,2048]{3,2,1,0:T(8,128)(2,1)} custom-call(s32[1]{0:T(128)} %bitcast.level_ref, bf16[128,2176]{1,0:T(8,128)(2,1)} %copy-done.1, bf16[128,2176]{1,0:T(8,128)(2,1)} %copy-done.4, bf16[128,2176]{1,0:T(8,128)(2,1)} %copy-done.6, bf16[128,2176]{1,0:T(8,128)(2,1)} %copy-done.9, bf16[128,2176]{1,0:T(8,128)(2,1)} %copy-done.3, ...), custom_call_target="tpu_custom_call" | custom-call | tf_op jit(solution)/shard_map/pallas_call | solution.py:198
  246.0 21.5 %collective-permute-done.18.refs_5_ = bf16[512,768]{1,0:T(8,128)(2,1)S(1)} collective-permute-done((bf16[512,768]{1,0:T(8,128)(2,1)S(1)}, bf16[512,768]{1,0:T(8,128)(2,1)S(1)}, u32[]{:S(2)}, u32[]{:S(2)}) %collective-permute-start.18) | collective-permute-done | bytes 786464 | tf_op jit(solution)/shard_map/ppermute | solution.py:35
  268.8 18.6 %collective-permute-done.19.refs_7_ = bf16[512,768]{1,0:T(8,128)(2,1)S(1)} collective-permute-done((bf16[512,768]{1,0:T(8,128)(2,1)S(1)}, bf16[512,768]{1,0:T(8,128)(2,1)S(1)}, u32[]{:S(2)}, u32[]{:S(2)}) %collective-permute-start.19) | collective-permute-done | bytes 786464 | tf_op jit(solution)/shard_map/ppermute | solution.py:35
  288.3 11.2 %shard_map.86 = (bf16[1024,768]{1,0:T(8,128)(2,1)S(1)}, f32[1024,768]{1,0:T(8,128)}, f32[1024,768]{1,0:T(8,128)}) custom-call(bf16[1024,2048]{1,0:T(8,128)(2,1)} %bitcast.1.refs_0_.rows_ref, bf16[512,1536]{1,0:T(8,128)(2,1)S(1)} %copy-done.11, bf16[512,1536]{1,0:T(8,128)(2,1)} %copy-done.12, bf16[512,1536]{1,0:T(8,128)(2,1)} %copy-done.56, ...), custom_call_target="tpu_custom_call" | custom-call | tf_op jit(solution)/shard_map/pallas_call | solution.py:306
  313.7 10.4 %collective-permute-done.20.refs_6_ = bf16[512,768]{1,0:T(8,128)(2,1)} collective-permute-done((bf16[512,768]{1,0:T(8,128)(2,1)}, bf16[512,768]{1,0:T(8,128)(2,1)}, u32[]{:S(2)}, u32[]{:S(2)}) %collective-permute-start.20) | collective-permute-done | bytes 786464 | tf_op jit(solution)/shard_map/ppermute | solution.py:35
  324.1 11.6 %shard_map.92 = (bf16[1024,2048]{1,0:T(8,128)(2,1)}, bf16[1024,1536]{1,0:T(8,128)(2,1)}) custom-call(bf16[1024,768]{1,0:T(8,128)(2,1)} %copy-done, bf16[1024,2048]{1,0:T(8,128)(2,1)} %bitcast.2.rows_ref.refs_1_, f32[1024,768]{1,0:T(8,128)} %get-tuple-element.108.refs_2_, f32[1024,768]{1,0:T(8,128)} %get-tuple-element.109.refs_3_, ...), custom_call_target="tpu_custom_call" | custom-call | tf_op jit(solution)/shard_map/pallas_call | solution.py:343
  342.1 18.2 %collective-permute-done.21.refs_1_ = bf16[512,768]{1,0:T(8,128)(2,1)S(1)} collective-permute-done((bf16[512,768]{1,0:T(8,128)(2,1)S(1)}, bf16[512,768]{1,0:T(8,128)(2,1)S(1)}, u32[]{:S(2)}, u32[]{:S(2)}) %collective-permute-start.21) | collective-permute-done | bytes 786464 | tf_op jit(solution)/shard_map/ppermute | solution.py:35
  361.2 20.9 %collective-permute-done.22.refs_3_ = bf16[512,768]{1,0:T(8,128)(2,1)S(1)} collective-permute-done((bf16[512,768]{1,0:T(8,128)(2,1)S(1)}, bf16[512,768]{1,0:T(8,128)(2,1)S(1)}, u32[]{:S(2)}, u32[]{:S(2)}) %collective-permute-start.22) | collective-permute-done | bytes 786464 | tf_op jit(solution)/shard_map/ppermute | solution.py:35
  400.9 11.1 %shard_map.97 = bf16[1024,2048]{1,0:T(8,128)(2,1)} custom-call(bf16[1024,1536]{1,0:T(8,128)(2,1)} %get-tuple-element.115.parts_ref.refs_0_, bf16[512,1536]{1,0:T(8,128)(2,1)S(1)} %copy-done.11, bf16[512,1536]{1,0:T(8,128)(2,1)S(1)} %copy-done.13, bf16[512,1536]{1,0:T(8,128)(2,1)} %copy-done.56, bf16[512,1536]{1,0:T(8,128)(2,1)} %collective-permute-done.7.refs_4_), custom_call_target="tpu_custom_call" | custom-call | tf_op jit(solution)/shard_map/pallas_call | solution.py:369
  412.0 5.9 collective-permute-done.23.refs_2_
  421.9 12.1 %shard_map.98 = (bf16[128,2048]{1,0:T(8,128)(2,1)S(1)}, bf16[128,2048]{1,0:T(8,128)(2,1)}, bf16[128,2048]{1,0:T(8,128)(2,1)S(1)}, bf16[128,2048]{1,0:T(8,128)(2,1)}, f32[4,4,128]{2,1,0:T(4,128)S(1)}) custom-call(s32[1]{0:T(128)} %bitcast.level_ref, bf16[128,2176]{1,0:T(8,128)(2,1)} %copy-done.1, bf16[128,2176]{1,0:T(8,128)(2,1)} %copy-done.4, ...), custom_call_target="tpu_custom_call" | custom-call | tf_op jit(solution)/shard_map/pallas_call | solution.py:272
  443.7 15.5 %collective-permute-done.39 = bf16[128,1536]{1,0:T(8,128)(2,1)S(1)} collective-permute-done((bf16[128,1536]{1,0:T(8,128)(2,1)}, bf16[128,1536]{1,0:T(8,128)(2,1)S(1)}, u32[]{:S(2)}, u32[]{:S(2)}) %collective-permute-start.39) | collective-permute-done | bytes 393248 | tf_op jit(solution)/shard_map/ppermute | solution.py:35
  469.4 9.8 %collective-permute-done.40 = bf16[128,1536]{1,0:T(8,128)(2,1)S(1)} collective-permute-done((bf16[128,1536]{1,0:T(8,128)(2,1)S(1)}, bf16[128,1536]{1,0:T(8,128)(2,1)S(1)}, u32[]{:S(2)}, u32[]{:S(2)}) %collective-permute-start.40) | collective-permute-done | bytes 393248 | tf_op jit(solution)/shard_map/ppermute | solution.py:35
  483.3 18.5 %collective-permute-start.26 = (bf16[128,2048]{1,0:T(8,128)(2,1)S(1)}, bf16[128,2048]{1,0:T(8,128)(2,1)S(1)}, u32[]{:S(2)}, u32[]{:S(2)}) collective-permute-start(bf16[128,2048]{1,0:T(8,128)(2,1)S(1)} %add_convert_fusion.5), channel_id=1, source_target_pairs={{0,1},{1,2},{2,3},{4,5},{5,6},{6,7},{8,9},{9,10},{10,11},{12,13},{... | collective-permute-start | bytes 1572872 | tf_op jit(solution)/shard_map/ppermute | solution.py:57
  510.6 23.8 %collective-permute-done.42 = bf16[128,1536]{1,0:T(8,128)(2,1)S(1)} collective-permute-done((bf16[128,1536]{1,0:T(8,128)(2,1)S(1)}, bf16[128,1536]{1,0:T(8,128)(2,1)S(1)}, u32[]{:S(2)}, u32[]{:S(2)}) %collective-permute-start.42) | collective-permute-done | bytes 393248 | tf_op jit(solution)/shard_map/ppermute | solution.py:35
  544.1 6.4 shard_map.100
  558.5 7.8 %collective-permute-done.30 = bf16[128,2048]{1,0:T(8,128)(2,1)S(1)} collective-permute-done((bf16[128,2048]{1,0:T(8,128)(2,1)S(1)}, bf16[128,2048]{1,0:T(8,128)(2,1)S(1)}, u32[]{:S(2)}, u32[]{:S(2)}) %collective-permute-start.30) | collective-permute-done | bytes 524320 | tf_op jit(solution)/shard_map/ppermute | solution.py:57
  571.9 11.3 %collective-permute-done.44 = bf16[256,1536]{1,0:T(8,128)(2,1)S(1)} collective-permute-done((bf16[256,1536]{1,0:T(8,128)(2,1)S(1)}, bf16[256,1536]{1,0:T(8,128)(2,1)S(1)}, u32[]{:S(2)}, u32[]{:S(2)}) %collective-permute-start.44) | collective-permute-done | bytes 786464 | tf_op jit(solution)/shard_map/ppermute | solution.py:35
  583.3 11.1 %collective-permute-done.31 = bf16[128,2048]{1,0:T(8,128)(2,1)S(1)} collective-permute-done((bf16[128,2048]{1,0:T(8,128)(2,1)S(1)}, bf16[128,2048]{1,0:T(8,128)(2,1)S(1)}, u32[]{:S(2)}, u32[]{:S(2)}) %collective-permute-start.31) | collective-permute-done | bytes 524320 | tf_op jit(solution)/shard_map/ppermute | solution.py:57
  600.4 11.3 %collective-permute-done.45 = bf16[256,1536]{1,0:T(8,128)(2,1)S(1)} collective-permute-done((bf16[256,1536]{1,0:T(8,128)(2,1)S(1)}, bf16[256,1536]{1,0:T(8,128)(2,1)S(1)}, u32[]{:S(2)}, u32[]{:S(2)}) %collective-permute-start.45) | collective-permute-done | bytes 786464 | tf_op jit(solution)/shard_map/ppermute | solution.py:35
  616.1 20.6 %collective-permute-done.37 = f32[4,128]{1,0:T(4,128)S(1)} collective-permute-done((f32[4,128]{1,0:T(4,128)S(1)}, f32[4,128]{1,0:T(4,128)S(1)}, u32[]{:S(2)}, u32[]{:S(2)}) %collective-permute-start.37) | collective-permute-done | bytes 2080 | tf_op jit(solution)/shard_map/ppermute | solution.py:35
  644.9 8.2 %shard_map.101 = bf16[512,4,2304]{2,1,0:T(4,128)(2,1)} custom-call(s32[1]{0:T(128)} %bitcast.level_ref, bf16[512,1536]{1,0:T(8,128)(2,1)S(1)} %copy-done.19, bf16[512,1536]{1,0:T(8,128)(2,1)S(1)} %constant_dynamic-update-slice_fusion.8.refs_1_, bf16[512,1536]{1,0:T(8,128)(2,1)} %constant_dynamic-update-slice_fusion.4.refs_2_, ...), custom_call_target="tpu_custom_call", output_to_operand_aliasing={{}: (5, {})} | custom-call | tf_op jit(solution)/shard_map/pallas_call | solution.py:124
  (245 shorter events, 166.0 us)
Async XLA Ops:
  23.5 49.9 %collective-permute-start.4 = (bf16[512,1536]{1,0:T(8,128)(2,1)}, bf16[512,1536]{1,0:T(8,128)(2,1)S(1)}, u32[]{:S(2)}, u32[]{:S(2)}) collective-permute-start(bf16[512,1536]{1,0:T(8,128)(2,1)} %get-tuple-element.76), channel_id=1, source_target_pairs={{0,1},{1,2},{2,3},{3,0},{4,5},{5,6},{6,7},{7,4},{8,9},{9,10},{10,1... | collective-permute-start | bytes 4718600 | tf_op jit(solution)/shard_map/ppermute | solution.py:35
  26.2 47.1 %collective-permute-start.3 = (bf16[128,2176]{1,0:T(8,128)(2,1)S(1)}, bf16[128,2176]{1,0:T(8,128)(2,1)S(1)}, u32[]{:S(2)}, u32[]{:S(2)}) collective-permute-start(bf16[128,2176]{1,0:T(8,128)(2,1)S(1)} %collective-permute-done.1.refs_4_.refs_11_), channel_id=1, source_target_pairs={{1,0},{2,1},{5,4},{6,5},{9,8},{10,9},{13,12},{14,13},{17,16},{18,1... | collective-permute-start | bytes 1671176 | tf_op jit(solution)/shard_map/ppermute | solution.py:57
  73.4 48.5 %collective-permute-start.7 = (bf16[512,1536]{1,0:T(8,128)(2,1)}, bf16[512,1536]{1,0:T(8,128)(2,1)}, u32[]{:S(2)}, u32[]{:S(2)}) collective-permute-start(bf16[512,1536]{1,0:T(8,128)(2,1)} %get-tuple-element.79), channel_id=1, source_target_pairs={{0,3},{1,0},{2,1},{3,2},{4,7},{5,4},{6,5},{7,6},{8,11},{9,8},{10,9... | collective-permute-start | bytes 4718600 | tf_op jit(solution)/shard_map/ppermute | solution.py:35
  75.1 46.7 %collective-permute-start.6 = (bf16[128,2176]{1,0:T(8,128)(2,1)S(1)}, bf16[128,2176]{1,0:T(8,128)(2,1)S(1)}, u32[]{:S(2)}, u32[]{:S(2)}) collective-permute-start(bf16[128,2176]{1,0:T(8,128)(2,1)S(1)} %collective-permute-done.3.refs_5_.refs_12_), channel_id=1, source_target_pairs={{1,0},{5,4},{9,8},{13,12},{17,16},{21,20},{25,24},{29,28}} | collective-permute-start | bytes 1671176 | tf_op jit(solution)/shard_map/ppermute | solution.py:57
  129.4 111.6 %all-to-all-start = ((bf16[8,4,32,2048]{3,2,1,0:T(8,128)(2,1)}), bf16[8,4,32,2048]{3,2,1,0:T(8,128)(2,1)}, u32[]{:S(2)}, u32[]{:S(2)}) async-start(bf16[8,4,32,2048]{3,2,1,0:T(8,128)(2,1)} %shard_map.85), calls=%async_computation | async-start | bytes 8388608 | tf_op jit(solution)/shard_map/all_to_all | solution.py:424
  137.0 24.9 %collective-permute-start.8 = (bf16[128,2048]{1,0:T(8,128)(2,1)S(1)}, bf16[128,2048]{1,0:T(8,128)(2,1)S(1)}, u32[]{:S(2)}, u32[]{:S(2)}) collective-permute-start(bf16[128,2048]{1,0:T(8,128)(2,1)S(1)} %copy-done.22), channel_id=1, source_target_pairs={{0,1},{1,2},{2,3},{4,5},{5,6},{6,7},{8,9},{9,10},{10,11},{12,13},{... | collective-permute-start | bytes 1572872 | tf_op jit(solution)/shard_map/ppermute | solution.py:57
  155.9 28.1 %collective-permute-start.15 = (bf16[128,1536]{1,0:T(8,128)(2,1)S(1)}, bf16[128,1536]{1,0:T(8,128)(2,1)S(1)}, u32[]{:S(2)}, u32[]{:S(2)}) collective-permute-start(bf16[128,1536]{1,0:T(8,128)(2,1)S(1)} %get-tuple-element.89), channel_id=1, source_target_pairs={{0,2},{1,3},{2,0},{3,1},{4,6},{5,7},{6,4},{7,5},{8,10},{9,11},{10,... | collective-permute-start | bytes 1179656 | tf_op jit(solution)/shard_map/ppermute | solution.py:35
  160.6 34.5 %collective-permute-start.12 = (bf16[128,2048]{1,0:T(8,128)(2,1)S(1)}, bf16[128,2048]{1,0:T(8,128)(2,1)S(1)}, u32[]{:S(2)}, u32[]{:S(2)}) collective-permute-start(bf16[128,2048]{1,0:T(8,128)(2,1)S(1)} %collective-permute-done.11.refs_11_), channel_id=1, source_target_pairs={{1,0},{2,1},{5,4},{6,5},{9,8},{10,9},{13,12},{14,13},{17,16},{18,1... | collective-permute-start | bytes 1572872 | tf_op jit(solution)/shard_map/ppermute | solution.py:57
  161.9 34.5 %collective-permute-start.9 = (bf16[128,2048]{1,0:T(8,128)(2,1)S(1)}, bf16[128,2048]{1,0:T(8,128)(2,1)S(1)}, u32[]{:S(2)}, u32[]{:S(2)}) collective-permute-start(bf16[128,2048]{1,0:T(8,128)(2,1)S(1)} %collective-permute-done.8.refs_8_), channel_id=1, source_target_pairs={{1,2},{2,3},{5,6},{6,7},{9,10},{10,11},{13,14},{14,15},{17,18},{18... | collective-permute-start | bytes 1572872 | tf_op jit(solution)/shard_map/ppermute | solution.py:57
  184.0 28.1 %collective-permute-start.16 = (bf16[128,1536]{1,0:T(8,128)(2,1)S(1)}, bf16[128,1536]{1,0:T(8,128)(2,1)S(1)}, u32[]{:S(2)}, u32[]{:S(2)}) collective-permute-start(bf16[128,1536]{1,0:T(8,128)(2,1)S(1)} %get-tuple-element.90), channel_id=1, source_target_pairs={{0,2},{1,3},{2,0},{3,1},{4,6},{5,7},{6,4},{7,5},{8,10},{9,11},{10,... | collective-permute-start | bytes 1179656 | tf_op jit(solution)/shard_map/ppermute | solution.py:35
  195.1 36.6 %collective-permute-start.13 = (bf16[128,2048]{1,0:T(8,128)(2,1)S(1)}, bf16[128,2048]{1,0:T(8,128)(2,1)S(1)}, u32[]{:S(2)}, u32[]{:S(2)}) collective-permute-start(bf16[128,2048]{1,0:T(8,128)(2,1)S(1)} %collective-permute-done.12.refs_12_), channel_id=1, source_target_pairs={{1,0},{5,4},{9,8},{13,12},{17,16},{21,20},{25,24},{29,28}} | collective-permute-start | bytes 1572872 | tf_op jit(solution)/shard_map/ppermute | solution.py:57
  196.4 36.3 %collective-permute-start.10 = (bf16[128,2048]{1,0:T(8,128)(2,1)S(1)}, bf16[128,2048]{1,0:T(8,128)(2,1)S(1)}, u32[]{:S(2)}, u32[]{:S(2)}) collective-permute-start(bf16[128,2048]{1,0:T(8,128)(2,1)S(1)} %collective-permute-done.9.refs_9_), channel_id=1, source_target_pairs={{2,3},{6,7},{10,11},{14,15},{18,19},{22,23},{26,27},{30,31}} | collective-permute-start | bytes 1572872 | tf_op jit(solution)/shard_map/ppermute | solution.py:57
  241.1 58.4 %all-to-all-start.1 = ((bf16[8,4,32,2048]{3,2,1,0:T(8,128)(2,1)}), bf16[8,4,32,2048]{3,2,1,0:T(8,128)(2,1)}, u32[]{:S(2)}, u32[]{:S(2)}) async-start(bf16[8,4,32,2048]{3,2,1,0:T(8,128)(2,1)} %shard_map.87), calls=%async_computation.1 | async-start | bytes 8388608 | tf_op jit(solution)/shard_map/all_to_all | solution.py:424
  288.3 35.8 %collective-permute-start.20 = (bf16[512,768]{1,0:T(8,128)(2,1)}, bf16[512,768]{1,0:T(8,128)(2,1)}, u32[]{:S(2)}, u32[]{:S(2)}) collective-permute-start(bf16[512,768]{1,0:T(8,128)(2,1)} %get-tuple-element.99), channel_id=1, source_target_pairs={{0,2},{1,3},{2,0},{3,1},{4,6},{5,7},{6,4},{7,5},{8,10},{9,11},{10,... | collective-permute-start | bytes 2359304 | tf_op jit(solution)/shard_map/ppermute | solution.py:35
  335.8 83.0 %all-to-all-start.2 = ((bf16[8,4,32,2048]{3,2,1,0:T(8,128)(2,1)}), bf16[8,4,32,2048]{3,2,1,0:T(8,128)(2,1)}, u32[]{:S(2)}, u32[]{:S(2)}) async-start(bf16[8,4,32,2048]{3,2,1,0:T(8,128)(2,1)} %bitcast.18), calls=%async_computation.2 | async-start | bytes 8388608 | tf_op jit(solution)/shard_map/all_to_all | solution.py:424
  383.0 34.9 %collective-permute-start.23 = (bf16[512,768]{1,0:T(8,128)(2,1)}, bf16[512,768]{1,0:T(8,128)(2,1)S(1)}, u32[]{:S(2)}, u32[]{:S(2)}) collective-permute-start(bf16[512,768]{1,0:T(8,128)(2,1)} %shard_map.90), channel_id=1, source_target_pairs={{0,2},{1,3},{2,0},{3,1},{4,6},{5,7},{6,4},{7,5},{8,10},{9,11},{10,... | collective-permute-start | bytes 2359304 | tf_op jit(solution)/shard_map/ppermute | solution.py:35
  434.0 27.3 %collective-permute-start.27 = (bf16[128,2048]{1,0:T(8,128)(2,1)}, bf16[128,2048]{1,0:T(8,128)(2,1)}, u32[]{:S(2)}, u32[]{:S(2)}) collective-permute-start(bf16[128,2048]{1,0:T(8,128)(2,1)} %get-tuple-element.118), channel_id=1, source_target_pairs={{3,2},{7,6},{11,10},{15,14},{19,18},{23,22},{27,26},{31,30}} | collective-permute-start | bytes 1572872 | tf_op jit(solution)/shard_map/ppermute | solution.py:57
  435.5 25.8 %collective-permute-start.24 = (bf16[128,2048]{1,0:T(8,128)(2,1)}, bf16[128,2048]{1,0:T(8,128)(2,1)}, u32[]{:S(2)}, u32[]{:S(2)}) collective-permute-start(bf16[128,2048]{1,0:T(8,128)(2,1)} %get-tuple-element.120), channel_id=1, source_target_pairs={{0,1},{4,5},{8,9},{12,13},{16,17},{20,21},{24,25},{28,29}} | collective-permute-start | bytes 1572872 | tf_op jit(solution)/shard_map/ppermute | solution.py:57
  439.0 97.1 %all-to-all-start.3 = ((bf16[8,4,32,2048]{3,2,1,0:T(8,128)(2,1)}), bf16[8,4,32,2048]{3,2,1,0:T(8,128)(2,1)}, u32[]{:S(2)}, u32[]{:S(2)}) async-start(bf16[8,4,32,2048]{3,2,1,0:T(8,128)(2,1)} %bitcast.17), calls=%async_computation.3 | async-start | bytes 8388608 | tf_op jit(solution)/shard_map/all_to_all | solution.py:424
  467.9 33.8 %collective-permute-start.28 = (bf16[128,2048]{1,0:T(8,128)(2,1)S(1)}, bf16[128,2048]{1,0:T(8,128)(2,1)S(1)}, u32[]{:S(2)}, u32[]{:S(2)}) collective-permute-start(bf16[128,2048]{1,0:T(8,128)(2,1)S(1)} %get-tuple-element.151), channel_id=1, source_target_pairs={{2,1},{3,2},{6,5},{7,6},{10,9},{11,10},{14,13},{15,14},{18,17},{19... | collective-permute-start | bytes 1572872 | tf_op jit(solution)/shard_map/ppermute | solution.py:57
  479.2 28.1 %collective-permute-start.41 = (bf16[128,1536]{1,0:T(8,128)(2,1)S(1)}, bf16[128,1536]{1,0:T(8,128)(2,1)S(1)}, u32[]{:S(2)}, u32[]{:S(2)}) collective-permute-start(bf16[128,1536]{1,0:T(8,128)(2,1)S(1)} %copy-done.58), channel_id=1, source_target_pairs={{0,2},{1,3},{2,0},{3,1},{4,6},{5,7},{6,4},{7,5},{8,10},{9,11},{10,... | collective-permute-start | bytes 1179656 | tf_op jit(solution)/shard_map/ppermute | solution.py:35
  483.3 51.8 %collective-permute-start.26 = (bf16[128,2048]{1,0:T(8,128)(2,1)S(1)}, bf16[128,2048]{1,0:T(8,128)(2,1)S(1)}, u32[]{:S(2)}, u32[]{:S(2)}) collective-permute-start(bf16[128,2048]{1,0:T(8,128)(2,1)S(1)} %add_convert_fusion.5), channel_id=1, source_target_pairs={{0,1},{1,2},{2,3},{4,5},{5,6},{6,7},{8,9},{9,10},{10,11},{12,13},{... | collective-permute-start | bytes 1572872 | tf_op jit(solution)/shard_map/ppermute | solution.py:57
  503.0 32.1 %collective-permute-start.29 = (bf16[128,2048]{1,0:T(8,128)(2,1)S(1)}, bf16[128,2048]{1,0:T(8,128)(2,1)S(1)}, u32[]{:S(2)}, u32[]{:S(2)}) collective-permute-start(bf16[128,2048]{1,0:T(8,128)(2,1)S(1)} %add_convert_fusion.4), channel_id=1, source_target_pairs={{1,0},{2,1},{3,2},{5,4},{6,5},{7,6},{9,8},{10,9},{11,10},{13,12},{... | collective-permute-start | bytes 1572872 | tf_op jit(solution)/shard_map/ppermute | solution.py:57
  507.3 27.0 %collective-permute-start.42 = (bf16[128,1536]{1,0:T(8,128)(2,1)S(1)}, bf16[128,1536]{1,0:T(8,128)(2,1)S(1)}, u32[]{:S(2)}, u32[]{:S(2)}) collective-permute-start(bf16[128,1536]{1,0:T(8,128)(2,1)S(1)} %get-tuple-element.131), channel_id=1, source_target_pairs={{0,2},{1,3},{2,0},{3,1},{4,6},{5,7},{6,4},{7,5},{8,10},{9,11},{10,... | collective-permute-start | bytes 1179656 | tf_op jit(solution)/shard_map/ppermute | solution.py:35
  554.3 28.9 %collective-permute-start.44 = (bf16[256,1536]{1,0:T(8,128)(2,1)S(1)}, bf16[256,1536]{1,0:T(8,128)(2,1)S(1)}, u32[]{:S(2)}, u32[]{:S(2)}) collective-permute-start(bf16[256,1536]{1,0:T(8,128)(2,1)S(1)} %copy-done.57), channel_id=1, source_target_pairs={{0,3},{1,0},{2,1},{3,2},{4,7},{5,4},{6,5},{7,6},{8,11},{9,8},{10,9... | collective-permute-start | bytes 2359304 | tf_op jit(solution)/shard_map/ppermute | solution.py:35
  566.6 27.8 %collective-permute-start.31 = (bf16[128,2048]{1,0:T(8,128)(2,1)S(1)}, bf16[128,2048]{1,0:T(8,128)(2,1)S(1)}, u32[]{:S(2)}, u32[]{:S(2)}) collective-permute-start(bf16[128,2048]{1,0:T(8,128)(2,1)S(1)} %get-tuple-element.148), channel_id=1, source_target_pairs={{0,1},{1,2},{4,5},{5,6},{8,9},{9,10},{12,13},{13,14},{16,17},{17,1... | collective-permute-start | bytes 1572872 | tf_op jit(solution)/shard_map/ppermute | solution.py:57
  571.1 27.8 %collective-permute-start.34 = (bf16[128,2048]{1,0:T(8,128)(2,1)S(1)}, bf16[128,2048]{1,0:T(8,128)(2,1)S(1)}, u32[]{:S(2)}, u32[]{:S(2)}) collective-permute-start(bf16[128,2048]{1,0:T(8,128)(2,1)S(1)} %get-tuple-element.149), channel_id=1, source_target_pairs={{2,1},{3,2},{6,5},{7,6},{10,9},{11,10},{14,13},{15,14},{18,17},{19... | collective-permute-start | bytes 1572872 | tf_op jit(solution)/shard_map/ppermute | solution.py:57
  583.2 28.4 %collective-permute-start.45 = (bf16[256,1536]{1,0:T(8,128)(2,1)S(1)}, bf16[256,1536]{1,0:T(8,128)(2,1)S(1)}, u32[]{:S(2)}, u32[]{:S(2)}) collective-permute-start(bf16[256,1536]{1,0:T(8,128)(2,1)S(1)} %get-tuple-element.134), channel_id=1, source_target_pairs={{0,1},{1,2},{2,3},{3,0},{4,5},{5,6},{6,7},{7,4},{8,9},{9,10},{10,1... | collective-permute-start | bytes 2359304 | tf_op jit(solution)/shard_map/ppermute | solution.py:35
  594.6 47.3 %collective-permute-start.32 = (bf16[128,2048]{1,0:T(8,128)(2,1)S(1)}, bf16[128,2048]{1,0:T(8,128)(2,1)S(1)}, u32[]{:S(2)}, u32[]{:S(2)}) collective-permute-start(bf16[128,2048]{1,0:T(8,128)(2,1)S(1)} %add_convert_fusion.2), channel_id=1, source_target_pairs={{0,1},{1,2},{2,3},{4,5},{5,6},{6,7},{8,9},{9,10},{10,11},{12,13},{... | collective-permute-start | bytes 1572872 | tf_op jit(solution)/shard_map/ppermute | solution.py:57
  599.1 42.7 %collective-permute-start.35 = (bf16[128,2048]{1,0:T(8,128)(2,1)S(1)}, bf16[128,2048]{1,0:T(8,128)(2,1)S(1)}, u32[]{:S(2)}, u32[]{:S(2)}) collective-permute-start(bf16[128,2048]{1,0:T(8,128)(2,1)S(1)} %add_convert_fusion.1), channel_id=1, source_target_pairs={{1,0},{2,1},{3,2},{5,4},{6,5},{7,6},{9,8},{10,9},{11,10},{13,12},{... | collective-permute-start | bytes 1572872 | tf_op jit(solution)/shard_map/ppermute | solution.py:57
  611.7 31.2 %collective-permute-start.46 = (bf16[256,1536]{1,0:T(8,128)(2,1)S(1)}, bf16[256,1536]{1,0:T(8,128)(2,1)S(1)}, u32[]{:S(2)}, u32[]{:S(2)}) collective-permute-start(bf16[256,1536]{1,0:T(8,128)(2,1)S(1)} %get-tuple-element.135), channel_id=1, source_target_pairs={{0,1},{1,2},{2,3},{3,0},{4,5},{5,6},{6,7},{7,4},{8,9},{9,10},{10,1... | collective-permute-start | bytes 2359304 | tf_op jit(solution)/shard_map/ppermute | solution.py:35
  613.8 26.2 %collective-permute-start.38 = (f32[4,128]{1,0:T(4,128)S(1)}, f32[4,128]{1,0:T(4,128)S(1)}, u32[]{:S(2)}, u32[]{:S(2)}) collective-permute-start(f32[4,128]{1,0:T(4,128)S(1)} %get-tuple-element.153), channel_id=1, source_target_pairs={{0,1},{1,2},{2,3},{3,0},{4,5},{5,6},{6,7},{7,4},{8,9},{9,10},{10,1... | collective-permute-start | bytes 6152 | tf_op jit(solution)/shard_map/ppermute | solution.py:35
  (81 other events, 1516.0 us)
where the time goes:
time: 655 us; the launch traced here: 653 us
  waiting for transfers between devices  391 us (60%)
  Pallas kernels  116 us (18%)
  starting transfers between devices  104 us (16%)
  local copies, waits for them, and re-layouts  30.8 us (5%)
  other arithmetic  9.74 us (1%)
    ppermute x23, waiting for transfers between devices, shift(): return lax.ppermute(x, 'narrow', [(i, (i + k) % n) for i in range(n)])  262 us
    ppermute x24, waiting for transfers between devices, hop(): return lax.ppermute(x, 'narrow', [(i, i + step) for i in sources])  129 us
    ppermute x24, starting transfers between devices, hop(): return lax.ppermute(x, 'narrow', [(i, i + step) for i in sources])  63.6 us
    pallas_call x8, Pallas kernels, weight_grad(): pl.pallas_call(weight_grad_kernel, out_shape=jax.ShapeDtypeStruct((width,...  28.8 us
    unnamed x131, local copies, waits for them, and re-layouts  24.2 us
    ppermute x23, starting transfers between devices, shift(): return lax.ppermute(x, 'narrow', [(i, (i + k) % n) for i in range(n)])  21.5 us
    all_to_all x4, starting transfers between devices, swap(): return lax.all_to_all(x, 'wide', split_axis=0, concat_axis=0, tiled=True)  18.8 us
    pallas_call x2, Pallas kernels, combine(): pl.pallas_call(functools.partial(kernel, n, chosen), out_shape=out_shape,...  18.5 us
  transfers between devices with their start and end apart: 51, of which 27 were waited for; matrix products, arithmetic and copies ran while one was open for 2% of the time, Pallas kernels for 12%

commit v1 on v0

--- a/solution.py
+++ b/solution.py
@@ -11,7 +11,8 @@
 BF16 = jnp.bfloat16
 VMEM_LIMIT = 50 * 1024 * 1024
 META = 128
-PIECES = 4
+LANES = 2
+FLOPS_PER_VALUE = 40000
 
 
 def dot(a, b, dims):
@@ -35,21 +36,48 @@
     return lax.ppermute(x, "narrow", [(i, (i + k) % n) for i in range(n)])
 
 
-def shift_pieces(x, k, pieces, first=()):
-    rows = x.shape[0] // pieces
-    moved, latest = [], first
-    for i in range(pieces):
-        moved.append(shift(after(x[i * rows : (i + 1) * rows], *latest), k))
-        latest = moved[-1:]
-    return jnp.concatenate(moved)
-
-
-def shift_chain(blocks, sign, order, first=()):
-    moved, latest = list(blocks), first
-    for k in order:
-        moved[k] = shift(after(blocks[k], *latest), sign * k)
-        latest = [moved[k]]
-    return moved
+def arrival_kernel(moved_ref, out_ref, done_ref):
+    done_ref[...] = jnp.zeros_like(done_ref)
+
+
+def arrival(moved, load):
+    anywhere = pl.BlockSpec(memory_space=pl.ANY)
+    return pl.pallas_call(
+        arrival_kernel,
+        out_shape=jax.ShapeDtypeStruct(moved.shape, moved.dtype),
+        in_specs=[anywhere],
+        out_specs=anywhere,
+        scratch_shapes=[pltpu.VMEM((8, 128), F32)],
+        input_output_aliases={0: 0},
+        cost_estimate=pl.CostEstimate(
+            flops=FLOPS_PER_VALUE * moved.size * load, bytes_accessed=0, transcendentals=0
+        ),
+    )(moved)
+
+
+class Lanes:
+    def __init__(self, count, first):
+        self.latest = [first] * count
+        self.sent = []
+
+    def send(self, x, k, others=()):
+        lane = len(self.sent) % len(self.latest)
+        n = lax.axis_size("narrow")
+        moved = shift(after(x, self.latest[lane], others), k)
+        moved = arrival(moved, min(k % n, -k % n))
+        self.latest[lane] = moved
+        self.sent.append(moved)
+        return moved
+
+    def send_all(self, blocks, sign, order, others=()):
+        waits = iter(others)
+        return {
+            k: [self.send(x, sign * k, next(waits, ())) if k else x for x in blocks[k]]
+            for k in order
+        }
+
+    def done(self, i):
+        return self.sent[min(i, len(self.sent) - 1)]
 
 
 def hop(x, up, sources):
@@ -60,6 +88,7 @@
 def reduce_chain(parts):
     n = len(parts)
     up = down = None
+    steps = []
     for step in range(1, n):
         up_send, down_send = parts[step], parts[n - step]
         if up is not None:
@@ -67,8 +96,9 @@
             down_send = (down_send.astype(F32) + down.astype(F32)).astype(BF16)
         up = hop(up_send, True, range(step))
         down = hop(down_send, False, range(n - step, n))
+        steps.append((up, down))
     total = parts[0].astype(F32) + up.astype(F32) + down.astype(F32)
-    return total.astype(BF16)
+    return total.astype(BF16), steps
 
 
 def mixing(level, n, depth):
@@ -83,29 +113,27 @@
     part = out_refs[0].shape[1]
     shard = shard_ref[...].reshape(depth * n, columns)
     apart = dot(mixing(level_ref[0], n, depth), shard, ((0,), (0,))).astype(BF16)
-    for k in range(n):
-        out_refs[k][...] = apart[k * depth : (k + 1) * depth, :part]
-        out_refs[n + k][...] = apart[k * depth : (k + 1) * depth, part:]
+    for i, out_ref in enumerate(out_refs):
+        k, group = i % n, i // n
+        out_ref[...] = apart[k * depth : (k + 1) * depth, group * part : (group + 1) * part]
 
 
 def split_shard(level, shard, part):
     rows, n, columns = shard.shape
     depth = min(rows, 256 // n)
-    rest = columns - part
+    count = columns // part
     outs = pl.pallas_call(
         functools.partial(split_kernel, n),
-        out_shape=[jax.ShapeDtypeStruct((rows, part), BF16)] * n
-        + [jax.ShapeDtypeStruct((rows, rest), BF16)] * n,
+        out_shape=[jax.ShapeDtypeStruct((rows, part), BF16)] * (n * count),
         grid_spec=pltpu.PrefetchScalarGridSpec(
             num_scalar_prefetch=1,
             grid=(rows // depth,),
             in_specs=[pl.BlockSpec((depth, n, columns), lambda i, level: (i, 0, 0))],
-            out_specs=[pl.BlockSpec((depth, part), lambda i, level: (i, 0))] * n
-            + [pl.BlockSpec((depth, rest), lambda i, level: (i, 0))] * n,
+            out_specs=[pl.BlockSpec((depth, part), lambda i, level: (i, 0))] * (n * count),
         ),
         compiler_params=params(),
     )(level, shard)
-    return outs[:n], outs[n:]
+    return [outs[i * n : (i + 1) * n] for i in range(count)]
 
 
 def join_kernel(n, level_ref, *refs):
@@ -282,16 +310,21 @@
     )(level, *metas, *extra, back)
 
 
+def spans(weights):
+    start = 0
+    for weight in weights:
+        yield weight, slice(start, start + weight.shape[0])
+        start += weight.shape[0]
+
+
+def times(rows_ref, weights):
+    return sum(dot(rows_ref[:, span], w[...], ((1,), (0,))) for w, span in spans(weights))
+
+
 def hidden_kernel(count, *refs):
-    rows_ref, weights, outs = refs[0], refs[1 : 1 + count], refs[1 + count :]
-    hidden_ref, active_ref, slope_ref = outs
-    width = weights[0].shape[0]
-    units = hidden_ref.shape[1]
-    pre = sum(
-        dot(rows_ref[:, k * width : (k + 1) * width], weights[k][...], ((1,), (0,)))
-        for k in range(count)
-    )
-    gate, up = pre[:, :units], pre[:, units:]
+    rows_ref, gates, ups = refs[0], refs[1 : 1 + count], refs[1 + count : 1 + 2 * count]
+    hidden_ref, active_ref, slope_ref = refs[1 + 2 * count :]
+    gate, up = times(rows_ref, gates), times(rows_ref, ups)
     sigmoid = jax.nn.sigmoid(gate)
     active = gate * sigmoid
     hidden_ref[...] = (active * up).astype(BF16)
@@ -299,12 +332,12 @@
     slope_ref[...] = up * (sigmoid * (1.0 + gate * (1.0 - sigmoid)))
 
 
-def hidden_pass(rows, weights, tile):
+def hidden_pass(rows, gates, ups, tile):
     slots, model = rows.shape
-    units = weights[0].shape[1] // 2
+    units = gates[0].shape[1]
     out_spec = pl.BlockSpec((tile, units), lambda i: (i, 0))
     return pl.pallas_call(
-        functools.partial(hidden_kernel, len(weights)),
+        functools.partial(hidden_kernel, len(gates)),
         out_shape=(
             jax.ShapeDtypeStruct((slots, units), BF16),
             jax.ShapeDtypeStruct((slots, units), F32),
@@ -312,89 +345,86 @@
         ),
         grid=(slots // tile,),
         in_specs=[pl.BlockSpec((tile, model), lambda i: (i, 0))]
-        + [whole(w.shape) for w in weights],
+        + [whole(w.shape) for w in gates + ups],
         out_specs=(out_spec, out_spec, out_spec),
         compiler_params=params(),
-    )(rows, *weights)
+    )(rows, *gates, *ups)
 
 
 def down_kernel(count, *refs):
     hidden_ref, cotangent_ref, active_ref, slope_ref = refs[:4]
-    weights = refs[4 : 4 + count]
-    out_ref, both_ref = refs[4 + count :]
-    width = weights[0].shape[0]
+    downs = refs[4 : 4 + count]
+    out_ref, gate_ref, up_ref = refs[4 + count :]
     hidden = hidden_ref[...]
-    units = hidden.shape[1]
-    grad = None
-    for k in range(count):
-        weight = weights[k][...]
-        out_ref[:, k * width : (k + 1) * width] = dot(hidden, weight, ((1,), (1,))).astype(BF16)
-        part = dot(cotangent_ref[:, k * width : (k + 1) * width], weight, ((1,), (0,)))
-        grad = part if grad is None else grad + part
-    both_ref[:, :units] = (grad * slope_ref[...]).astype(BF16)
-    both_ref[:, units:] = (grad * active_ref[...]).astype(BF16)
-
-
-def down_pass(hidden, cotangent, active, slope, weights, tile):
+    for weight, span in spans(downs):
+        out_ref[:, span] = dot(hidden, weight[...], ((1,), (1,))).astype(BF16)
+    grad = times(cotangent_ref, downs)
+    gate_ref[...] = (grad * slope_ref[...]).astype(BF16)
+    up_ref[...] = (grad * active_ref[...]).astype(BF16)
+
+
+def down_pass(hidden, cotangent, active, slope, downs, tile):
     slots, model = cotangent.shape
     units = hidden.shape[1]
     unit_spec = pl.BlockSpec((tile, units), lambda i: (i, 0))
     model_spec = pl.BlockSpec((tile, model), lambda i: (i, 0))
     return pl.pallas_call(
-        functools.partial(down_kernel, len(weights)),
+        functools.partial(down_kernel, len(downs)),
         out_shape=(
             jax.ShapeDtypeStruct((slots, model), BF16),
-            jax.ShapeDtypeStruct((slots, 2 * units), BF16),
+            jax.ShapeDtypeStruct((slots, units), BF16),
+            jax.ShapeDtypeStruct((slots, units), BF16),
         ),
         grid=(slots // tile,),
         in_specs=[unit_spec, model_spec, unit_spec, unit_spec]
-        + [whole(w.shape) for w in weights],
-        out_specs=(model_spec, pl.BlockSpec((tile, 2 * units), lambda i: (i, 0))),
-        compiler_params=params(),
-    )(hidden, cotangent, active, slope, *weights)
+        + [whole(w.shape) for w in downs],
+        out_specs=(model_spec, unit_spec, unit_spec),
+        compiler_params=params(),
+    )(hidden, cotangent, active, slope, *downs)
 
 
 def row_grad_kernel(count, *refs):
-    both_ref, weights, out_ref = refs[0], refs[1 : 1 + count], refs[1 + count]
-    width = weights[0].shape[0]
-    for k in range(count):
-        out_ref[:, k * width : (k + 1) * width] = dot(
-            both_ref[...], weights[k][...], ((1,), (1,))
-        ).astype(BF16)
-
-
-def row_grad_pass(both, weights, tile):
-    slots, units = both.shape
-    model = len(weights) * weights[0].shape[0]
-    return pl.pallas_call(
-        functools.partial(row_grad_kernel, len(weights)),
+    gate_ref, up_ref = refs[:2]
+    gates, ups, out_ref = refs[2 : 2 + count], refs[2 + count : 2 + 2 * count], refs[-1]
+    for (gate, span), up in zip(spans(gates), ups):
+        total = dot(gate_ref[...], gate[...], ((1,), (1,)))
+        total += dot(up_ref[...], up[...], ((1,), (1,)))
+        out_ref[:, span] = total.astype(BF16)
+
+
+def row_grad_pass(gate_part, up_part, gates, ups, tile):
+    slots, units = gate_part.shape
+    model = sum(w.shape[0] for w in gates)
+    unit_spec = pl.BlockSpec((tile, units), lambda i: (i, 0))
+    return pl.pallas_call(
+        functools.partial(row_grad_kernel, len(gates)),
         out_shape=jax.ShapeDtypeStruct((slots, model), BF16),
         grid=(slots // tile,),
-        in_specs=[pl.BlockSpec((tile, units), lambda i: (i, 0))]
-        + [whole(w.shape) for w in weights],
+        in_specs=[unit_spec, unit_spec] + [whole(w.shape) for w in gates + ups],
         out_specs=pl.BlockSpec((tile, model), lambda i: (i, 0)),
         compiler_params=params(),
-    )(both, *weights)
-
-
-def weight_grad_kernel(rows_ref, parts_ref, out_ref):
-    out_ref[...] = dot(rows_ref[...], parts_ref[...], ((0,), (0,))).astype(BF16)
-
-
-def weight_grad(rows, parts, k, width):
-    slots, columns = parts.shape
+    )(gate_part, up_part, *gates, *ups)
+
+
+def weight_grad_kernel(rows_ref, *refs):
+    half = len(refs) // 2
+    for part_ref, out_ref in zip(refs[:half], refs[half:]):
+        out_ref[...] = dot(rows_ref[...], part_ref[...], ((0,), (0,))).astype(BF16)
+
+
+def weight_grad(rows, parts, place, width):
+    slots, columns = parts[0].shape
     tile = columns // 2 if columns % 256 == 0 else columns
+    count = len(parts)
     return pl.pallas_call(
         weight_grad_kernel,
-        out_shape=jax.ShapeDtypeStruct((width, columns), BF16),
+        out_shape=[jax.ShapeDtypeStruct((width, columns), BF16)] * count,
         grid=(columns // tile,),
-        in_specs=[
-            pl.BlockSpec((slots, width), lambda i: (0, k)),
-            pl.BlockSpec((slots, tile), lambda i: (0, i)),
-        ],
-        out_specs=pl.BlockSpec((width, tile), lambda i: (0, i)),
-        compiler_params=params(),
-    )(rows, parts)
+        in_specs=[pl.BlockSpec((slots, width), lambda i: (0, place))]
+        + [pl.BlockSpec((slots, tile), lambda i: (0, i))] * count,
+        out_specs=[pl.BlockSpec((width, tile), lambda i: (0, i))] * count,
+        compiler_params=params(),
+    )(rows, *parts)
 
 
 def on_device(tokens, out_grad, routes, route_gates, expert_weights):
@@ -411,14 +441,23 @@
     level = me.astype(jnp.int32).reshape(1)
     tile = min(256, slots)
 
-    high = route_gates.astype(BF16)
-    rest = route_gates - high.astype(F32)
-    middle = rest.astype(BF16)
-    low = (rest - middle.astype(F32)).astype(BF16)
+    high = lax.reduce_precision(route_gates, 8, 7)
+    middle = lax.reduce_precision(route_gates - high, 8, 7)
+    low = route_gates - high - middle
+    thirds = [x.astype(BF16) for x in (high, middle, low)]
     pad = jnp.zeros((token_count, META - 4 * chosen), BF16)
-    sent = jnp.concatenate([tokens, routes.astype(BF16), high, middle, low, pad], axis=1)
-    in_blocks, down_blocks = split_shard(level, expert_weights, 2 * units)
-    middle, others = n // 2, [k for k in range(1, n) if k != n // 2]
+    sent = jnp.concatenate([tokens, routes.astype(BF16), *thirds, pad], axis=1)
+    middle = n // 2
+    order = [k for k in range(1, n) if k != middle] + [middle, 0]
+
+    def halves(k):
+        return 2 if k == middle else 1
+
+    def pieces(blocks):
+        return [jnp.split(x, halves(k)) for k, x in enumerate(blocks)]
+
+    def in_order(moved):
+        return [x for k in range(n) for x in moved[k]]
 
     def swap(x):
         return lax.all_to_all(x, "wide", split_axis=0, concat_axis=0, tiled=True)
@@ -426,67 +465,104 @@
     def as_slots(x):
         return x.reshape(groups, n, capacity, model)
 
-    w_in = [in_blocks[0]] + [None] * (n - 1)
-    token_up, token_down = [sent], [sent]
-    stage = list(in_blocks)
+    gate_blocks, up_blocks, down_blocks = split_shard(level, expert_weights, units)
+
+    def hop_on(ups, downs, *others):
+        step = len(ups)
+        up, down = after((ups[-1], downs[-1]), others)
+        ups.append(hop(up, True, range(step - 1, n - 1)))
+        downs.append(hop(down, False, range(1, n - step + 1)))
+
+    token_up, token_down, grad_up, grad_down = [sent], [sent], [out_grad], [out_grad]
+    hop_on(token_up, token_down)
+    lanes = Lanes(LANES, (token_up[1], token_down[1]))
+    for step in range(2, n):
+        hop_on(token_up, token_down, gate_blocks if step == 2 else ())
     for step in range(1, n):
-        up, down = token_up[-1], token_down[-1]
-        if step > 1:
-            up, down = after((up, down), *stage)
-            k = others[step - 2]
-            w_in[k] = shift(after(in_blocks[k], token_up[-1], token_down[-1], *stage), k)
-            stage = [w_in[k]]
-        token_up.append(hop(up, True, range(step - 1, n - 1)))
-        token_down.append(hop(down, False, range(1, n - step + 1)))
+        hop_on(grad_up, grad_down, token_up[1], token_down[1])
     token_blocks = token_up + token_down[1:]
-    stage = stage + [token_up[-1], token_down[-1]]
+    grad_blocks = grad_up + grad_down[1:]
+
+    def both_ways(ups, downs, step):
+        return ups[min(step, n - 1)], downs[min(step, n - 1)]
+
+    tokens_at = functools.partial(both_ways, token_up, token_down)
+    grads_at = functools.partial(both_ways, grad_up, grad_down)
+    waits = ((), (), (), tokens_at(2), grads_at(1), tokens_at(n - 1), grads_at(2), grads_at(n - 1))
+    gates = in_order(lanes.send_all(pieces(gate_blocks), 1, order, waits[:4]))
+    ups = in_order(lanes.send_all(pieces(up_blocks), 1, order, waits[4:]))
 
     place = functools.partial(
-        dispatch, level, groups=groups, capacity=capacity, chosen=chosen
+        dispatch, level, token_blocks, groups=groups, capacity=capacity, chosen=chosen
     )
-    sent_rows = place(after(token_blocks, *stage), blocks=token_blocks, gated=False)
-    w_in[middle] = shift_pieces(in_blocks[middle], middle, PIECES, stage)
-    start = after(out_grad, *stage)
-    grad_up, grad_down = [start], [start]
-    for step in range(1, n):
-        grad_up.append(hop(grad_up[-1], True, range(step - 1, n - 1)))
-        grad_down.append(hop(grad_down[-1], False, range(1, n - step + 1)))
-    grad_blocks = grad_up + grad_down[1:]
-    rows_in = swap(sent_rows).reshape(slots, model)
-    stage = [w_in[middle], grad_up[-1], grad_down[-1]]
-
-    w_down = shift_chain(down_blocks, 1, others + [middle], stage)
-    sent_grads = place(after(token_blocks, *stage), blocks=grad_blocks, gated=True)
-    cotangent = swap(sent_grads).reshape(slots, model)
-    hidden, active, slope = hidden_pass(rows_in, w_in, tile)
-    down_grads = [weight_grad(cotangent, hidden, k, width) for k in range(n)]
-    stage = w_down + down_grads
-
-    hidden = after(hidden, *stage)
-    down_grads = shift_chain(down_grads, -1, others + [middle], stage)
-    expert_out, both = down_pass(hidden, cotangent, active, slope, w_down, tile)
-    in_grads = [weight_grad(rows_in, both, k, width) for k in range(n)]
-    both = after(both, *in_grads)
-    row_grad = row_grad_pass(both, w_in, tile)
-    back_out = swap(as_slots(expert_out))
-    stage = down_grads + [back_out, row_grad]
+    rows_in = swap(place(blocks=token_blocks, gated=False)).reshape(slots, model)
+    cotangent = swap(place(blocks=grad_blocks, gated=True)).reshape(slots, model)
+    hidden, active, slope = hidden_pass(rows_in, gates, ups, tile)
+    waits = (rows_in, (), hidden, cotangent)
+    downs = in_order(lanes.send_all(pieces(down_blocks), 1, order, waits))
+
+    def weight_grads(rows, *parts):
+        made = [
+            [
+                weight_grad(rows, parts, k * halves(k) + i, width // halves(k))
+                for i in range(halves(k))
+            ]
+            for k in range(n)
+        ]
+        return [[[x[j] for x in blocks] for blocks in made] for j in range(len(parts))]
+
+    def send_back(blocks, others=()):
+        moved, waits = {0: blocks[0]}, list(others)
+        for k in order[:-1]:
+            moved[k] = []
+            for x in blocks[k]:
+                wait = waits.pop(0) if waits else ()
+                moved[k].append(lanes.send(x, -k, wait() if callable(wait) else wait))
+        return [jnp.concatenate(moved[k]) if halves(k) > 1 else moved[k][0] for k in range(n)]
+
+    (down_grads,) = weight_grads(cotangent, hidden)
+    hidden = after(hidden, down_grads)
+    first = len(lanes.sent)
+    down_grads = send_back(down_grads)
+    expert_out, gate_part, up_part = down_pass(hidden, cotangent, active, slope, downs, tile)
+    back_out = swap(as_slots(after(expert_out, lanes.done(first))))
+    gate_grads, up_grads = weight_grads(
+        rows_in, after(gate_part, lanes.done(first + 1)), up_part
+    )
+    row_grad = row_grad_pass(
+        after(gate_part, gate_grads, lanes.done(first + 2)), up_part, gates, ups, tile
+    )
+    back_grad = swap(as_slots(after(row_grad, back_out)))
+
+    sums = {}
+
+    def sum_outputs():
+        back = after(back_out, lanes.done(first + 4))
+        *parts, sums["dots"] = combine(level, token_blocks, back, chosen, grad_blocks)
+        sums["output"], sums["steps"] = reduce_chain(parts)
+        return parts
+
+    gate_grads = send_back(gate_grads, ((), row_grad, (), sum_outputs))
+    layer_output, out_steps, dots = sums["output"], sums["steps"], sums["dots"]
+    gate_grad = dots[0] + sum(shift(dots[d], -d) for d in range(1, n))
+    grad_parts = combine(
+        level, token_blocks, after(back_grad, lanes.done(first + 6)), chosen
+    )
+    token_grad, grad_steps = reduce_chain(grad_parts)
+    up_grads = send_back(
+        up_grads,
+        (
+            (out_steps[0], back_grad),
+            (out_steps[1], grad_parts),
+            (out_steps[-1], grad_steps[0]),
+            (grad_steps[1], gate_grad),
+        ),
+    )
+
     columns = 3 * units
-    shard = join_shard(level, down_grads, columns, 2)
-
-    in_grads[middle] = shift_pieces(in_grads[middle], -middle, PIECES, stage)
-    back_grad = swap(as_slots(after(row_grad, *stage)))
-    back_out = after(back_out, *stage)
-    *out_parts, dots = combine(level, token_blocks, back_out, chosen, grad_blocks)
-    layer_output = reduce_chain(out_parts)
-    stage = [in_grads[middle], layer_output, back_grad]
-    for k in others:
-        in_grads[k] = shift_pieces(in_grads[k], -k, PIECES // 2, stage)
-        stage = [in_grads[k]]
-    grad_parts = combine(level, token_blocks, after(back_grad, shard, layer_output), chosen)
-    token_grad = reduce_chain(grad_parts)
-    gate_grad = dots[0] + sum(shift(dots[d], -d) for d in range(1, n))
-
-    shard = join_shard(level, in_grads, columns, 0, shard)
+    shard = join_shard(level, after(down_grads, lanes.done(first + 7)), columns, 2)
+    shard = join_shard(level, after(gate_grads, lanes.done(first + 9)), columns, 0, shard)
+    shard = join_shard(level, up_grads, columns, 1, shard)
     return (layer_output, token_grad, gate_grad.T, shard)
 
 

time: 655 us -> 591 us (0.902)
  the two profiles are of different devices: /device:TPU:0 before, /device:TPU:26 now
where the time goes in v1:
time: 591 us; the launch traced here: 588 us
  waiting for transfers between devices  255 us (43%)
  starting transfers between devices  153 us (26%)
  Pallas kernels  127 us (21%)
  local copies, waits for them, and re-layouts  30 us (5%)
  other arithmetic  20.1 us (3%)
    ppermute x27, waiting for transfers between devices, shift(): return lax.ppermute(x, 'narrow', [(i, (i + k) % n) for i in range(n)])  184 us
    ppermute x27, starting transfers between devices, shift(): return lax.ppermute(x, 'narrow', [(i, (i + k) % n) for i in range(n)])  75.4 us
    ppermute x24, waiting for transfers between devices, hop(): return lax.ppermute(x, 'narrow', [(i, i + step) for i in sources])  59.2 us
    ppermute x24, starting transfers between devices, hop(): return lax.ppermute(x, 'narrow', [(i, i + step) for i in sources])  57.7 us
    pallas_call x10, Pallas kernels, weight_grad(): pl.pallas_call(weight_grad_kernel, out_shape=[jax.ShapeDtypeStruct((width...  32.8 us
    unnamed x159, local copies, waits for them, and re-layouts  23.9 us
    all_to_all x4, starting transfers between devices, swap(): return lax.all_to_all(x, 'wide', split_axis=0, concat_axis=0, tiled=True)  20.4 us
    pallas_call x3, Pallas kernels, join_shard(): pl.pallas_call(functools.partial(join_kernel, n), out_shape=jax.ShapeDtyp...  19.9 us
  transfers between devices with their start and end apart: 55, of which 24 were waited for; matrix products, arithmetic and copies ran while one was open for 4% of the time, Pallas kernels for 22%

profile of v1, /device:TPU:26, one launch (start us, length us, event | category | flops | bytes accessed | tf_op | source)
XLA Modules:
  0.0 587.5 jit_solution(17990101228329259048)
XLA Ops:
  10.3 9.7 %shard_map.84 = (bf16[512,768]{1,0:T(8,128)(2,1)S(1)}, bf16[512,768]{1,0:T(8,128)(2,1)S(1)}, bf16[512,768]{1,0:T(8,128)(2,1)S(1)}, bf16[512,768]{1,0:T(8,128)(2,...) custom-call(s32[1]{0:T(128)} %bitcast.level_ref, ...), custom_call_target="tpu_custom_call" | custom-call | tf_op jit(solution)/shard_map/pallas_call | solution.py:125
  36.7 17.5 %collective-permute-done.6.refs_8_ = bf16[128,2048]{1,0:T(8,128)(2,1)} collective-permute-done((bf16[128,2048]{1,0:T(8,128)(2,1)S(1)}, bf16[128,2048]{1,0:T(8,128)(2,1)}, u32[]{:S(2)}, u32[]{:S(2)}) %collective-permute-start.6) | collective-permute-done | bytes 524320 | tf_op jit(solution)/shard_map/ppermute | solution.py:85
  54.1 18.9 %collective-permute-start.14 = (bf16[512,768]{1,0:T(8,128)(2,1)}, bf16[512,768]{1,0:T(8,128)(2,1)}, u32[]{:S(2)}, u32[]{:S(2)}) collective-permute-start(bf16[512,768]{1,0:T(8,128)(2,1)} %get-tuple-element.110), channel_id=1, source_target_pairs={{0,3},{1,0},{2,1},{3,2},{4,7},{5,4},{6,5},{7,6},{8,11},{9,8},{10,9... | collective-permute-start | bytes 2359304 | tf_op jit(solution)/shard_map/ppermute | solution.py:36
  74.3 8.5 %collective-permute-done.2.refs_2_.refs_9_ = bf16[128,2176]{1,0:T(8,128)(2,1)S(1)} collective-permute-done((bf16[128,2176]{1,0:T(8,128)(2,1)S(1)}, bf16[128,2176]{1,0:T(8,128)(2,1)S(1)}, u32[]{:S(2)}, u32[]{:S(2)}) %collective-permute-start.2) | collective-permute-done | bytes 557088 | tf_op jit(solution)/shard_map/ppermute | solution.py:85
  94.2 13.6 %collective-permute-start.15 = (bf16[256,768]{1,0:T(8,128)(2,1)}, bf16[256,768]{1,0:T(8,128)(2,1)}, u32[]{:S(2)}, u32[]{:S(2)}) collective-permute-start(bf16[256,768]{1,0:T(8,128)(2,1)} %get-tuple-element.111), channel_id=1, source_target_pairs={{0,2},{1,3},{2,0},{3,1},{4,6},{5,7},{6,4},{7,5},{8,10},{9,11},{10,... | collective-permute-start | bytes 1179656 | tf_op jit(solution)/shard_map/ppermute | solution.py:36
  110.6 6.6 %shard_map.85 = bf16[8,4,32,2048]{3,2,1,0:T(8,128)(2,1)} custom-call(s32[1]{0:T(128)} %bitcast.level_ref, bf16[128,2176]{1,0:T(8,128)(2,1)S(1)} %concatenate.12.refs_0_.refs_7_, bf16[128,2176]{1,0:T(8,128)(2,1)S(1)} %collective-permute-done.refs_1_.refs_8_, bf16[128,2176]{1,0:T(8,128)(2,1)S(1)} %collective-permute-done.2.refs_2_.refs_9_, ...), custom_call_target="tpu_custom_call" | custom-call | tf_op jit(solution)/shard_map/pallas_call | solution.py:226
  127.8 7.1 %collective-permute-done.10.refs_10_ = bf16[128,2048]{1,0:T(8,128)(2,1)} collective-permute-done((bf16[128,2048]{1,0:T(8,128)(2,1)}, bf16[128,2048]{1,0:T(8,128)(2,1)}, u32[]{:S(2)}, u32[]{:S(2)}) %collective-permute-start.10) | collective-permute-done | bytes 524320 | tf_op jit(solution)/shard_map/ppermute | solution.py:85
  134.9 7.1 %shard_map.95 = bf16[8,4,32,2048]{3,2,1,0:T(8,128)(2,1)} custom-call(s32[1]{0:T(128)} %bitcast.level_ref, bf16[128,2176]{1,0:T(8,128)(2,1)} %copy-done.3, bf16[128,2176]{1,0:T(8,128)(2,1)} %copy-done.5, bf16[128,2176]{1,0:T(8,128)(2,1)} %copy-done.8, bf16[128,2176]{1,0:T(8,128)(2,1)} %copy-done.11, bf16[128,2176]{1,0:T(8,128)(2,1)} %copy-done.7, ...), custom_call_target="tpu_custom_call" | custom-call | tf_op jit(solution)/shard_map/pallas_call | solution.py:226
  142.1 7.1 %collective-permute-done.16.moved_ref = bf16[512,768]{1,0:T(8,128)(2,1)S(1)} collective-permute-done((bf16[512,768]{1,0:T(8,128)(2,1)S(1)}, bf16[512,768]{1,0:T(8,128)(2,1)S(1)}, u32[]{:S(2)}, u32[]{:S(2)}) %collective-permute-start.16) | collective-permute-done | bytes 786464 | tf_op jit(solution)/shard_map/ppermute | solution.py:36
  150.1 14.0 %collective-permute-start.17 = (bf16[256,768]{1,0:T(8,128)(2,1)S(1)}, bf16[256,768]{1,0:T(8,128)(2,1)S(1)}, u32[]{:S(2)}, u32[]{:S(2)}) collective-permute-start(bf16[256,768]{1,0:T(8,128)(2,1)S(1)} %copy-done.74), channel_id=1, source_target_pairs={{0,2},{1,3},{2,0},{3,1},{4,6},{5,7},{6,4},{7,5},{8,10},{9,11},{10,... | collective-permute-start | bytes 1179656 | tf_op jit(solution)/shard_map/ppermute | solution.py:36
  164.1 5.9 %collective-permute-done.18.moved_ref = bf16[512,768]{1,0:T(8,128)(2,1)S(1)} collective-permute-done((bf16[512,768]{1,0:T(8,128)(2,1)}, bf16[512,768]{1,0:T(8,128)(2,1)S(1)}, u32[]{:S(2)}, u32[]{:S(2)}) %collective-permute-start.18) | collective-permute-done | bytes 786464 | tf_op jit(solution)/shard_map/ppermute | solution.py:36
  170.9 23.6 %collective-permute-done.17.moved_ref = bf16[256,768]{1,0:T(8,128)(2,1)S(1)} collective-permute-done((bf16[256,768]{1,0:T(8,128)(2,1)S(1)}, bf16[256,768]{1,0:T(8,128)(2,1)S(1)}, u32[]{:S(2)}, u32[]{:S(2)}) %collective-permute-start.17) | collective-permute-done | bytes 393248 | tf_op jit(solution)/shard_map/ppermute | solution.py:36
  204.7 11.2 %shard_map.94 = (bf16[1024,768]{1,0:T(8,128)(2,1)}, f32[1024,768]{1,0:T(8,128)}, f32[1024,768]{1,0:T(8,128)}) custom-call(bf16[1024,2048]{1,0:T(8,128)(2,1)} %bitcast.1.refs_0_.rows_ref, bf16[512,768]{1,0:T(8,128)(2,1)S(1)} %copy-done.15, bf16[512,768]{1,0:T(8,128)(2,1)S(1)} %copy-done.19, bf16[256,768]{1,0:T(8,128)(2,1)} %shard_map.87.refs_3_.refs_4_, ...), custom_call_target="tpu_custom_call" | custom-call | tf_op jit(solution)/shard_map/pallas_call | solution.py:339
  215.9 20.9 %collective-permute-done.20.moved_ref = bf16[512,768]{1,0:T(8,128)(2,1)S(1)} collective-permute-done((bf16[512,768]{1,0:T(8,128)(2,1)}, bf16[512,768]{1,0:T(8,128)(2,1)S(1)}, u32[]{:S(2)}, u32[]{:S(2)}) %collective-permute-start.20) | collective-permute-done | bytes 786464 | tf_op jit(solution)/shard_map/ppermute | solution.py:36
  237.7 10.1 %all-to-all-done.1 = bf16[8,4,32,2048]{3,2,1,0:T(8,128)(2,1)} async-done(((bf16[8,4,32,2048]{3,2,1,0:T(8,128)(2,1)}), bf16[8,4,32,2048]{3,2,1,0:T(8,128)(2,1)}, u32[]{:S(2)}, u32[]{:S(2)}) %all-to-all-start.1) | async-done | bytes 4194336 | tf_op jit(solution)/shard_map/all_to_all | solution.py:463
  263.9 30.8 %collective-permute-done.23.moved_ref = bf16[256,768]{1,0:T(8,128)(2,1)} collective-permute-done((bf16[256,768]{1,0:T(8,128)(2,1)}, bf16[256,768]{1,0:T(8,128)(2,1)}, u32[]{:S(2)}, u32[]{:S(2)}) %collective-permute-start.23) | collective-permute-done | bytes 393248 | tf_op jit(solution)/shard_map/ppermute | solution.py:36
  295.6 11.2 %shard_map.105 = (bf16[1024,2048]{1,0:T(8,128)(2,1)}, bf16[1024,768]{1,0:T(8,128)(2,1)}, bf16[1024,768]{1,0:T(8,128)(2,1)}) custom-call(bf16[1024,768]{1,0:T(8,128)(2,1)} %get-tuple-element.121.refs_0_, bf16[1024,2048]{1,0:T(8,128)(2,1)} %bitcast.2.rows_ref.refs_1_, f32[1024,768]{1,0:T(8,128)} %get-tuple-element.122.refs_2_, ...), custom_call_target="tpu_custom_call" | custom-call | tf_op jit(solution)/shard_map/pallas_call | solution.py:371
  307.8 7.9 %collective-permute-done.25.moved_ref = bf16[512,768]{1,0:T(8,128)(2,1)} collective-permute-done((bf16[512,768]{1,0:T(8,128)(2,1)}, bf16[512,768]{1,0:T(8,128)(2,1)}, u32[]{:S(2)}, u32[]{:S(2)}) %collective-permute-start.25) | collective-permute-done | bytes 786464 | tf_op jit(solution)/shard_map/ppermute | solution.py:36
  346.4 28.5 %collective-permute-done.46.moved_ref = bf16[256,768]{1,0:T(8,128)(2,1)S(1)} collective-permute-done((bf16[256,768]{1,0:T(8,128)(2,1)S(1)}, bf16[256,768]{1,0:T(8,128)(2,1)S(1)}, u32[]{:S(2)}, u32[]{:S(2)}) %collective-permute-start.46) | collective-permute-done | bytes 393248 | tf_op jit(solution)/shard_map/ppermute | solution.py:36
  375.8 10.8 %shard_map.116 = bf16[1024,2048]{1,0:T(8,128)(2,1)} custom-call(bf16[1024,768]{1,0:T(8,128)(2,1)} %get-tuple-element.151.refs_0_, bf16[1024,768]{1,0:T(8,128)(2,1)} %get-tuple-element.138.refs_1_, bf16[512,768]{1,0:T(8,128)(2,1)S(1)} %copy-done.16, bf16[512,768]{1,0:T(8,128)(2,1)S(1)} %copy-done.20, bf16[256,768]{1,0:T(8,128)(2,1)} %shard_map.87.refs_3_.refs_4_, ...), custom_call_target="tpu_custom_call" | custom-call | tf_op jit(solution)/shard_map/pallas_call | solution.py:399
  390.8 11.7 %shard_map.111 = (bf16[128,2048]{1,0:T(8,128)(2,1)S(1)}, bf16[128,2048]{1,0:T(8,128)(2,1)S(1)}, bf16[128,2048]{1,0:T(8,128)(2,1)S(1)}, bf16[128,2048]{1,0:T(8,128)(2,1)S(1)}, f32[4,4,128]{2,1,0:T(4,128)S(1)}) custom-call(s32[1]{0:T(128)} %bitcast.level_ref, bf16[128,2176]{1,0:T(8,128)(2,1)} %copy-done.3, bf16[128,2176]{1,0:T(8,128)(2,1)} %copy-done.5, ...), custom_call_target="tpu_custom_call" | custom-call | tf_op jit(solution)/shard_map/pallas_call | solution.py:300
  410.4 6.1 %all-to-all-start.3 = ((bf16[8,4,32,2048]{3,2,1,0:T(8,128)(2,1)}), bf16[8,4,32,2048]{3,2,1,0:T(8,128)(2,1)}, u32[]{:S(2)}, u32[]{:S(2)}) async-start(bf16[8,4,32,2048]{3,2,1,0:T(8,128)(2,1)} %bitcast.14), calls=%async_computation.3 | async-start | bytes 8388608 | tf_op jit(solution)/shard_map/all_to_all | solution.py:463
  439.3 13.0 %collective-permute-done.32 = bf16[128,2048]{1,0:T(8,128)(2,1)S(1)} collective-permute-done((bf16[128,2048]{1,0:T(8,128)(2,1)S(1)}, bf16[128,2048]{1,0:T(8,128)(2,1)S(1)}, u32[]{:S(2)}, u32[]{:S(2)}) %collective-permute-start.32) | collective-permute-done | bytes 524320 | tf_op jit(solution)/shard_map/ppermute | solution.py:85
  453.2 11.1 %collective-permute-start.33 = (bf16[128,2048]{1,0:T(8,128)(2,1)}, bf16[128,2048]{1,0:T(8,128)(2,1)}, u32[]{:S(2)}, u32[]{:S(2)}) collective-permute-start(bf16[128,2048]{1,0:T(8,128)(2,1)} %add_convert_fusion.4), channel_id=1, source_target_pairs={{1,0},{2,1},{3,2},{5,4},{6,5},{7,6},{9,8},{10,9},{11,10},{13,12},{... | collective-permute-start | bytes 1572872 | tf_op jit(solution)/shard_map/ppermute | solution.py:85
  464.3 6.5 %shard_map.118 = (bf16[128,2048]{1,0:T(8,128)(2,1)S(1)}, bf16[128,2048]{1,0:T(8,128)(2,1)S(1)}, bf16[128,2048]{1,0:T(8,128)(2,1)S(1)}, bf16[128,2048]{1,0:T(8,128)(2,1)S(1)}) custom-call(s32[1]{0:T(128)} %bitcast.level_ref, bf16[128,2176]{1,0:T(8,128)(2,1)S(1)} %copy-done.4, bf16[128,2176]{1,0:T(8,128)(2,1)S(1)} %copy-done.6, ...), custom_call_target="tpu_custom_call" | custom-call | tf_op jit(solution)/shard_map/pallas_call | solution.py:300
  477.2 6.7 %shard_map.126.refs_4_ = bf16[512,4,2304]{2,1,0:T(4,128)(2,1)} custom-call(s32[1]{0:T(128)} %bitcast.level_ref, bf16[512,768]{1,0:T(8,128)(2,1)S(1)} %copy-done.13, bf16[512,768]{1,0:T(8,128)(2,1)S(1)} %copy-done.39, bf16[512,768]{1,0:T(8,128)(2,1)S(1)} %pad_maximum_fusion.2.refs_2_, bf16[512,768]{1,0:T(8,128)(2,1)} %shard_map.107.refs_3_), custom_call_target="tpu_custom_call" | custom-call | tf_op jit(solution)/shard_map/pallas_call | solution.py:152
  495.2 11.3 %collective-permute-done.44.moved_ref = bf16[512,768]{1,0:T(8,128)(2,1)S(1)} collective-permute-done((bf16[512,768]{1,0:T(8,128)(2,1)S(1)}, bf16[512,768]{1,0:T(8,128)(2,1)S(1)}, u32[]{:S(2)}, u32[]{:S(2)}) %collective-permute-start.44) | collective-permute-done | bytes 786464 | tf_op jit(solution)/shard_map/ppermute | solution.py:36
  507.5 13.5 %collective-permute-done.49.moved_ref = bf16[512,768]{1,0:T(8,128)(2,1)} collective-permute-done((bf16[512,768]{1,0:T(8,128)(2,1)S(1)}, bf16[512,768]{1,0:T(8,128)(2,1)}, u32[]{:S(2)}, u32[]{:S(2)}) %collective-permute-start.49) | collective-permute-done | bytes 786464 | tf_op jit(solution)/shard_map/ppermute | solution.py:36
  521.0 6.6 %shard_map.127.refs_4_ = bf16[512,4,2304]{2,1,0:T(4,128)(2,1)} custom-call(s32[1]{0:T(128)} %bitcast.level_ref, bf16[512,768]{1,0:T(8,128)(2,1)S(1)} %copy-done.33, bf16[512,768]{1,0:T(8,128)(2,1)} %shard_map.110.refs_1_, bf16[512,768]{1,0:T(8,128)(2,1)S(1)} %pad_maximum_fusion.1.refs_2_, ...), custom_call_target="tpu_custom_call", output_to_operand_aliasing={{}: (5, {})} | custom-call | tf_op jit(solution)/shard_map/pallas_call | solution.py:152
  532.3 7.2 %collective-permute-start.50 = (bf16[256,768]{1,0:T(8,128)(2,1)S(1)}, bf16[256,768]{1,0:T(8,128)(2,1)S(1)}, u32[]{:S(2)}, u32[]{:S(2)}) collective-permute-start(bf16[256,768]{1,0:T(8,128)(2,1)S(1)} %copy-done.61), channel_id=1, source_target_pairs={{0,2},{1,3},{2,0},{3,1},{4,6},{5,7},{6,4},{7,5},{8,10},{9,11},{10,... | collective-permute-start | bytes 1179656 | tf_op jit(solution)/shard_map/ppermute | solution.py:36
  549.8 27.0 %collective-permute-done.50.moved_ref = bf16[256,768]{1,0:T(8,128)(2,1)S(1)} collective-permute-done((bf16[256,768]{1,0:T(8,128)(2,1)S(1)}, bf16[256,768]{1,0:T(8,128)(2,1)S(1)}, u32[]{:S(2)}, u32[]{:S(2)}) %collective-permute-start.50) | collective-permute-done | bytes 393248 | tf_op jit(solution)/shard_map/ppermute | solution.py:36
  578.7 6.6 %shard_map.128 = bf16[512,4,2304]{2,1,0:T(4,128)(2,1)} custom-call(s32[1]{0:T(128)} %bitcast.level_ref, bf16[512,768]{1,0:T(8,128)(2,1)S(1)} %copy-done.31, bf16[512,768]{1,0:T(8,128)(2,1)S(1)} %copy-done.37, bf16[512,768]{1,0:T(8,128)(2,1)S(1)} %pad_maximum_fusion.refs_2_, bf16[512,768]{1,0:T(8,128)(2,1)} %shard_map.124.refs_3_, ...), custom_call_target="tpu_custom_call", output_to_operand_aliasing={{}: (5, {})} | custom-call | tf_op jit(solution)/shard_map/pallas_call | solution.py:152
  (306 shorter events, 187.9 us)
Async XLA Ops:
  21.9 63.7 %collective-permute-start.12 = (bf16[512,768]{1,0:T(8,128)(2,1)S(1)}, bf16[512,768]{1,0:T(8,128)(2,1)S(1)}, u32[]{:S(2)}, u32[]{:S(2)}) collective-permute-start(bf16[512,768]{1,0:T(8,128)(2,1)S(1)} %get-tuple-element.108), channel_id=1, source_target_pairs={{0,1},{1,2},{2,3},{3,0},{4,5},{5,6},{6,7},{7,4},{8,9},{9,10},{10,1... | collective-permute-start | bytes 2359304 | tf_op jit(solution)/shard_map/ppermute | solution.py:36
  25.4 47.6 %collective-permute-start.7 = (bf16[128,2048]{1,0:T(8,128)(2,1)S(1)}, bf16[128,2048]{1,0:T(8,128)(2,1)}, u32[]{:S(2)}, u32[]{:S(2)}) collective-permute-start(bf16[128,2048]{1,0:T(8,128)(2,1)S(1)} %copy-done.21), channel_id=1, source_target_pairs={{1,0},{2,1},{3,2},{5,4},{6,5},{7,6},{9,8},{10,9},{11,10},{13,12},{... | collective-permute-start | bytes 1572872 | tf_op jit(solution)/shard_map/ppermute | solution.py:85
  30.8 52.0 %collective-permute-start.2 = (bf16[128,2176]{1,0:T(8,128)(2,1)S(1)}, bf16[128,2176]{1,0:T(8,128)(2,1)S(1)}, u32[]{:S(2)}, u32[]{:S(2)}) collective-permute-start(bf16[128,2176]{1,0:T(8,128)(2,1)S(1)} %collective-permute-done.refs_1_.refs_8_), channel_id=1, source_target_pairs={{1,2},{2,3},{5,6},{6,7},{9,10},{10,11},{13,14},{14,15},{17,18},{18... | collective-permute-start | bytes 1671176 | tf_op jit(solution)/shard_map/ppermute | solution.py:85
  32.1 52.2 %collective-permute-start.3 = (bf16[128,2176]{1,0:T(8,128)(2,1)S(1)}, bf16[128,2176]{1,0:T(8,128)(2,1)S(1)}, u32[]{:S(2)}, u32[]{:S(2)}) collective-permute-start(bf16[128,2176]{1,0:T(8,128)(2,1)S(1)} %collective-permute-done.1.refs_4_.refs_11_), channel_id=1, source_target_pairs={{1,0},{2,1},{5,4},{6,5},{9,8},{10,9},{13,12},{14,13},{17,16},{18,1... | collective-permute-start | bytes 1671176 | tf_op jit(solution)/shard_map/ppermute | solution.py:85
  54.1 33.8 %collective-permute-start.14 = (bf16[512,768]{1,0:T(8,128)(2,1)}, bf16[512,768]{1,0:T(8,128)(2,1)}, u32[]{:S(2)}, u32[]{:S(2)}) collective-permute-start(bf16[512,768]{1,0:T(8,128)(2,1)} %get-tuple-element.110), channel_id=1, source_target_pairs={{0,3},{1,0},{2,1},{3,2},{4,7},{5,4},{6,5},{7,6},{8,11},{9,8},{10,9... | collective-permute-start | bytes 2359304 | tf_op jit(solution)/shard_map/ppermute | solution.py:36
  88.0 34.3 %collective-permute-start.13 = (bf16[256,768]{1,0:T(8,128)(2,1)}, bf16[256,768]{1,0:T(8,128)(2,1)}, u32[]{:S(2)}, u32[]{:S(2)}) collective-permute-start(bf16[256,768]{1,0:T(8,128)(2,1)} %get-tuple-element.109), channel_id=1, source_target_pairs={{0,2},{1,3},{2,0},{3,1},{4,6},{5,7},{6,4},{7,5},{8,10},{9,11},{10,... | collective-permute-start | bytes 1179656 | tf_op jit(solution)/shard_map/ppermute | solution.py:36
  94.2 32.9 %collective-permute-start.15 = (bf16[256,768]{1,0:T(8,128)(2,1)}, bf16[256,768]{1,0:T(8,128)(2,1)}, u32[]{:S(2)}, u32[]{:S(2)}) collective-permute-start(bf16[256,768]{1,0:T(8,128)(2,1)} %get-tuple-element.111), channel_id=1, source_target_pairs={{0,2},{1,3},{2,0},{3,1},{4,6},{5,7},{6,4},{7,5},{8,10},{9,11},{10,... | collective-permute-start | bytes 1179656 | tf_op jit(solution)/shard_map/ppermute | solution.py:36
  117.3 78.0 %all-to-all-start = ((bf16[8,4,32,2048]{3,2,1,0:T(8,128)(2,1)}), bf16[8,4,32,2048]{3,2,1,0:T(8,128)(2,1)}, u32[]{:S(2)}, u32[]{:S(2)}) async-start(bf16[8,4,32,2048]{3,2,1,0:T(8,128)(2,1)} %shard_map.85), calls=%async_computation | async-start | bytes 8388608 | tf_op jit(solution)/shard_map/all_to_all | solution.py:463
  127.1 42.9 %collective-permute-start.18 = (bf16[512,768]{1,0:T(8,128)(2,1)}, bf16[512,768]{1,0:T(8,128)(2,1)S(1)}, u32[]{:S(2)}, u32[]{:S(2)}) collective-permute-start(bf16[512,768]{1,0:T(8,128)(2,1)} %get-tuple-element.118), channel_id=1, source_target_pairs={{0,3},{1,0},{2,1},{3,2},{4,7},{5,4},{6,5},{7,6},{8,11},{9,8},{10,9... | collective-permute-start | bytes 2359304 | tf_op jit(solution)/shard_map/ppermute | solution.py:36
  150.1 44.4 %collective-permute-start.17 = (bf16[256,768]{1,0:T(8,128)(2,1)S(1)}, bf16[256,768]{1,0:T(8,128)(2,1)S(1)}, u32[]{:S(2)}, u32[]{:S(2)}) collective-permute-start(bf16[256,768]{1,0:T(8,128)(2,1)S(1)} %copy-done.74), channel_id=1, source_target_pairs={{0,2},{1,3},{2,0},{3,1},{4,6},{5,7},{6,4},{7,5},{8,10},{9,11},{10,... | collective-permute-start | bytes 1179656 | tf_op jit(solution)/shard_map/ppermute | solution.py:36
  170.9 32.0 %collective-permute-start.19 = (bf16[256,768]{1,0:T(8,128)(2,1)S(1)}, bf16[256,768]{1,0:T(8,128)(2,1)S(1)}, u32[]{:S(2)}, u32[]{:S(2)}) collective-permute-start(bf16[256,768]{1,0:T(8,128)(2,1)S(1)} %copy-done.73), channel_id=1, source_target_pairs={{0,2},{1,3},{2,0},{3,1},{4,6},{5,7},{6,4},{7,5},{8,10},{9,11},{10,... | collective-permute-start | bytes 1179656 | tf_op jit(solution)/shard_map/ppermute | solution.py:36
  195.3 52.5 %all-to-all-start.1 = ((bf16[8,4,32,2048]{3,2,1,0:T(8,128)(2,1)}), bf16[8,4,32,2048]{3,2,1,0:T(8,128)(2,1)}, u32[]{:S(2)}, u32[]{:S(2)}) async-start(bf16[8,4,32,2048]{3,2,1,0:T(8,128)(2,1)} %shard_map.95), calls=%async_computation.1 | async-start | bytes 8388608 | tf_op jit(solution)/shard_map/all_to_all | solution.py:463
  200.1 36.7 %collective-permute-start.20 = (bf16[512,768]{1,0:T(8,128)(2,1)}, bf16[512,768]{1,0:T(8,128)(2,1)S(1)}, u32[]{:S(2)}, u32[]{:S(2)}) collective-permute-start(bf16[512,768]{1,0:T(8,128)(2,1)} %get-tuple-element.126), channel_id=1, source_target_pairs={{0,1},{1,2},{2,3},{3,0},{4,5},{5,6},{6,7},{7,4},{8,9},{9,10},{10,1... | collective-permute-start | bytes 2359304 | tf_op jit(solution)/shard_map/ppermute | solution.py:36
  203.7 34.0 %collective-permute-start.22 = (bf16[512,768]{1,0:T(8,128)(2,1)}, bf16[512,768]{1,0:T(8,128)(2,1)}, u32[]{:S(2)}, u32[]{:S(2)}) collective-permute-start(bf16[512,768]{1,0:T(8,128)(2,1)} %get-tuple-element.130), channel_id=1, source_target_pairs={{0,3},{1,0},{2,1},{3,2},{4,7},{5,4},{6,5},{7,6},{8,11},{9,8},{10,9... | collective-permute-start | bytes 2359304 | tf_op jit(solution)/shard_map/ppermute | solution.py:36
  263.1 31.5 %collective-permute-start.23 = (bf16[256,768]{1,0:T(8,128)(2,1)}, bf16[256,768]{1,0:T(8,128)(2,1)}, u32[]{:S(2)}, u32[]{:S(2)}) collective-permute-start(bf16[256,768]{1,0:T(8,128)(2,1)} %get-tuple-element.131), channel_id=1, source_target_pairs={{0,2},{1,3},{2,0},{3,1},{4,6},{5,7},{6,4},{7,5},{8,10},{9,11},{10,... | collective-permute-start | bytes 1179656 | tf_op jit(solution)/shard_map/ppermute | solution.py:36
  263.9 43.0 %collective-permute-start.24 = (bf16[512,768]{1,0:T(8,128)(2,1)S(1)}, bf16[512,768]{1,0:T(8,128)(2,1)S(1)}, u32[]{:S(2)}, u32[]{:S(2)}) collective-permute-start(bf16[512,768]{1,0:T(8,128)(2,1)S(1)} %shard_map.97), channel_id=1, source_target_pairs={{0,3},{1,0},{2,1},{3,2},{4,7},{5,4},{6,5},{7,6},{8,11},{9,8},{10,9... | collective-permute-start | bytes 2359304 | tf_op jit(solution)/shard_map/ppermute | solution.py:36
  307.8 36.4 %collective-permute-start.26 = (bf16[256,768]{1,0:T(8,128)(2,1)}, bf16[256,768]{1,0:T(8,128)(2,1)}, u32[]{:S(2)}, u32[]{:S(2)}) collective-permute-start(bf16[256,768]{1,0:T(8,128)(2,1)} %copy-done.53), channel_id=1, source_target_pairs={{0,2},{1,3},{2,0},{3,1},{4,6},{5,7},{6,4},{7,5},{8,10},{9,11},{10,... | collective-permute-start | bytes 1179656 | tf_op jit(solution)/shard_map/ppermute | solution.py:36
  339.8 35.2 %collective-permute-start.46 = (bf16[256,768]{1,0:T(8,128)(2,1)S(1)}, bf16[256,768]{1,0:T(8,128)(2,1)S(1)}, u32[]{:S(2)}, u32[]{:S(2)}) collective-permute-start(bf16[256,768]{1,0:T(8,128)(2,1)S(1)} %shard_map.99), channel_id=1, source_target_pairs={{0,2},{1,3},{2,0},{3,1},{4,6},{5,7},{6,4},{7,5},{8,10},{9,11},{10,... | collective-permute-start | bytes 1179656 | tf_op jit(solution)/shard_map/ppermute | solution.py:36
  339.8 51.0 %all-to-all-start.2 = ((bf16[8,4,32,2048]{3,2,1,0:T(8,128)(2,1)}), bf16[8,4,32,2048]{3,2,1,0:T(8,128)(2,1)}, u32[]{:S(2)}, u32[]{:S(2)}) async-start(bf16[8,4,32,2048]{3,2,1,0:T(8,128)(2,1)} %bitcast.15), calls=%async_computation.2 | async-start | bytes 8388608 | tf_op jit(solution)/shard_map/all_to_all | solution.py:463
  344.3 43.3 %collective-permute-start.27 = (bf16[512,768]{1,0:T(8,128)(2,1)}, bf16[512,768]{1,0:T(8,128)(2,1)}, u32[]{:S(2)}, u32[]{:S(2)}) collective-permute-start(bf16[512,768]{1,0:T(8,128)(2,1)} %get-tuple-element.141), channel_id=1, source_target_pairs={{0,3},{1,0},{2,1},{3,2},{4,7},{5,4},{6,5},{7,6},{8,11},{9,8},{10,9... | collective-permute-start | bytes 2359304 | tf_op jit(solution)/shard_map/ppermute | solution.py:36
  388.6 41.7 %collective-permute-start.34 = (bf16[256,768]{1,0:T(8,128)(2,1)S(1)}, bf16[256,768]{1,0:T(8,128)(2,1)}, u32[]{:S(2)}, u32[]{:S(2)}) collective-permute-start(bf16[256,768]{1,0:T(8,128)(2,1)S(1)} %copy-done.67), channel_id=1, source_target_pairs={{0,2},{1,3},{2,0},{3,1},{4,6},{5,7},{6,4},{7,5},{8,10},{9,11},{10,... | collective-permute-start | bytes 1179656 | tf_op jit(solution)/shard_map/ppermute | solution.py:36
  410.4 53.9 %all-to-all-start.3 = ((bf16[8,4,32,2048]{3,2,1,0:T(8,128)(2,1)}), bf16[8,4,32,2048]{3,2,1,0:T(8,128)(2,1)}, u32[]{:S(2)}, u32[]{:S(2)}) async-start(bf16[8,4,32,2048]{3,2,1,0:T(8,128)(2,1)} %bitcast.14), calls=%async_computation.3 | async-start | bytes 8388608 | tf_op jit(solution)/shard_map/all_to_all | solution.py:463
  430.3 34.0 %collective-permute-start.48 = (bf16[256,768]{1,0:T(8,128)(2,1)S(1)}, bf16[256,768]{1,0:T(8,128)(2,1)}, u32[]{:S(2)}, u32[]{:S(2)}) collective-permute-start(bf16[256,768]{1,0:T(8,128)(2,1)S(1)} %copy-done.65), channel_id=1, source_target_pairs={{0,2},{1,3},{2,0},{3,1},{4,6},{5,7},{6,4},{7,5},{8,10},{9,11},{10,... | collective-permute-start | bytes 1179656 | tf_op jit(solution)/shard_map/ppermute | solution.py:36
  438.0 46.0 %collective-permute-start.30 = (bf16[128,2048]{1,0:T(8,128)(2,1)}, bf16[128,2048]{1,0:T(8,128)(2,1)}, u32[]{:S(2)}, u32[]{:S(2)}) collective-permute-start(bf16[128,2048]{1,0:T(8,128)(2,1)} %add_convert_fusion.5), channel_id=1, source_target_pairs={{0,1},{1,2},{2,3},{4,5},{5,6},{6,7},{8,9},{9,10},{10,11},{12,13},{... | collective-permute-start | bytes 1572872 | tf_op jit(solution)/shard_map/ppermute | solution.py:85
  453.2 30.8 %collective-permute-start.33 = (bf16[128,2048]{1,0:T(8,128)(2,1)}, bf16[128,2048]{1,0:T(8,128)(2,1)}, u32[]{:S(2)}, u32[]{:S(2)}) collective-permute-start(bf16[128,2048]{1,0:T(8,128)(2,1)} %add_convert_fusion.4), channel_id=1, source_target_pairs={{1,0},{2,1},{3,2},{5,4},{6,5},{7,6},{9,8},{10,9},{11,10},{13,12},{... | collective-permute-start | bytes 1572872 | tf_op jit(solution)/shard_map/ppermute | solution.py:85
  486.2 34.7 %collective-permute-start.49 = (bf16[512,768]{1,0:T(8,128)(2,1)S(1)}, bf16[512,768]{1,0:T(8,128)(2,1)}, u32[]{:S(2)}, u32[]{:S(2)}) collective-permute-start(bf16[512,768]{1,0:T(8,128)(2,1)S(1)} %copy-done.57), channel_id=1, source_target_pairs={{0,1},{1,2},{2,3},{3,0},{4,5},{5,6},{6,7},{7,4},{8,9},{9,10},{10,1... | collective-permute-start | bytes 2359304 | tf_op jit(solution)/shard_map/ppermute | solution.py:36
  491.3 36.3 %collective-permute-start.36 = (bf16[128,2048]{1,0:T(8,128)(2,1)}, bf16[128,2048]{1,0:T(8,128)(2,1)}, u32[]{:S(2)}, u32[]{:S(2)}) collective-permute-start(bf16[128,2048]{1,0:T(8,128)(2,1)} %get-tuple-element.186), channel_id=1, source_target_pairs={{0,1},{1,2},{4,5},{5,6},{8,9},{9,10},{12,13},{13,14},{16,17},{17,1... | collective-permute-start | bytes 1572872 | tf_op jit(solution)/shard_map/ppermute | solution.py:85
  492.8 39.5 %collective-permute-start.39 = (bf16[128,2048]{1,0:T(8,128)(2,1)}, bf16[128,2048]{1,0:T(8,128)(2,1)}, u32[]{:S(2)}, u32[]{:S(2)}) collective-permute-start(bf16[128,2048]{1,0:T(8,128)(2,1)} %get-tuple-element.187), channel_id=1, source_target_pairs={{2,1},{3,2},{6,5},{7,6},{10,9},{11,10},{14,13},{15,14},{18,17},{19... | collective-permute-start | bytes 1572872 | tf_op jit(solution)/shard_map/ppermute | solution.py:85
  507.4 42.4 %collective-permute-start.45 = (bf16[256,768]{1,0:T(8,128)(2,1)S(1)}, bf16[256,768]{1,0:T(8,128)(2,1)}, u32[]{:S(2)}, u32[]{:S(2)}) collective-permute-start(bf16[256,768]{1,0:T(8,128)(2,1)S(1)} %copy-done.63), channel_id=1, source_target_pairs={{0,2},{1,3},{2,0},{3,1},{4,6},{5,7},{6,4},{7,5},{8,10},{9,11},{10,... | collective-permute-start | bytes 1179656 | tf_op jit(solution)/shard_map/ppermute | solution.py:36
  528.8 56.5 %collective-permute-start.37 = (bf16[128,2048]{1,0:T(8,128)(2,1)S(1)}, bf16[128,2048]{1,0:T(8,128)(2,1)}, u32[]{:S(2)}, u32[]{:S(2)}) collective-permute-start(bf16[128,2048]{1,0:T(8,128)(2,1)S(1)} %add_convert_fusion.2), channel_id=1, source_target_pairs={{0,1},{1,2},{2,3},{4,5},{5,6},{6,7},{8,9},{9,10},{10,11},{12,13},{... | collective-permute-start | bytes 1572872 | tf_op jit(solution)/shard_map/ppermute | solution.py:85
  532.3 44.4 %collective-permute-start.50 = (bf16[256,768]{1,0:T(8,128)(2,1)S(1)}, bf16[256,768]{1,0:T(8,128)(2,1)S(1)}, u32[]{:S(2)}, u32[]{:S(2)}) collective-permute-start(bf16[256,768]{1,0:T(8,128)(2,1)S(1)} %copy-done.61), channel_id=1, source_target_pairs={{0,2},{1,3},{2,0},{3,1},{4,6},{5,7},{6,4},{7,5},{8,10},{9,11},{10,... | collective-permute-start | bytes 1179656 | tf_op jit(solution)/shard_map/ppermute | solution.py:36
  541.5 43.8 %collective-permute-start.40 = (bf16[128,2048]{1,0:T(8,128)(2,1)}, bf16[128,2048]{1,0:T(8,128)(2,1)}, u32[]{:S(2)}, u32[]{:S(2)}) collective-permute-start(bf16[128,2048]{1,0:T(8,128)(2,1)} %add_convert_fusion.1), channel_id=1, source_target_pairs={{1,0},{2,1},{3,2},{5,4},{6,5},{7,6},{9,8},{10,9},{11,10},{13,12},{... | collective-permute-start | bytes 1572872 | tf_op jit(solution)/shard_map/ppermute | solution.py:85
  (102 other events, 1580.4 us)

commit v2 on v1

--- a/solution.py
+++ b/solution.py
@@ -13,6 +13,33 @@
 META = 128
 LANES = 2
 FLOPS_PER_VALUE = 40000
+BACK_TURNS = (2, 0, 1)
+MIDDLE_FIRST = (False, False)
+WAITS = {3: ['t2'],
+ 4: ['g1'],
+ 5: ['t3'],
+ 6: ['g2'],
+ 7: ['g3'],
+ 10: ['units_pass', 'cotangent'],
+ 12: ['middle_down_grad', 'own_down_grad', 'other_down_grads'],
+ 17: ['row_grad'],
+ 18: ['back_out'],
+ 19: ['out_parts'],
+ 20: ['o1'],
+ 21: ['o2', 'back_grad'],
+ 22: ['o3', 'grad_parts', 'gate_grad']}
+GATES = {'back_out': [12],
+ 'down': ['other_down_grads', 'middle_down_grad', 'own_down_grad'],
+ 'g1': ['t1'],
+ 'grad_parts': [19],
+ 'join0': [19],
+ 'join1': [21],
+ 'middle_in_grad': ['row_grad'],
+ 'other_in_grads': [13],
+ 'out_sums': [16],
+ 'own_in_grad': [18],
+ 'row_grad': ['other_in_grads', 14],
+ 't2': ['split']}
 
 
 def dot(a, b, dims):
@@ -69,15 +96,15 @@
         self.sent.append(moved)
         return moved
 
-    def send_all(self, blocks, sign, order, others=()):
-        waits = iter(others)
-        return {
-            k: [self.send(x, sign * k, next(waits, ())) if k else x for x in blocks[k]]
-            for k in order
-        }
-
-    def done(self, i):
-        return self.sent[min(i, len(self.sent) - 1)]
+
+class Parts:
+    def __init__(self):
+        self.made = {}
+
+    def __call__(self, name):
+        if name not in self.made:
+            self.made[name] = getattr(self, name)()
+        return self.made[name]
 
 
 def hop(x, up, sources):
@@ -85,20 +112,18 @@
     return lax.ppermute(x, "narrow", [(i, i + step) for i in sources])
 
 
-def reduce_chain(parts):
+def reduce_step(parts, last, step):
     n = len(parts)
-    up = down = None
-    steps = []
-    for step in range(1, n):
-        up_send, down_send = parts[step], parts[n - step]
-        if up is not None:
-            up_send = (up_send.astype(F32) + up.astype(F32)).astype(BF16)
-            down_send = (down_send.astype(F32) + down.astype(F32)).astype(BF16)
-        up = hop(up_send, True, range(step))
-        down = hop(down_send, False, range(n - step, n))
-        steps.append((up, down))
-    total = parts[0].astype(F32) + up.astype(F32) + down.astype(F32)
-    return total.astype(BF16), steps
+    up_send, down_send = parts[step], parts[n - step]
+    if last is not None:
+        up_send = (up_send.astype(F32) + last[0].astype(F32)).astype(BF16)
+        down_send = (down_send.astype(F32) + last[1].astype(F32)).astype(BF16)
+    return hop(up_send, True, range(step)), hop(down_send, False, range(n - step, n))
+
+
+def reduce_end(parts, last):
+    total = parts[0].astype(F32) + last[0].astype(F32) + last[1].astype(F32)
+    return total.astype(BF16)
 
 
 def mixing(level, n, depth):
@@ -448,122 +473,208 @@
     pad = jnp.zeros((token_count, META - 4 * chosen), BF16)
     sent = jnp.concatenate([tokens, routes.astype(BF16), *thirds, pad], axis=1)
     middle = n // 2
-    order = [k for k in range(1, n) if k != middle] + [middle, 0]
+    others = [k for k in range(1, n) if k != middle]
+    blocks = split_shard(level, expert_weights, units)
+    lanes = Lanes(LANES, ())
 
     def halves(k):
         return 2 if k == middle else 1
 
-    def pieces(blocks):
-        return [jnp.split(x, halves(k)) for k, x in enumerate(blocks)]
-
-    def in_order(moved):
-        return [x for k in range(n) for x in moved[k]]
-
     def swap(x):
+        x = x.reshape(groups, n, capacity, model)
         return lax.all_to_all(x, "wide", split_axis=0, concat_axis=0, tiled=True)
 
-    def as_slots(x):
-        return x.reshape(groups, n, capacity, model)
-
-    gate_blocks, up_blocks, down_blocks = split_shard(level, expert_weights, units)
-
-    def hop_on(ups, downs, *others):
+    def place(x, gated):
+        token_blocks = part("token_blocks")
+        return dispatch(
+            level, token_blocks, blocks=x, groups=groups, capacity=capacity, chosen=chosen, gated=gated
+        )
+
+    def gated(name, x):
+        waits = [
+            part(y) if isinstance(y, str) else lanes.sent[y * n // 4] for y in GATES.get(name, ())
+        ]
+        return after(x, *waits) if waits else x
+
+    def hop_on(ups, downs, name):
         step = len(ups)
-        up, down = after((ups[-1], downs[-1]), others)
+        up, down = gated(name, (ups[-1], downs[-1]))
         ups.append(hop(up, True, range(step - 1, n - 1)))
         downs.append(hop(down, False, range(1, n - step + 1)))
 
-    token_up, token_down, grad_up, grad_down = [sent], [sent], [out_grad], [out_grad]
-    hop_on(token_up, token_down)
-    lanes = Lanes(LANES, (token_up[1], token_down[1]))
-    for step in range(2, n):
-        hop_on(token_up, token_down, gate_blocks if step == 2 else ())
-    for step in range(1, n):
-        hop_on(grad_up, grad_down, token_up[1], token_down[1])
-    token_blocks = token_up + token_down[1:]
-    grad_blocks = grad_up + grad_down[1:]
-
-    def both_ways(ups, downs, step):
-        return ups[min(step, n - 1)], downs[min(step, n - 1)]
-
-    tokens_at = functools.partial(both_ways, token_up, token_down)
-    grads_at = functools.partial(both_ways, grad_up, grad_down)
-    waits = ((), (), (), tokens_at(2), grads_at(1), tokens_at(n - 1), grads_at(2), grads_at(n - 1))
-    gates = in_order(lanes.send_all(pieces(gate_blocks), 1, order, waits[:4]))
-    ups = in_order(lanes.send_all(pieces(up_blocks), 1, order, waits[4:]))
-
-    place = functools.partial(
-        dispatch, level, token_blocks, groups=groups, capacity=capacity, chosen=chosen
-    )
-    rows_in = swap(place(blocks=token_blocks, gated=False)).reshape(slots, model)
-    cotangent = swap(place(blocks=grad_blocks, gated=True)).reshape(slots, model)
-    hidden, active, slope = hidden_pass(rows_in, gates, ups, tile)
-    waits = (rows_in, (), hidden, cotangent)
-    downs = in_order(lanes.send_all(pieces(down_blocks), 1, order, waits))
-
-    def weight_grads(rows, *parts):
+    def moved(group):
+        return [x for k in range(n) for x in came[group][k]]
+
+    came = [{0: [x[0]]} for x in blocks] + [{} for _ in blocks]
+    part = Parts()
+    steps = [n - 1 if i == 3 else i * (n - 1) // 3 for i in range(4)]
+    lines = {"t": ([sent], [sent]), "g": ([out_grad], [out_grad])}
+
+    def line_part(letter, i):
+        def make():
+            if i > 1:
+                part(f"{letter}{i - 1}")
+            ups, downs = lines[letter]
+            while len(ups) <= steps[i]:
+                hop_on(ups, downs, f"{letter}{i}")
+            return ups[-1], downs[-1]
+
+        return make
+
+    def sum_part(letter, i):
+        def make():
+            last = part(f"{letter}{i - 1}") if i > 1 else None
+            parts = part("out_parts" if letter == "o" else "grad_parts")
+            for step in range(steps[i - 1] + 1, steps[i] + 1):
+                last = reduce_step(parts, last, step)
+            return last
+
+        return make
+
+    for i in (1, 2, 3):
+        for letter in "tg":
+            setattr(part, f"{letter}{i}", line_part(letter, i))
+        for letter in "or":
+            setattr(part, f"{letter}{i}", sum_part(letter, i))
+
+    def define(make):
+        setattr(part, make.__name__, make)
+
+    @define
+    def split():
+        return blocks
+
+    @define
+    def token_blocks():
+        part("t3")
+        return lines["t"][0] + lines["t"][1][1:]
+
+    @define
+    def grad_blocks():
+        part("g3")
+        return lines["g"][0] + lines["g"][1][1:]
+
+    @define
+    def rows():
+        return swap(place(part("token_blocks"), False)).reshape(slots, model)
+
+    @define
+    def cotangent():
+        return swap(place(part("grad_blocks"), True)).reshape(slots, model)
+
+    @define
+    def units_pass():
+        return hidden_pass(gated("units_pass", part("rows")), moved(0), moved(1), tile)
+
+    def grad_pieces(k, rows, *parts):
         made = [
-            [
-                weight_grad(rows, parts, k * halves(k) + i, width // halves(k))
-                for i in range(halves(k))
-            ]
-            for k in range(n)
+            weight_grad(rows, parts, k * halves(k) + i, width // halves(k))
+            for i in range(halves(k))
         ]
-        return [[[x[j] for x in blocks] for blocks in made] for j in range(len(parts))]
-
-    def send_back(blocks, others=()):
-        moved, waits = {0: blocks[0]}, list(others)
-        for k in order[:-1]:
-            moved[k] = []
-            for x in blocks[k]:
-                wait = waits.pop(0) if waits else ()
-                moved[k].append(lanes.send(x, -k, wait() if callable(wait) else wait))
-        return [jnp.concatenate(moved[k]) if halves(k) > 1 else moved[k][0] for k in range(n)]
-
-    (down_grads,) = weight_grads(cotangent, hidden)
-    hidden = after(hidden, down_grads)
-    first = len(lanes.sent)
-    down_grads = send_back(down_grads)
-    expert_out, gate_part, up_part = down_pass(hidden, cotangent, active, slope, downs, tile)
-    back_out = swap(as_slots(after(expert_out, lanes.done(first))))
-    gate_grads, up_grads = weight_grads(
-        rows_in, after(gate_part, lanes.done(first + 1)), up_part
-    )
-    row_grad = row_grad_pass(
-        after(gate_part, gate_grads, lanes.done(first + 2)), up_part, gates, ups, tile
-    )
-    back_grad = swap(as_slots(after(row_grad, back_out)))
-
-    sums = {}
-
-    def sum_outputs():
-        back = after(back_out, lanes.done(first + 4))
-        *parts, sums["dots"] = combine(level, token_blocks, back, chosen, grad_blocks)
-        sums["output"], sums["steps"] = reduce_chain(parts)
-        return parts
-
-    gate_grads = send_back(gate_grads, ((), row_grad, (), sum_outputs))
-    layer_output, out_steps, dots = sums["output"], sums["steps"], sums["dots"]
-    gate_grad = dots[0] + sum(shift(dots[d], -d) for d in range(1, n))
-    grad_parts = combine(
-        level, token_blocks, after(back_grad, lanes.done(first + 6)), chosen
-    )
-    token_grad, grad_steps = reduce_chain(grad_parts)
-    up_grads = send_back(
-        up_grads,
-        (
-            (out_steps[0], back_grad),
-            (out_steps[1], grad_parts),
-            (out_steps[-1], grad_steps[0]),
-            (grad_steps[1], gate_grad),
-        ),
-    )
-
-    columns = 3 * units
-    shard = join_shard(level, after(down_grads, lanes.done(first + 7)), columns, 2)
-    shard = join_shard(level, after(gate_grads, lanes.done(first + 9)), columns, 0, shard)
-    shard = join_shard(level, up_grads, columns, 1, shard)
-    return (layer_output, token_grad, gate_grad.T, shard)
+        return [[x[j] for x in made] for j in range(len(parts))]
+
+    def down_grad(k, name):
+        return grad_pieces(k, part("cotangent"), gated(name, part("units_pass")[0]))[0]
+
+    def in_grad(k, name):
+        _, gate_part, up_part = part("down")
+        return grad_pieces(k, part("rows"), gated(name, gate_part), up_part)
+
+    @define
+    def middle_down_grad():
+        return {middle: down_grad(middle, "middle_down_grad")}
+
+    @define
+    def other_down_grads():
+        return {k: down_grad(k, "other_down_grads") for k in others}
+
+    @define
+    def own_down_grad():
+        return {0: down_grad(0, "own_down_grad")}
+
+    @define
+    def down():
+        hidden, active, slope = part("units_pass")
+        return down_pass(gated("down", hidden), part("cotangent"), active, slope, moved(2), tile)
+
+    @define
+    def middle_in_grad():
+        return {middle: in_grad(middle, "middle_in_grad")}
+
+    @define
+    def other_in_grads():
+        return {k: in_grad(k, "other_in_grads") for k in others}
+
+    @define
+    def own_in_grad():
+        return {0: in_grad(0, "own_in_grad")}
+
+    @define
+    def row_grad():
+        _, gate_part, up_part = part("down")
+        return row_grad_pass(gated("row_grad", gate_part), up_part, moved(0), moved(1), tile)
+
+    @define
+    def back_out():
+        return swap(gated("back_out", part("down")[0]))
+
+    @define
+    def back_grad():
+        return swap(gated("back_grad", after(part("row_grad"), part("back_out"))))
+
+    @define
+    def out_sums():
+        back = gated("out_sums", part("back_out"))
+        return combine(level, part("token_blocks"), back, chosen, part("grad_blocks"))
+
+    @define
+    def out_parts():
+        return part("out_sums")[:-1]
+
+    @define
+    def grad_parts():
+        return combine(level, part("token_blocks"), gated("grad_parts", part("back_grad")), chosen)
+
+    @define
+    def gate_grad():
+        dots = gated("gate_grad", part("out_sums")[-1])
+        return dots[0] + sum(shift(dots[d], -d) for d in range(1, n))
+
+    def joined(group, name, shard=None):
+        grads = [part(own)[0] for own in ("own_down_grad",)] if group == 2 else None
+        if grads is None:
+            grads = [part("own_in_grad")[0][group]]
+        grads = [jnp.concatenate(x) for x in grads]
+        grads += [jnp.concatenate(came[3 + group][k]) for k in range(1, n)]
+        return join_shard(level, gated(name, grads), 3 * units, group, shard)
+
+    def pieces_of(group, back, k):
+        if not back:
+            return jnp.split(blocks[group][k], halves(k))
+        name = "middle" if k == middle else "other"
+        if group == 2:
+            return part("middle_down_grad" if k == middle else "other_down_grads")[k]
+        return part("middle_in_grad" if k == middle else "other_in_grads")[k][group]
+
+    part("t1")
+    lanes.latest = [part("t1")] * LANES
+    for back, turns in ((False, (0, 1, 2)), (True, BACK_TURNS)):
+        for group in turns:
+            order = [middle, *others] if MIDDLE_FIRST[back] else [*others, middle]
+            for k in order:
+                arrived = came[group + (3 if back else 0)].setdefault(k, [])
+                for i in range(halves(k)):
+                    names = WAITS.get(len(lanes.sent) * 4 // n, ())
+                    names = names if len(lanes.sent) % max(1, n // 4) == 0 else ()
+                    waits = [part(name) for name in names]
+                    x = pieces_of(group, back, k)[i]
+                    arrived.append(lanes.send(x, -k if back else k, waits))
+    layer_output = reduce_end(part("out_parts"), part("o3"))
+    token_grad = reduce_end(part("grad_parts"), part("r3"))
+    shard = None
+    for i, group in enumerate(BACK_TURNS):
+        shard = joined(group, f"join{i}", shard)
+    return (layer_output, token_grad, part("gate_grad").T, shard)
 
 
 def solution(mesh):

time: 591 us -> 568 us (0.961)
  the two profiles are of different devices: /device:TPU:26 before, /device:TPU:0 now
where the time goes in v2:
time: 568 us; the launch traced here: 565 us
  waiting for transfers between devices  197 us (35%)
  starting transfers between devices  188 us (33%)
  Pallas kernels  127 us (22%)
  local copies, waits for them, and re-layouts  31.9 us (6%)
  other arithmetic  19.4 us (3%)
    ppermute x27, waiting for transfers between devices, shift(): return lax.ppermute(x, 'narrow', [(i, (i + k) % n) for i in range(n)])  131 us
    ppermute x27, starting transfers between devices, shift(): return lax.ppermute(x, 'narrow', [(i, (i + k) % n) for i in range(n)])  116 us
    ppermute x24, waiting for transfers between devices, hop(): return lax.ppermute(x, 'narrow', [(i, i + step) for i in sources])  60.2 us
    ppermute x24, starting transfers between devices, hop(): return lax.ppermute(x, 'narrow', [(i, i + step) for i in sources])  53.6 us
    pallas_call x10, Pallas kernels, weight_grad(): pl.pallas_call(weight_grad_kernel, out_shape=[jax.ShapeDtypeStruct((width...  33.5 us
    unnamed x147, local copies, waits for them, and re-layouts  26.5 us
    pallas_call x2, Pallas kernels, combine(): pl.pallas_call(functools.partial(kernel, n, chosen), out_shape=out_shape,...  18.7 us
    all_to_all x4, starting transfers between devices, swap(): return lax.all_to_all(x, 'wide', split_axis=0, concat_axis=0, tiled=True)  18.3 us
  transfers between devices with their start and end apart: 55, of which 27 were waited for; matrix products, arithmetic and copies ran while one was open for 3% of the time, Pallas kernels for 22%

profile of v2, /device:TPU:0, one launch (start us, length us, event | category | flops | bytes accessed | tf_op | source)
XLA Modules:
  0.0 565.2 jit_solution(10672567540730306316)
XLA Ops:
  5.7 5.6 collective-permute-start
  11.3 9.7 %shard_map.84 = (bf16[512,768]{1,0:T(8,128)(2,1)S(1)}, bf16[512,768]{1,0:T(8,128)(2,1)S(1)}, bf16[512,768]{1,0:T(8,128)(2,1)S(1)}, bf16[512,768]{1,0:T(8,128)(2,...) custom-call(s32[1]{0:T(128)} %bitcast.level_ref, ...), custom_call_target="tpu_custom_call" | custom-call | tf_op jit(solution)/shard_map/pallas_call | solution.py:150
  37.3 15.5 %collective-permute-done.6.refs_8_ = bf16[128,2048]{1,0:T(8,128)(2,1)} collective-permute-done((bf16[128,2048]{1,0:T(8,128)(2,1)S(1)}, bf16[128,2048]{1,0:T(8,128)(2,1)}, u32[]{:S(2)}, u32[]{:S(2)}) %collective-permute-start.6) | collective-permute-done | bytes 524320 | tf_op jit(solution)/shard_map/ppermute | solution.py:112
  52.8 6.9 %collective-permute-start.14 = (bf16[512,768]{1,0:T(8,128)(2,1)}, bf16[512,768]{1,0:T(8,128)(2,1)}, u32[]{:S(2)}, u32[]{:S(2)}) collective-permute-start(bf16[512,768]{1,0:T(8,128)(2,1)} %get-tuple-element.104), channel_id=1, source_target_pairs={{0,3},{1,0},{2,1},{3,2},{4,7},{5,4},{6,5},{7,6},{8,11},{9,8},{10,9... | collective-permute-start | bytes 2359304 | tf_op jit(solution)/shard_map/ppermute | solution.py:63
  70.5 14.0 %collective-permute-done.14.moved_ref = bf16[512,768]{1,0:T(8,128)(2,1)} collective-permute-done((bf16[512,768]{1,0:T(8,128)(2,1)}, bf16[512,768]{1,0:T(8,128)(2,1)}, u32[]{:S(2)}, u32[]{:S(2)}) %collective-permute-start.14) | collective-permute-done | bytes 786464 | tf_op jit(solution)/shard_map/ppermute | solution.py:63
  84.5 10.3 %collective-permute-start.13 = (bf16[256,768]{1,0:T(8,128)(2,1)}, bf16[256,768]{1,0:T(8,128)(2,1)}, u32[]{:S(2)}, u32[]{:S(2)}) collective-permute-start(bf16[256,768]{1,0:T(8,128)(2,1)} %get-tuple-element.103), channel_id=1, source_target_pairs={{0,2},{1,3},{2,0},{3,1},{4,6},{5,7},{6,4},{7,5},{8,10},{9,11},{10,... | collective-permute-start | bytes 1179656 | tf_op jit(solution)/shard_map/ppermute | solution.py:63
  94.7 16.5 %collective-permute-start.15 = (bf16[256,768]{1,0:T(8,128)(2,1)}, bf16[256,768]{1,0:T(8,128)(2,1)}, u32[]{:S(2)}, u32[]{:S(2)}) collective-permute-start(bf16[256,768]{1,0:T(8,128)(2,1)} %get-tuple-element.105), channel_id=1, source_target_pairs={{0,2},{1,3},{2,0},{3,1},{4,6},{5,7},{6,4},{7,5},{8,10},{9,11},{10,... | collective-permute-start | bytes 1179656 | tf_op jit(solution)/shard_map/ppermute | solution.py:63
  115.9 6.6 %shard_map.85 = bf16[8,4,32,2048]{3,2,1,0:T(8,128)(2,1)} custom-call(s32[1]{0:T(128)} %bitcast.level_ref, bf16[128,2176]{1,0:T(8,128)(2,1)S(1)} %concatenate.12.refs_0_.refs_7_, bf16[128,2176]{1,0:T(8,128)(2,1)S(1)} %collective-permute-done.refs_1_.refs_8_, bf16[128,2176]{1,0:T(8,128)(2,1)S(1)} %collective-permute-done.2.refs_2_.refs_9_, ...), custom_call_target="tpu_custom_call" | custom-call | tf_op jit(solution)/shard_map/pallas_call | solution.py:251
  127.1 6.6 %collective-permute-start.16 = (bf16[512,768]{1,0:T(8,128)(2,1)}, bf16[512,768]{1,0:T(8,128)(2,1)S(1)}, u32[]{:S(2)}, u32[]{:S(2)}) collective-permute-start(bf16[512,768]{1,0:T(8,128)(2,1)} %get-tuple-element.106), channel_id=1, source_target_pairs={{0,1},{1,2},{2,3},{3,0},{4,5},{5,6},{6,7},{7,4},{8,9},{9,10},{10,1... | collective-permute-start | bytes 2359304 | tf_op jit(solution)/shard_map/ppermute | solution.py:63
  133.7 21.3 %collective-permute-done.11.refs_13_ = bf16[128,2048]{1,0:T(8,128)(2,1)} collective-permute-done((bf16[128,2048]{1,0:T(8,128)(2,1)}, bf16[128,2048]{1,0:T(8,128)(2,1)}, u32[]{:S(2)}, u32[]{:S(2)}) %collective-permute-start.11) | collective-permute-done | bytes 524320 | tf_op jit(solution)/shard_map/ppermute | solution.py:112
  155.0 7.1 %shard_map.95 = bf16[8,4,32,2048]{3,2,1,0:T(8,128)(2,1)} custom-call(s32[1]{0:T(128)} %bitcast.level_ref, bf16[128,2176]{1,0:T(8,128)(2,1)} %copy-done.4, bf16[128,2176]{1,0:T(8,128)(2,1)} %copy-done.7, bf16[128,2176]{1,0:T(8,128)(2,1)} %copy-done.9, bf16[128,2176]{1,0:T(8,128)(2,1)} %copy-done.12, bf16[128,2176]{1,0:T(8,128)(2,1)} %copy-done.6, ...), custom_call_target="tpu_custom_call" | custom-call | tf_op jit(solution)/shard_map/pallas_call | solution.py:251
  163.3 6.1 %collective-permute-done.18.moved_ref = bf16[512,768]{1,0:T(8,128)(2,1)S(1)} collective-permute-done((bf16[512,768]{1,0:T(8,128)(2,1)S(1)}, bf16[512,768]{1,0:T(8,128)(2,1)S(1)}, u32[]{:S(2)}, u32[]{:S(2)}) %collective-permute-start.18) | collective-permute-done | bytes 786464 | tf_op jit(solution)/shard_map/ppermute | solution.py:63
  170.3 5.9 %all-to-all-done = bf16[8,4,32,2048]{3,2,1,0:T(8,128)(2,1)} async-done(((bf16[8,4,32,2048]{3,2,1,0:T(8,128)(2,1)}), bf16[8,4,32,2048]{3,2,1,0:T(8,128)(2,1)}, u32[]{:S(2)}, u32[]{:S(2)}) %all-to-all-start) | async-done | bytes 4194336 | tf_op jit(solution)/shard_map/all_to_all | solution.py:485
  180.7 11.4 %collective-permute-done.17.moved_ref = bf16[256,768]{1,0:T(8,128)(2,1)S(1)} collective-permute-done((bf16[256,768]{1,0:T(8,128)(2,1)S(1)}, bf16[256,768]{1,0:T(8,128)(2,1)S(1)}, u32[]{:S(2)}, u32[]{:S(2)}) %collective-permute-start.17) | collective-permute-done | bytes 393248 | tf_op jit(solution)/shard_map/ppermute | solution.py:63
  195.6 21.6 %collective-permute-done.19.moved_ref = bf16[256,768]{1,0:T(8,128)(2,1)S(1)} collective-permute-done((bf16[256,768]{1,0:T(8,128)(2,1)S(1)}, bf16[256,768]{1,0:T(8,128)(2,1)S(1)}, u32[]{:S(2)}, u32[]{:S(2)}) %collective-permute-start.19) | collective-permute-done | bytes 393248 | tf_op jit(solution)/shard_map/ppermute | solution.py:63
  219.6 11.2 %shard_map.94 = (bf16[1024,768]{1,0:T(8,128)(2,1)}, f32[1024,768]{1,0:T(8,128)}, f32[1024,768]{1,0:T(8,128)}) custom-call(bf16[1024,2048]{1,0:T(8,128)(2,1)} %bitcast.1.refs_0_.rows_ref, bf16[512,768]{1,0:T(8,128)(2,1)S(1)} %copy-done.16, bf16[512,768]{1,0:T(8,128)(2,1)S(1)} %copy-done.20, bf16[256,768]{1,0:T(8,128)(2,1)} %shard_map.87.refs_3_.refs_4_, ...), custom_call_target="tpu_custom_call" | custom-call | tf_op jit(solution)/shard_map/pallas_call | solution.py:364
  230.8 28.0 %collective-permute-start.21 = (bf16[256,768]{1,0:T(8,128)(2,1)}, bf16[256,768]{1,0:T(8,128)(2,1)}, u32[]{:S(2)}, u32[]{:S(2)}) collective-permute-start(bf16[256,768]{1,0:T(8,128)(2,1)} %get-tuple-element.115), channel_id=1, source_target_pairs={{0,2},{1,3},{2,0},{3,1},{4,6},{5,7},{6,4},{7,5},{8,10},{9,11},{10,... | collective-permute-start | bytes 1179656 | tf_op jit(solution)/shard_map/ppermute | solution.py:63
  277.5 10.1 %collective-permute-start.25 = (bf16[512,768]{1,0:T(8,128)(2,1)S(1)}, bf16[512,768]{1,0:T(8,128)(2,1)}, u32[]{:S(2)}, u32[]{:S(2)}) collective-permute-start(bf16[512,768]{1,0:T(8,128)(2,1)S(1)} %shard_map.97), channel_id=1, source_target_pairs={{0,1},{1,2},{2,3},{3,0},{4,5},{5,6},{6,7},{7,4},{8,9},{9,10},{10,1... | collective-permute-start | bytes 2359304 | tf_op jit(solution)/shard_map/ppermute | solution.py:63
  288.7 11.2 %shard_map.105 = (bf16[1024,2048]{1,0:T(8,128)(2,1)}, bf16[1024,768]{1,0:T(8,128)(2,1)}, bf16[1024,768]{1,0:T(8,128)(2,1)}) custom-call(bf16[1024,768]{1,0:T(8,128)(2,1)} %get-tuple-element.111.refs_0_, bf16[1024,2048]{1,0:T(8,128)(2,1)} %bitcast.2.rows_ref.refs_1_, f32[1024,768]{1,0:T(8,128)} %get-tuple-element.112.refs_2_, ...), custom_call_target="tpu_custom_call" | custom-call | tf_op jit(solution)/shard_map/pallas_call | solution.py:396
  324.1 9.5 %collective-permute-done.26.moved_ref = bf16[256,768]{1,0:T(8,128)(2,1)} collective-permute-done((bf16[256,768]{1,0:T(8,128)(2,1)S(1)}, bf16[256,768]{1,0:T(8,128)(2,1)}, u32[]{:S(2)}, u32[]{:S(2)}) %collective-permute-start.26) | collective-permute-done | bytes 393248 | tf_op jit(solution)/shard_map/ppermute | solution.py:63
  334.5 7.6 %collective-permute-done.34.moved_ref = bf16[256,768]{1,0:T(8,128)(2,1)S(1)} collective-permute-done((bf16[256,768]{1,0:T(8,128)(2,1)S(1)}, bf16[256,768]{1,0:T(8,128)(2,1)S(1)}, u32[]{:S(2)}, u32[]{:S(2)}) %collective-permute-start.34) | collective-permute-done | bytes 393248 | tf_op jit(solution)/shard_map/ppermute | solution.py:63
  346.1 10.9 %shard_map.113 = bf16[1024,2048]{1,0:T(8,128)(2,1)} custom-call(bf16[1024,768]{1,0:T(8,128)(2,1)} %get-tuple-element.151.refs_0_, bf16[1024,768]{1,0:T(8,128)(2,1)} %get-tuple-element.124.refs_1_, bf16[512,768]{1,0:T(8,128)(2,1)S(1)} %copy-done.17, bf16[512,768]{1,0:T(8,128)(2,1)S(1)} %copy-done.21, bf16[256,768]{1,0:T(8,128)(2,1)} %shard_map.87.refs_3_.refs_4_, ...), custom_call_target="tpu_custom_call" | custom-call | tf_op jit(solution)/shard_map/pallas_call | solution.py:424
  364.3 14.0 %collective-permute-start.35 = (bf16[512,768]{1,0:T(8,128)(2,1)}, bf16[512,768]{1,0:T(8,128)(2,1)}, u32[]{:S(2)}, u32[]{:S(2)}) collective-permute-start(bf16[512,768]{1,0:T(8,128)(2,1)} %get-tuple-element.141), channel_id=1, source_target_pairs={{0,1},{1,2},{2,3},{3,0},{4,5},{5,6},{6,7},{7,4},{8,9},{9,10},{10,1... | collective-permute-start | bytes 2359304 | tf_op jit(solution)/shard_map/ppermute | solution.py:63
  380.4 11.6 %shard_map.111 = (bf16[128,2048]{1,0:T(8,128)(2,1)S(1)}, bf16[128,2048]{1,0:T(8,128)(2,1)S(1)}, bf16[128,2048]{1,0:T(8,128)(2,1)S(1)}, bf16[128,2048]{1,0:T(8,128)(2,1)S(1)}, f32[4,4,128]{2,1,0:T(4,128)S(1)}) custom-call(s32[1]{0:T(128)} %bitcast.level_ref, bf16[128,2176]{1,0:T(8,128)(2,1)} %copy-done.4, bf16[128,2176]{1,0:T(8,128)(2,1)} %copy-done.7, ...), custom_call_target="tpu_custom_call" | custom-call | tf_op jit(solution)/shard_map/pallas_call | solution.py:325
  413.4 6.6 %collective-permute-done.46.moved_ref = bf16[256,768]{1,0:T(8,128)(2,1)} collective-permute-done((bf16[256,768]{1,0:T(8,128)(2,1)}, bf16[256,768]{1,0:T(8,128)(2,1)}, u32[]{:S(2)}, u32[]{:S(2)}) %collective-permute-start.46) | collective-permute-done | bytes 393248 | tf_op jit(solution)/shard_map/ppermute | solution.py:63
  444.9 6.7 %shard_map.126.refs_4_ = bf16[512,4,2304]{2,1,0:T(4,128)(2,1)} custom-call(s32[1]{0:T(128)} %bitcast.level_ref, bf16[512,768]{1,0:T(8,128)(2,1)S(1)} %copy-done.14, bf16[512,768]{1,0:T(8,128)(2,1)S(1)} %copy-done.39, bf16[512,768]{1,0:T(8,128)(2,1)S(1)} %pad_maximum_fusion.2.refs_2_, bf16[512,768]{1,0:T(8,128)(2,1)} %shard_map.107.refs_3_), custom_call_target="tpu_custom_call" | custom-call | tf_op jit(solution)/shard_map/pallas_call | solution.py:177
  461.1 11.6 %collective-permute-done.47.moved_ref = bf16[512,768]{1,0:T(8,128)(2,1)S(1)} collective-permute-done((bf16[512,768]{1,0:T(8,128)(2,1)S(1)}, bf16[512,768]{1,0:T(8,128)(2,1)S(1)}, u32[]{:S(2)}, u32[]{:S(2)}) %collective-permute-start.47) | collective-permute-done | bytes 786464 | tf_op jit(solution)/shard_map/ppermute | solution.py:63
  473.7 7.1 %shard_map.118 = (bf16[128,2048]{1,0:T(8,128)(2,1)S(1)}, bf16[128,2048]{1,0:T(8,128)(2,1)}, bf16[128,2048]{1,0:T(8,128)(2,1)S(1)}, bf16[128,2048]{1,0:T(8,128)(2,1)}) custom-call(s32[1]{0:T(128)} %bitcast.level_ref, bf16[128,2176]{1,0:T(8,128)(2,1)S(1)} %copy-done.5, bf16[128,2176]{1,0:T(8,128)(2,1)S(1)} %copy-done.8, bf16[128,2176]{1,0:T(8,128)(2,1)S(1)} %copy-done.10, ...), custom_call_target="tpu_custom_call" | custom-call | tf_op jit(solution)/shard_map/pallas_call | solution.py:325
  491.7 11.3 %collective-permute-done.48.moved_ref = bf16[256,768]{1,0:T(8,128)(2,1)S(1)} collective-permute-done((bf16[256,768]{1,0:T(8,128)(2,1)S(1)}, bf16[256,768]{1,0:T(8,128)(2,1)S(1)}, u32[]{:S(2)}, u32[]{:S(2)}) %collective-permute-start.48) | collective-permute-done | bytes 393248 | tf_op jit(solution)/shard_map/ppermute | solution.py:63
  514.1 10.8 %collective-permute-done.49.moved_ref = bf16[512,768]{1,0:T(8,128)(2,1)S(1)} collective-permute-done((bf16[512,768]{1,0:T(8,128)(2,1)}, bf16[512,768]{1,0:T(8,128)(2,1)S(1)}, u32[]{:S(2)}, u32[]{:S(2)}) %collective-permute-start.49) | collective-permute-done | bytes 786464 | tf_op jit(solution)/shard_map/ppermute | solution.py:63
  525.8 6.7 %shard_map.127.refs_4_ = bf16[512,4,2304]{2,1,0:T(4,128)(2,1)} custom-call(s32[1]{0:T(128)} %bitcast.level_ref, bf16[512,768]{1,0:T(8,128)(2,1)S(1)} %copy-done.33, bf16[512,768]{1,0:T(8,128)(2,1)} %shard_map.110.refs_1_, bf16[512,768]{1,0:T(8,128)(2,1)S(1)} %pad_maximum_fusion.1.refs_2_, ...), custom_call_target="tpu_custom_call", output_to_operand_aliasing={{}: (5, {})} | custom-call | tf_op jit(solution)/shard_map/pallas_call | solution.py:177
  543.5 8.3 %collective-permute-done.50.moved_ref = bf16[256,768]{1,0:T(8,128)(2,1)} collective-permute-done((bf16[256,768]{1,0:T(8,128)(2,1)}, bf16[256,768]{1,0:T(8,128)(2,1)}, u32[]{:S(2)}, u32[]{:S(2)}) %collective-permute-start.50) | collective-permute-done | bytes 393248 | tf_op jit(solution)/shard_map/ppermute | solution.py:63
  (294 shorter events, 215.7 us)
Async XLA Ops:
  23.2 45.1 %collective-permute-start.12 = (bf16[512,768]{1,0:T(8,128)(2,1)S(1)}, bf16[512,768]{1,0:T(8,128)(2,1)S(1)}, u32[]{:S(2)}, u32[]{:S(2)}) collective-permute-start(bf16[512,768]{1,0:T(8,128)(2,1)S(1)} %get-tuple-element.102), channel_id=1, source_target_pairs={{0,1},{1,2},{2,3},{3,0},{4,5},{5,6},{6,7},{7,4},{8,9},{9,10},{10,1... | collective-permute-start | bytes 2359304 | tf_op jit(solution)/shard_map/ppermute | solution.py:63
  25.6 27.2 %collective-permute-start.6 = (bf16[128,2048]{1,0:T(8,128)(2,1)S(1)}, bf16[128,2048]{1,0:T(8,128)(2,1)}, u32[]{:S(2)}, u32[]{:S(2)}) collective-permute-start(bf16[128,2048]{1,0:T(8,128)(2,1)S(1)} %copy-done.22), channel_id=1, source_target_pairs={{0,1},{1,2},{2,3},{4,5},{5,6},{6,7},{8,9},{9,10},{10,11},{12,13},{... | collective-permute-start | bytes 1572872 | tf_op jit(solution)/shard_map/ppermute | solution.py:112
  30.1 29.6 %collective-permute-start.9 = (bf16[128,2048]{1,0:T(8,128)(2,1)S(1)}, bf16[128,2048]{1,0:T(8,128)(2,1)}, u32[]{:S(2)}, u32[]{:S(2)}) collective-permute-start(bf16[128,2048]{1,0:T(8,128)(2,1)S(1)} %copy-done.22), channel_id=1, source_target_pairs={{1,0},{2,1},{3,2},{5,4},{6,5},{7,6},{9,8},{10,9},{11,10},{13,12},{... | collective-permute-start | bytes 1572872 | tf_op jit(solution)/shard_map/ppermute | solution.py:112
  31.4 29.7 %collective-permute-start.2 = (bf16[128,2176]{1,0:T(8,128)(2,1)S(1)}, bf16[128,2176]{1,0:T(8,128)(2,1)S(1)}, u32[]{:S(2)}, u32[]{:S(2)}) collective-permute-start(bf16[128,2176]{1,0:T(8,128)(2,1)S(1)} %collective-permute-done.refs_1_.refs_8_), channel_id=1, source_target_pairs={{1,2},{2,3},{5,6},{6,7},{9,10},{10,11},{13,14},{14,15},{17,18},{18... | collective-permute-start | bytes 1671176 | tf_op jit(solution)/shard_map/ppermute | solution.py:112
  32.1 35.4 %collective-permute-start.4 = (bf16[128,2176]{1,0:T(8,128)(2,1)S(1)}, bf16[128,2176]{1,0:T(8,128)(2,1)S(1)}, u32[]{:S(2)}, u32[]{:S(2)}) collective-permute-start(bf16[128,2176]{1,0:T(8,128)(2,1)S(1)} %collective-permute-done.1.refs_4_.refs_11_), channel_id=1, source_target_pairs={{1,0},{2,1},{5,4},{6,5},{9,8},{10,9},{13,12},{14,13},{17,16},{18,1... | collective-permute-start | bytes 1671176 | tf_op jit(solution)/shard_map/ppermute | solution.py:112
  52.8 31.7 %collective-permute-start.14 = (bf16[512,768]{1,0:T(8,128)(2,1)}, bf16[512,768]{1,0:T(8,128)(2,1)}, u32[]{:S(2)}, u32[]{:S(2)}) collective-permute-start(bf16[512,768]{1,0:T(8,128)(2,1)} %get-tuple-element.104), channel_id=1, source_target_pairs={{0,3},{1,0},{2,1},{3,2},{4,7},{5,4},{6,5},{7,6},{8,11},{9,8},{10,9... | collective-permute-start | bytes 2359304 | tf_op jit(solution)/shard_map/ppermute | solution.py:63
  59.7 35.1 %collective-permute-start.7 = (bf16[128,2048]{1,0:T(8,128)(2,1)}, bf16[128,2048]{1,0:T(8,128)(2,1)}, u32[]{:S(2)}, u32[]{:S(2)}) collective-permute-start(bf16[128,2048]{1,0:T(8,128)(2,1)} %collective-permute-done.6.refs_8_), channel_id=1, source_target_pairs={{1,2},{2,3},{5,6},{6,7},{9,10},{10,11},{13,14},{14,15},{17,18},{18... | collective-permute-start | bytes 1572872 | tf_op jit(solution)/shard_map/ppermute | solution.py:112
  61.1 50.2 %collective-permute-start.10 = (bf16[128,2048]{1,0:T(8,128)(2,1)}, bf16[128,2048]{1,0:T(8,128)(2,1)}, u32[]{:S(2)}, u32[]{:S(2)}) collective-permute-start(bf16[128,2048]{1,0:T(8,128)(2,1)} %collective-permute-done.9.refs_11_), channel_id=1, source_target_pairs={{1,0},{2,1},{5,4},{6,5},{9,8},{10,9},{13,12},{14,13},{17,16},{18,1... | collective-permute-start | bytes 1572872 | tf_op jit(solution)/shard_map/ppermute | solution.py:112
  67.5 45.2 %collective-permute-start.3 = (bf16[128,2176]{1,0:T(8,128)(2,1)S(1)}, bf16[128,2176]{1,0:T(8,128)(2,1)S(1)}, u32[]{:S(2)}, u32[]{:S(2)}) collective-permute-start(bf16[128,2176]{1,0:T(8,128)(2,1)S(1)} %collective-permute-done.2.refs_2_.refs_9_), channel_id=1, source_target_pairs={{2,3},{6,7},{10,11},{14,15},{18,19},{22,23},{26,27},{30,31}} | collective-permute-start | bytes 1671176 | tf_op jit(solution)/shard_map/ppermute | solution.py:112
  69.2 46.7 %collective-permute-start.5 = (bf16[128,2176]{1,0:T(8,128)(2,1)S(1)}, bf16[128,2176]{1,0:T(8,128)(2,1)}, u32[]{:S(2)}, u32[]{:S(2)}) collective-permute-start(bf16[128,2176]{1,0:T(8,128)(2,1)S(1)} %collective-permute-done.4.refs_5_.refs_12_), channel_id=1, source_target_pairs={{1,0},{5,4},{9,8},{13,12},{17,16},{21,20},{25,24},{29,28}} | collective-permute-start | bytes 1671176 | tf_op jit(solution)/shard_map/ppermute | solution.py:112
  84.5 42.6 %collective-permute-start.13 = (bf16[256,768]{1,0:T(8,128)(2,1)}, bf16[256,768]{1,0:T(8,128)(2,1)}, u32[]{:S(2)}, u32[]{:S(2)}) collective-permute-start(bf16[256,768]{1,0:T(8,128)(2,1)} %get-tuple-element.103), channel_id=1, source_target_pairs={{0,2},{1,3},{2,0},{3,1},{4,6},{5,7},{6,4},{7,5},{8,10},{9,11},{10,... | collective-permute-start | bytes 1179656 | tf_op jit(solution)/shard_map/ppermute | solution.py:63
  94.7 38.9 %collective-permute-start.15 = (bf16[256,768]{1,0:T(8,128)(2,1)}, bf16[256,768]{1,0:T(8,128)(2,1)}, u32[]{:S(2)}, u32[]{:S(2)}) collective-permute-start(bf16[256,768]{1,0:T(8,128)(2,1)} %get-tuple-element.105), channel_id=1, source_target_pairs={{0,2},{1,3},{2,0},{3,1},{4,6},{5,7},{6,4},{7,5},{8,10},{9,11},{10,... | collective-permute-start | bytes 1179656 | tf_op jit(solution)/shard_map/ppermute | solution.py:63
  112.7 42.2 %collective-permute-start.11 = (bf16[128,2048]{1,0:T(8,128)(2,1)}, bf16[128,2048]{1,0:T(8,128)(2,1)}, u32[]{:S(2)}, u32[]{:S(2)}) collective-permute-start(bf16[128,2048]{1,0:T(8,128)(2,1)} %collective-permute-done.10.refs_12_), channel_id=1, source_target_pairs={{1,0},{5,4},{9,8},{13,12},{17,16},{21,20},{25,24},{29,28}} | collective-permute-start | bytes 1572872 | tf_op jit(solution)/shard_map/ppermute | solution.py:112
  122.5 53.7 %all-to-all-start = ((bf16[8,4,32,2048]{3,2,1,0:T(8,128)(2,1)}), bf16[8,4,32,2048]{3,2,1,0:T(8,128)(2,1)}, u32[]{:S(2)}, u32[]{:S(2)}) async-start(bf16[8,4,32,2048]{3,2,1,0:T(8,128)(2,1)} %shard_map.85), calls=%async_computation | async-start | bytes 8388608 | tf_op jit(solution)/shard_map/all_to_all | solution.py:485
  127.1 35.0 %collective-permute-start.16 = (bf16[512,768]{1,0:T(8,128)(2,1)}, bf16[512,768]{1,0:T(8,128)(2,1)S(1)}, u32[]{:S(2)}, u32[]{:S(2)}) collective-permute-start(bf16[512,768]{1,0:T(8,128)(2,1)} %get-tuple-element.106), channel_id=1, source_target_pairs={{0,1},{1,2},{2,3},{3,0},{4,5},{5,6},{6,7},{7,4},{8,9},{9,10},{10,1... | collective-permute-start | bytes 2359304 | tf_op jit(solution)/shard_map/ppermute | solution.py:63
  133.7 35.7 %collective-permute-start.18 = (bf16[512,768]{1,0:T(8,128)(2,1)S(1)}, bf16[512,768]{1,0:T(8,128)(2,1)S(1)}, u32[]{:S(2)}, u32[]{:S(2)}) collective-permute-start(bf16[512,768]{1,0:T(8,128)(2,1)S(1)} %copy-done.72), channel_id=1, source_target_pairs={{0,3},{1,0},{2,1},{3,2},{4,7},{5,4},{6,5},{7,6},{8,11},{9,8},{10,9... | collective-permute-start | bytes 2359304 | tf_op jit(solution)/shard_map/ppermute | solution.py:63
  163.3 28.9 %collective-permute-start.17 = (bf16[256,768]{1,0:T(8,128)(2,1)S(1)}, bf16[256,768]{1,0:T(8,128)(2,1)S(1)}, u32[]{:S(2)}, u32[]{:S(2)}) collective-permute-start(bf16[256,768]{1,0:T(8,128)(2,1)S(1)} %copy-done.68), channel_id=1, source_target_pairs={{0,2},{1,3},{2,0},{3,1},{4,6},{5,7},{6,4},{7,5},{8,10},{9,11},{10,... | collective-permute-start | bytes 1179656 | tf_op jit(solution)/shard_map/ppermute | solution.py:63
  170.3 47.0 %collective-permute-start.19 = (bf16[256,768]{1,0:T(8,128)(2,1)S(1)}, bf16[256,768]{1,0:T(8,128)(2,1)S(1)}, u32[]{:S(2)}, u32[]{:S(2)}) collective-permute-start(bf16[256,768]{1,0:T(8,128)(2,1)S(1)} %copy-done.67), channel_id=1, source_target_pairs={{0,2},{1,3},{2,0},{3,1},{4,6},{5,7},{6,4},{7,5},{8,10},{9,11},{10,... | collective-permute-start | bytes 1179656 | tf_op jit(solution)/shard_map/ppermute | solution.py:63
  176.2 54.6 %all-to-all-start.1 = ((bf16[8,4,32,2048]{3,2,1,0:T(8,128)(2,1)}), bf16[8,4,32,2048]{3,2,1,0:T(8,128)(2,1)}, u32[]{:S(2)}, u32[]{:S(2)}) async-start(bf16[8,4,32,2048]{3,2,1,0:T(8,128)(2,1)} %shard_map.95), calls=%async_computation.1 | async-start | bytes 8388608 | tf_op jit(solution)/shard_map/all_to_all | solution.py:485
  218.0 40.8 %collective-permute-start.22 = (bf16[512,768]{1,0:T(8,128)(2,1)}, bf16[512,768]{1,0:T(8,128)(2,1)S(1)}, u32[]{:S(2)}, u32[]{:S(2)}) collective-permute-start(bf16[512,768]{1,0:T(8,128)(2,1)} %get-tuple-element.116), channel_id=1, source_target_pairs={{0,3},{1,0},{2,1},{3,2},{4,7},{5,4},{6,5},{7,6},{8,11},{9,8},{10,9... | collective-permute-start | bytes 2359304 | tf_op jit(solution)/shard_map/ppermute | solution.py:63
  230.8 43.5 %collective-permute-start.21 = (bf16[256,768]{1,0:T(8,128)(2,1)}, bf16[256,768]{1,0:T(8,128)(2,1)}, u32[]{:S(2)}, u32[]{:S(2)}) collective-permute-start(bf16[256,768]{1,0:T(8,128)(2,1)} %get-tuple-element.115), channel_id=1, source_target_pairs={{0,2},{1,3},{2,0},{3,1},{4,6},{5,7},{6,4},{7,5},{8,10},{9,11},{10,... | collective-permute-start | bytes 1179656 | tf_op jit(solution)/shard_map/ppermute | solution.py:63
  277.5 31.4 %collective-permute-start.25 = (bf16[512,768]{1,0:T(8,128)(2,1)S(1)}, bf16[512,768]{1,0:T(8,128)(2,1)}, u32[]{:S(2)}, u32[]{:S(2)}) collective-permute-start(bf16[512,768]{1,0:T(8,128)(2,1)S(1)} %shard_map.97), channel_id=1, source_target_pairs={{0,1},{1,2},{2,3},{3,0},{4,5},{5,6},{6,7},{7,4},{8,9},{9,10},{10,1... | collective-permute-start | bytes 2359304 | tf_op jit(solution)/shard_map/ppermute | solution.py:63
  301.8 31.9 %collective-permute-start.26 = (bf16[256,768]{1,0:T(8,128)(2,1)S(1)}, bf16[256,768]{1,0:T(8,128)(2,1)}, u32[]{:S(2)}, u32[]{:S(2)}) collective-permute-start(bf16[256,768]{1,0:T(8,128)(2,1)S(1)} %copy-done.58), channel_id=1, source_target_pairs={{0,2},{1,3},{2,0},{3,1},{4,6},{5,7},{6,4},{7,5},{8,10},{9,11},{10,... | collective-permute-start | bytes 1179656 | tf_op jit(solution)/shard_map/ppermute | solution.py:63
  319.6 59.8 %all-to-all-start.2 = ((bf16[8,4,32,2048]{3,2,1,0:T(8,128)(2,1)}), bf16[8,4,32,2048]{3,2,1,0:T(8,128)(2,1)}, u32[]{:S(2)}, u32[]{:S(2)}) async-start(bf16[8,4,32,2048]{3,2,1,0:T(8,128)(2,1)} %bitcast.15), calls=%async_computation.2 | async-start | bytes 8388608 | tf_op jit(solution)/shard_map/all_to_all | solution.py:485
  333.7 45.7 %collective-permute-start.27 = (bf16[512,768]{1,0:T(8,128)(2,1)}, bf16[512,768]{1,0:T(8,128)(2,1)}, u32[]{:S(2)}, u32[]{:S(2)}) collective-permute-start(bf16[512,768]{1,0:T(8,128)(2,1)} %get-tuple-element.127), channel_id=1, source_target_pairs={{0,3},{1,0},{2,1},{3,2},{4,7},{5,4},{6,5},{7,6},{8,11},{9,8},{10,9... | collective-permute-start | bytes 2359304 | tf_op jit(solution)/shard_map/ppermute | solution.py:63
  364.3 38.1 %collective-permute-start.35 = (bf16[512,768]{1,0:T(8,128)(2,1)}, bf16[512,768]{1,0:T(8,128)(2,1)}, u32[]{:S(2)}, u32[]{:S(2)}) collective-permute-start(bf16[512,768]{1,0:T(8,128)(2,1)} %get-tuple-element.141), channel_id=1, source_target_pairs={{0,1},{1,2},{2,3},{3,0},{4,5},{5,6},{6,7},{7,4},{8,9},{9,10},{10,1... | collective-permute-start | bytes 2359304 | tf_op jit(solution)/shard_map/ppermute | solution.py:63
  402.4 71.3 %all-to-all-start.3 = ((bf16[8,4,32,2048]{3,2,1,0:T(8,128)(2,1)}), bf16[8,4,32,2048]{3,2,1,0:T(8,128)(2,1)}, u32[]{:S(2)}, u32[]{:S(2)}) async-start(bf16[8,4,32,2048]{3,2,1,0:T(8,128)(2,1)} %bitcast.14), calls=%async_computation.3 | async-start | bytes 8388608 | tf_op jit(solution)/shard_map/all_to_all | solution.py:485
  425.9 28.8 %collective-permute-start.29 = (bf16[128,2048]{1,0:T(8,128)(2,1)}, bf16[128,2048]{1,0:T(8,128)(2,1)}, u32[]{:S(2)}, u32[]{:S(2)}) collective-permute-start(bf16[128,2048]{1,0:T(8,128)(2,1)} %get-tuple-element.176), channel_id=1, source_target_pairs={{0,1},{1,2},{4,5},{5,6},{8,9},{9,10},{12,13},{13,14},{16,17},{17,1... | collective-permute-start | bytes 1572872 | tf_op jit(solution)/shard_map/ppermute | solution.py:112
  491.6 33.3 %collective-permute-start.49 = (bf16[512,768]{1,0:T(8,128)(2,1)}, bf16[512,768]{1,0:T(8,128)(2,1)S(1)}, u32[]{:S(2)}, u32[]{:S(2)}) collective-permute-start(bf16[512,768]{1,0:T(8,128)(2,1)} %get-tuple-element.157), channel_id=1, source_target_pairs={{0,1},{1,2},{2,3},{3,0},{4,5},{5,6},{6,7},{7,4},{8,9},{9,10},{10,1... | collective-permute-start | bytes 2359304 | tf_op jit(solution)/shard_map/ppermute | solution.py:63
  507.4 26.8 %collective-permute-start.38 = (bf16[128,2048]{1,0:T(8,128)(2,1)}, bf16[128,2048]{1,0:T(8,128)(2,1)}, u32[]{:S(2)}, u32[]{:S(2)}) collective-permute-start(bf16[128,2048]{1,0:T(8,128)(2,1)} %get-tuple-element.174), channel_id=1, source_target_pairs={{0,1},{1,2},{4,5},{5,6},{8,9},{9,10},{12,13},{13,14},{16,17},{17,1... | collective-permute-start | bytes 1572872 | tf_op jit(solution)/shard_map/ppermute | solution.py:112
  512.5 28.2 %collective-permute-start.41 = (bf16[128,2048]{1,0:T(8,128)(2,1)}, bf16[128,2048]{1,0:T(8,128)(2,1)}, u32[]{:S(2)}, u32[]{:S(2)}) collective-permute-start(bf16[128,2048]{1,0:T(8,128)(2,1)} %get-tuple-element.175), channel_id=1, source_target_pairs={{2,1},{3,2},{6,5},{7,6},{10,9},{11,10},{14,13},{15,14},{18,17},{19... | collective-permute-start | bytes 1572872 | tf_op jit(solution)/shard_map/ppermute | solution.py:112
  525.8 26.1 %collective-permute-start.50 = (bf16[256,768]{1,0:T(8,128)(2,1)}, bf16[256,768]{1,0:T(8,128)(2,1)}, u32[]{:S(2)}, u32[]{:S(2)}) collective-permute-start(bf16[256,768]{1,0:T(8,128)(2,1)} %get-tuple-element.158), channel_id=1, source_target_pairs={{0,2},{1,3},{2,0},{3,1},{4,6},{5,7},{6,4},{7,5},{8,10},{9,11},{10,... | collective-permute-start | bytes 1179656 | tf_op jit(solution)/shard_map/ppermute | solution.py:63
  (96 other events, 1365.6 us)

commit v3 on v2

--- a/solution.py
+++ b/solution.py
@@ -34,7 +34,7 @@
  'grad_parts': [19],
  'join0': [19],
  'join1': [21],
- 'middle_in_grad': ['row_grad'],
+ 'middle_in_grad': [16],
  'other_in_grads': [13],
  'out_sums': [16],
  'own_in_grad': [18],
@@ -222,17 +222,26 @@
 def dispatch_kernel(n, chosen, gated, level_ref, *refs):
     count = 2 * n - 1
     metas, blocks, out_ref = refs[:count], refs[count : 2 * count], refs[2 * count]
+    matrix_ref, weight_ref = refs[2 * count + 1 :]
     groups, _, capacity, width = out_ref.shape
+
+    @pl.when(pl.program_id(0) == 0)
+    def _():
+        for d in range(n):
+            meta = arrived(metas, n, d)
+            tokens = meta.shape[0]
+            named, gates, taken = slots_of(level_ref[0], n, groups, chosen, capacity, meta)
+            matrix = jnp.where(taken, 1.0, 0.0).astype(BF16)
+            matrix_ref[d] = matrix.reshape(groups * capacity, tokens)
+            if gated:
+                weight = jnp.where(taken, gates_of(named, gates)[:, None, :], 0.0)
+                weight = jnp.sum(weight, axis=2, keepdims=True)
+                weight_ref[d] = weight.reshape(groups * capacity, 1)
+
     for d in range(n):
-        meta, x = arrived(metas, n, d), arrived(blocks, n, d)
-        named, gates, taken = slots_of(level_ref[0], n, groups, chosen, capacity, meta)
-        tokens = x.shape[0]
-        matrix = jnp.where(taken, 1.0, 0.0).astype(BF16).reshape(groups * capacity, tokens)
-        rows = dot(matrix, x, ((1,), (0,)))
+        rows = dot(matrix_ref[d], arrived(blocks, n, d), ((1,), (0,)))
         if gated:
-            weight = jnp.where(taken, gates_of(named, gates)[:, None, :], 0.0)
-            weight = jnp.sum(weight, axis=2, keepdims=True)
-            rows = rows * weight.reshape(groups * capacity, 1)
+            rows = rows * weight_ref[d]
         out_ref[:, d] = rows.astype(BF16).reshape(groups, capacity, width)
 
 
@@ -257,6 +266,10 @@
             in_specs=[meta_spec(tokens, model)] * len(metas)
             + [rolled(n, tokens, width)] * len(blocks),
             out_specs=pl.BlockSpec((groups, n, capacity, width), lambda k, level: (0, 0, 0, k)),
+            scratch_shapes=[
+                pltpu.VMEM((n, groups * capacity, tokens), BF16),
+                pltpu.VMEM((n, groups * capacity, 1), F32),
+            ],
         ),
         compiler_params=params(),
     )(level, *metas, *blocks)
@@ -265,45 +278,63 @@
 def combine_out_kernel(n, chosen, level_ref, *refs):
     count = 2 * n - 1
     metas, grads, back_ref = refs[:count], refs[count : 2 * count], refs[2 * count]
-    out_refs, dots_ref = refs[2 * count + 1 : -1], refs[-1]
+    out_refs, dots_ref = refs[2 * count + 1 : 2 * count + 1 + n], refs[2 * count + 1 + n]
+    matrix_ref, high_ref, low_ref, pairs_ref = refs[2 * count + 2 + n :]
     groups, _, capacity, width = back_ref.shape
+    tokens = metas[0].shape[0]
+    step = pl.program_id(0)
+
+    def slots(d):
+        return slots_of(level_ref[0], n, groups, chosen, capacity, arrived(metas, n, d))
+
+    @pl.when(step == 0)
+    def _():
+        for d in range(n):
+            named, gates, taken = slots(d)
+            weight = jnp.where(taken, gates_of(named, gates)[:, None, :], 0.0)
+            weight = weight.reshape(groups * capacity, tokens)
+            high = weight.astype(BF16)
+            high_ref[d] = high
+            low_ref[d] = (weight - high.astype(F32)).astype(BF16)
+            matrix = jnp.where(taken, 1.0, 0.0)
+            matrix_ref[d] = matrix.reshape(groups * capacity, tokens)
+        pairs_ref[...] = jnp.zeros_like(pairs_ref)
+
     for d in range(n):
-        meta, grad = arrived(metas, n, d), arrived(grads, n, d)
-        named, gates, taken = slots_of(level_ref[0], n, groups, chosen, capacity, meta)
-        tokens = grad.shape[0]
-        weight = jnp.where(taken, gates_of(named, gates)[:, None, :], 0.0)
-        weight = weight.reshape(groups * capacity, tokens)
-        high = weight.astype(BF16)
-        low = (weight - high.astype(F32)).astype(BF16)
         rows = back_ref[:, d].reshape(groups * capacity, width)
-        total = dot(high, rows, ((0,), (0,))) + dot(low, rows, ((0,), (0,)))
+        total = dot(high_ref[d], rows, ((0,), (0,))) + dot(low_ref[d], rows, ((0,), (0,)))
         out_refs[d][...] = total.astype(BF16)
-        pairs = dot(rows, grad, ((1,), (1,))).reshape(groups, capacity, tokens)
-        pairs = jnp.sum(jnp.where(taken, pairs, 0.0), axis=1)
-        part = jnp.concatenate(
-            [jnp.sum(jnp.where(name, pairs, 0.0), axis=0, keepdims=True) for name in named]
-        )
-
-        @pl.when(pl.program_id(0) == 0)
-        def _():
-            dots_ref[d] = part
-
-        @pl.when(pl.program_id(0) > 0)
-        def _():
-            dots_ref[d] += part
+        pairs_ref[d] += dot(rows, arrived(grads, n, d), ((1,), (1,)))
+
+    @pl.when(step == n - 1)
+    def _():
+        for d in range(n):
+            named, _, _ = slots(d)
+            pairs = pairs_ref[d] * matrix_ref[d]
+            pairs = jnp.sum(pairs.reshape(groups, capacity, tokens), axis=1)
+            dots_ref[d] = jnp.concatenate(
+                [jnp.sum(jnp.where(name, pairs, 0.0), axis=0, keepdims=True) for name in named]
+            )
 
 
 def combine_grad_kernel(n, chosen, level_ref, *refs):
     count = 2 * n - 1
-    metas, back_ref, out_refs = refs[:count], refs[count], refs[count + 1 :]
+    metas, back_ref, out_refs = refs[:count], refs[count], refs[count + 1 : count + 1 + n]
+    matrix_ref = refs[count + 1 + n]
     groups, _, capacity, width = back_ref.shape
+    tokens = metas[0].shape[0]
+
+    @pl.when(pl.program_id(0) == 0)
+    def _():
+        for d in range(n):
+            meta = arrived(metas, n, d)
+            _, _, taken = slots_of(level_ref[0], n, groups, chosen, capacity, meta)
+            matrix = jnp.where(taken, 1.0, 0.0).astype(BF16)
+            matrix_ref[d] = matrix.reshape(groups * capacity, tokens)
+
     for d in range(n):
-        meta = arrived(metas, n, d)
-        _, _, taken = slots_of(level_ref[0], n, groups, chosen, capacity, meta)
-        matrix = jnp.where(taken, 1.0, 0.0).astype(BF16)
-        matrix = matrix.reshape(groups * capacity, meta.shape[0])
         rows = back_ref[:, d].reshape(groups * capacity, width)
-        out_refs[d][...] = dot(matrix, rows, ((0,), (0,))).astype(BF16)
+        out_refs[d][...] = dot(matrix_ref[d], rows, ((0,), (0,))).astype(BF16)
 
 
 def combine(level, metas, back, chosen, grads=None):
@@ -317,11 +348,14 @@
     in_specs = [meta_spec(tokens, model)] * len(metas)
     if grads is None:
         kernel, extra = combine_grad_kernel, []
+        scratch = [pltpu.VMEM((n, groups * capacity, tokens), BF16)]
     else:
         kernel, extra = combine_out_kernel, grads
         in_specs = in_specs + [x_spec] * len(grads)
         out_shape = out_shape + [jax.ShapeDtypeStruct((n, chosen, tokens), F32)]
         out_specs = out_specs + [whole((n, chosen, tokens))]
+        shape = (n, groups * capacity, tokens)
+        scratch = [pltpu.VMEM(shape, x) for x in (F32, BF16, BF16, F32)]
     return pl.pallas_call(
         functools.partial(kernel, n, chosen),
         out_shape=out_shape,
@@ -330,6 +364,7 @@
             grid=(n,),
             in_specs=in_specs + [back_spec],
             out_specs=out_specs,
+            scratch_shapes=scratch,
         ),
         compiler_params=params(),
     )(level, *metas, *extra, back)

time: 568 us -> 560 us (0.986)
  Pallas kernels: 127 us -> 120 us
    ppermute x27, waiting for transfers between devices: 131 us -> 120 us  [shift(): return lax.ppermute(x, 'narrow', [(i, (i + k) % n) for i in range(n)])]
    ppermute x24, waiting for transfers between devices: 60.2 us -> 69.9 us  [hop(): return lax.ppermute(x, 'narrow', [(i, i + step) for i in sources])]
    pallas_call x2, Pallas kernels: 18.7 us -> 11.7 us  [combine(): pl.pallas_call(functools.partial(kernel, n, chosen), out_shape=out_shape,...]
    unnamed x147 -> x135, local copies, waits for them, and re-layouts: 26.5 us -> 24.2 us
  transfers between devices with their start and end apart: 55 -> 55, of which waited for: 27 -> 29; matrix products, arithmetic and copies ran while one was open for 3% -> 4% of each run, Pallas kernels for 22% -> 22%
where the time goes in v3:
time: 560 us; the launch traced here: 557 us
  waiting for transfers between devices  200 us (36%)
  starting transfers between devices  184 us (33%)
  Pallas kernels  120 us (21%)
  local copies, waits for them, and re-layouts  30.3 us (5%)
  other arithmetic  21.7 us (4%)
    ppermute x27, waiting for transfers between devices, shift(): return lax.ppermute(x, 'narrow', [(i, (i + k) % n) for i in range(n)])  120 us
    ppermute x27, starting transfers between devices, shift(): return lax.ppermute(x, 'narrow', [(i, (i + k) % n) for i in range(n)])  112 us
    ppermute x24, waiting for transfers between devices, hop(): return lax.ppermute(x, 'narrow', [(i, i + step) for i in sources])  69.9 us
    ppermute x24, starting transfers between devices, hop(): return lax.ppermute(x, 'narrow', [(i, i + step) for i in sources])  53.9 us
    pallas_call x10, Pallas kernels, weight_grad(): pl.pallas_call(weight_grad_kernel, out_shape=[jax.ShapeDtypeStruct((width...  34.1 us
    unnamed x135, local copies, waits for them, and re-layouts  24.2 us
    pallas_call x3, Pallas kernels, join_shard(): pl.pallas_call(functools.partial(join_kernel, n), out_shape=jax.ShapeDtyp...  20 us
    all_to_all x4, starting transfers between devices, swap(): return lax.all_to_all(x, 'wide', split_axis=0, concat_axis=0, tiled=True)  18.4 us
  transfers between devices with their start and end apart: 55, of which 29 were waited for; matrix products, arithmetic and copies ran while one was open for 4% of the time, Pallas kernels for 22%

profile of v3, /device:TPU:0, one launch (start us, length us, event | category | flops | bytes accessed | tf_op | source)
XLA Modules:
  0.0 557.1 jit_solution(16565943995000488288)
XLA Ops:
  5.7 5.6 %collective-permute-start = (bf16[128,2176]{1,0:T(8,128)(2,1)S(1)}, bf16[128,2176]{1,0:T(8,128)(2,1)S(1)}, u32[]{:S(2)}, u32[]{:S(2)}) collective-permute-start(bf16[128,2176]{1,0:T(8,128)(2,1)S(1)} %concatenate.12.refs_0_.refs_7_), channel_id=1, source_target_pairs={{0,1},{1,2},{2,3},{4,5},{5,6},{6,7},{8,9},{9,10},{10,11},{12,13},{... | collective-permute-start | bytes 1671176 | tf_op jit(solution)/shard_map/ppermute | solution.py:112
  11.3 9.7 %shard_map.84 = (bf16[512,768]{1,0:T(8,128)(2,1)S(1)}, bf16[512,768]{1,0:T(8,128)(2,1)S(1)}, bf16[512,768]{1,0:T(8,128)(2,1)S(1)}, bf16[512,768]{1,0:T(8,128)(2,...) custom-call(s32[1]{0:T(128)} %bitcast.level_ref, ...), custom_call_target="tpu_custom_call" | custom-call | tf_op jit(solution)/shard_map/pallas_call | solution.py:150
  37.3 15.5 %collective-permute-done.6.refs_8_ = bf16[128,2048]{1,0:T(8,128)(2,1)} collective-permute-done((bf16[128,2048]{1,0:T(8,128)(2,1)S(1)}, bf16[128,2048]{1,0:T(8,128)(2,1)}, u32[]{:S(2)}, u32[]{:S(2)}) %collective-permute-start.6) | collective-permute-done | bytes 524320 | tf_op jit(solution)/shard_map/ppermute | solution.py:112
  52.8 6.9 %collective-permute-start.14 = (bf16[512,768]{1,0:T(8,128)(2,1)}, bf16[512,768]{1,0:T(8,128)(2,1)}, u32[]{:S(2)}, u32[]{:S(2)}) collective-permute-start(bf16[512,768]{1,0:T(8,128)(2,1)} %get-tuple-element.104), channel_id=1, source_target_pairs={{0,3},{1,0},{2,1},{3,2},{4,7},{5,4},{6,5},{7,6},{8,11},{9,8},{10,9... | collective-permute-start | bytes 2359304 | tf_op jit(solution)/shard_map/ppermute | solution.py:63
  70.4 14.0 %collective-permute-done.14.moved_ref = bf16[512,768]{1,0:T(8,128)(2,1)} collective-permute-done((bf16[512,768]{1,0:T(8,128)(2,1)}, bf16[512,768]{1,0:T(8,128)(2,1)}, u32[]{:S(2)}, u32[]{:S(2)}) %collective-permute-start.14) | collective-permute-done | bytes 786464 | tf_op jit(solution)/shard_map/ppermute | solution.py:63
  84.5 10.3 %collective-permute-start.13 = (bf16[256,768]{1,0:T(8,128)(2,1)}, bf16[256,768]{1,0:T(8,128)(2,1)}, u32[]{:S(2)}, u32[]{:S(2)}) collective-permute-start(bf16[256,768]{1,0:T(8,128)(2,1)} %get-tuple-element.103), channel_id=1, source_target_pairs={{0,2},{1,3},{2,0},{3,1},{4,6},{5,7},{6,4},{7,5},{8,10},{9,11},{10,... | collective-permute-start | bytes 1179656 | tf_op jit(solution)/shard_map/ppermute | solution.py:63
  94.8 16.5 %collective-permute-start.15 = (bf16[256,768]{1,0:T(8,128)(2,1)}, bf16[256,768]{1,0:T(8,128)(2,1)}, u32[]{:S(2)}, u32[]{:S(2)}) collective-permute-start(bf16[256,768]{1,0:T(8,128)(2,1)} %get-tuple-element.105), channel_id=1, source_target_pairs={{0,2},{1,3},{2,0},{3,1},{4,6},{5,7},{6,4},{7,5},{8,10},{9,11},{10,... | collective-permute-start | bytes 1179656 | tf_op jit(solution)/shard_map/ppermute | solution.py:63
  125.9 6.4 %collective-permute-start.16 = (bf16[512,768]{1,0:T(8,128)(2,1)}, bf16[512,768]{1,0:T(8,128)(2,1)S(1)}, u32[]{:S(2)}, u32[]{:S(2)}) collective-permute-start(bf16[512,768]{1,0:T(8,128)(2,1)} %get-tuple-element.106), channel_id=1, source_target_pairs={{0,1},{1,2},{2,3},{3,0},{4,5},{5,6},{6,7},{7,4},{8,9},{9,10},{10,1... | collective-permute-start | bytes 2359304 | tf_op jit(solution)/shard_map/ppermute | solution.py:63
  132.3 24.1 %collective-permute-done.11.refs_13_ = bf16[128,2048]{1,0:T(8,128)(2,1)} collective-permute-done((bf16[128,2048]{1,0:T(8,128)(2,1)}, bf16[128,2048]{1,0:T(8,128)(2,1)}, u32[]{:S(2)}, u32[]{:S(2)}) %collective-permute-start.11) | collective-permute-done | bytes 524320 | tf_op jit(solution)/shard_map/ppermute | solution.py:112
  156.4 6.1 %shard_map.95 = bf16[8,4,32,2048]{3,2,1,0:T(8,128)(2,1)} custom-call(s32[1]{0:T(128)} %bitcast.level_ref, bf16[128,2176]{1,0:T(8,128)(2,1)} %copy-done.4, bf16[128,2176]{1,0:T(8,128)(2,1)} %copy-done.7, bf16[128,2176]{1,0:T(8,128)(2,1)} %copy-done.9, bf16[128,2176]{1,0:T(8,128)(2,1)} %copy-done.12, bf16[128,2176]{1,0:T(8,128)(2,1)} %copy-done.6, ...), custom_call_target="tpu_custom_call" | custom-call | tf_op jit(solution)/shard_map/pallas_call | solution.py:260
  163.7 5.7 %collective-permute-done.18.moved_ref = bf16[512,768]{1,0:T(8,128)(2,1)S(1)} collective-permute-done((bf16[512,768]{1,0:T(8,128)(2,1)}, bf16[512,768]{1,0:T(8,128)(2,1)S(1)}, u32[]{:S(2)}, u32[]{:S(2)}) %collective-permute-start.18) | collective-permute-done | bytes 786464 | tf_op jit(solution)/shard_map/ppermute | solution.py:63
  179.3 11.4 %collective-permute-done.17.moved_ref = bf16[256,768]{1,0:T(8,128)(2,1)S(1)} collective-permute-done((bf16[256,768]{1,0:T(8,128)(2,1)S(1)}, bf16[256,768]{1,0:T(8,128)(2,1)S(1)}, u32[]{:S(2)}, u32[]{:S(2)}) %collective-permute-start.17) | collective-permute-done | bytes 393248 | tf_op jit(solution)/shard_map/ppermute | solution.py:63
  194.2 21.6 %collective-permute-done.19.moved_ref = bf16[256,768]{1,0:T(8,128)(2,1)S(1)} collective-permute-done((bf16[256,768]{1,0:T(8,128)(2,1)S(1)}, bf16[256,768]{1,0:T(8,128)(2,1)S(1)}, u32[]{:S(2)}, u32[]{:S(2)}) %collective-permute-start.19) | collective-permute-done | bytes 393248 | tf_op jit(solution)/shard_map/ppermute | solution.py:63
  218.4 11.2 %shard_map.94 = (bf16[1024,768]{1,0:T(8,128)(2,1)}, f32[1024,768]{1,0:T(8,128)}, f32[1024,768]{1,0:T(8,128)}) custom-call(bf16[1024,2048]{1,0:T(8,128)(2,1)} %bitcast.1.refs_0_.rows_ref, bf16[512,768]{1,0:T(8,128)(2,1)S(1)} %copy-done.17, bf16[512,768]{1,0:T(8,128)(2,1)S(1)} %copy-done.20, bf16[256,768]{1,0:T(8,128)(2,1)} %shard_map.87.refs_3_.refs_4_, ...), custom_call_target="tpu_custom_call" | custom-call | tf_op jit(solution)/shard_map/pallas_call | solution.py:399
  229.6 28.5 %collective-permute-start.21 = (bf16[256,768]{1,0:T(8,128)(2,1)}, bf16[256,768]{1,0:T(8,128)(2,1)}, u32[]{:S(2)}, u32[]{:S(2)}) collective-permute-start(bf16[256,768]{1,0:T(8,128)(2,1)} %get-tuple-element.115), channel_id=1, source_target_pairs={{0,2},{1,3},{2,0},{3,1},{4,6},{5,7},{6,4},{7,5},{8,10},{9,11},{10,... | collective-permute-start | bytes 1179656 | tf_op jit(solution)/shard_map/ppermute | solution.py:63
  280.0 11.3 %shard_map.105 = (bf16[1024,2048]{1,0:T(8,128)(2,1)}, bf16[1024,768]{1,0:T(8,128)(2,1)}, bf16[1024,768]{1,0:T(8,128)(2,1)}) custom-call(bf16[1024,768]{1,0:T(8,128)(2,1)} %get-tuple-element.111.refs_0_, bf16[1024,2048]{1,0:T(8,128)(2,1)} %bitcast.2.rows_ref.refs_1_, f32[1024,768]{1,0:T(8,128)} %get-tuple-element.112.refs_2_, ...), custom_call_target="tpu_custom_call" | custom-call | tf_op jit(solution)/shard_map/pallas_call | solution.py:431
  299.2 11.7 %collective-permute-done.25.moved_ref = bf16[512,768]{1,0:T(8,128)(2,1)} collective-permute-done((bf16[512,768]{1,0:T(8,128)(2,1)}, bf16[512,768]{1,0:T(8,128)(2,1)}, u32[]{:S(2)}, u32[]{:S(2)}) %collective-permute-start.25) | collective-permute-done | bytes 786464 | tf_op jit(solution)/shard_map/ppermute | solution.py:63
  332.0 8.4 %collective-permute-done.34.moved_ref = bf16[256,768]{1,0:T(8,128)(2,1)S(1)} collective-permute-done((bf16[256,768]{1,0:T(8,128)(2,1)}, bf16[256,768]{1,0:T(8,128)(2,1)S(1)}, u32[]{:S(2)}, u32[]{:S(2)}) %collective-permute-start.34) | collective-permute-done | bytes 393248 | tf_op jit(solution)/shard_map/ppermute | solution.py:63
  341.1 10.7 %shard_map.113 = bf16[1024,2048]{1,0:T(8,128)(2,1)} custom-call(bf16[1024,768]{1,0:T(8,128)(2,1)} %get-tuple-element.151.refs_0_, bf16[1024,768]{1,0:T(8,128)(2,1)} %get-tuple-element.124.refs_1_, bf16[512,768]{1,0:T(8,128)(2,1)S(1)} %copy-done.17, bf16[512,768]{1,0:T(8,128)(2,1)S(1)} %copy-done.20, bf16[256,768]{1,0:T(8,128)(2,1)} %shard_map.87.refs_3_.refs_4_, ...), custom_call_target="tpu_custom_call" | custom-call | tf_op jit(solution)/shard_map/pallas_call | solution.py:459
  351.9 13.6 %collective-permute-start.35 = (bf16[512,768]{1,0:T(8,128)(2,1)}, bf16[512,768]{1,0:T(8,128)(2,1)}, u32[]{:S(2)}, u32[]{:S(2)}) collective-permute-start(bf16[512,768]{1,0:T(8,128)(2,1)} %get-tuple-element.141), channel_id=1, source_target_pairs={{0,1},{1,2},{2,3},{3,0},{4,5},{5,6},{6,7},{7,4},{8,9},{9,10},{10,1... | collective-permute-start | bytes 2359304 | tf_op jit(solution)/shard_map/ppermute | solution.py:63
  378.8 6.5 %shard_map.111 = (bf16[128,2048]{1,0:T(8,128)(2,1)S(1)}, bf16[128,2048]{1,0:T(8,128)(2,1)S(1)}, bf16[128,2048]{1,0:T(8,128)(2,1)S(1)}, bf16[128,2048]{1,0:T(8,128)(2,1)S(1)}, f32[4,4,128]{2,1,0:T(4,128)S(1)}) custom-call(s32[1]{0:T(128)} %bitcast.level_ref, bf16[128,2176]{1,0:T(8,128)(2,1)} %copy-done.4, bf16[128,2176]{1,0:T(8,128)(2,1)} %copy-done.7, ...), custom_call_target="tpu_custom_call" | custom-call | tf_op jit(solution)/shard_map/pallas_call | solution.py:359
  408.9 9.5 %collective-permute-done.28 = bf16[128,2048]{1,0:T(8,128)(2,1)} collective-permute-done((bf16[128,2048]{1,0:T(8,128)(2,1)S(1)}, bf16[128,2048]{1,0:T(8,128)(2,1)}, u32[]{:S(2)}, u32[]{:S(2)}) %collective-permute-start.28) | collective-permute-done | bytes 524320 | tf_op jit(solution)/shard_map/ppermute | solution.py:112
  420.9 5.3 collective-permute-start.29
  434.2 6.6 %shard_map.126.refs_4_ = bf16[512,4,2304]{2,1,0:T(4,128)(2,1)} custom-call(s32[1]{0:T(128)} %bitcast.level_ref, bf16[512,768]{1,0:T(8,128)(2,1)S(1)} %copy-done.14, bf16[512,768]{1,0:T(8,128)(2,1)S(1)} %copy-done.36, bf16[512,768]{1,0:T(8,128)(2,1)S(1)} %copy-done.15, bf16[512,768]{1,0:T(8,128)(2,1)} %shard_map.107.refs_3_), custom_call_target="tpu_custom_call" | custom-call | tf_op jit(solution)/shard_map/pallas_call | solution.py:177
  440.9 6.1 %collective-permute-start.47 = (bf16[512,768]{1,0:T(8,128)(2,1)S(1)}, bf16[512,768]{1,0:T(8,128)(2,1)}, u32[]{:S(2)}, u32[]{:S(2)}) collective-permute-start(bf16[512,768]{1,0:T(8,128)(2,1)S(1)} %copy-done.56), channel_id=1, source_target_pairs={{0,3},{1,0},{2,1},{3,2},{4,7},{5,4},{6,5},{7,6},{8,11},{9,8},{10,9... | collective-permute-start | bytes 2359304 | tf_op jit(solution)/shard_map/ppermute | solution.py:63
  453.4 11.6 %collective-permute-done.47.moved_ref = bf16[512,768]{1,0:T(8,128)(2,1)} collective-permute-done((bf16[512,768]{1,0:T(8,128)(2,1)S(1)}, bf16[512,768]{1,0:T(8,128)(2,1)}, u32[]{:S(2)}, u32[]{:S(2)}) %collective-permute-start.47) | collective-permute-done | bytes 786464 | tf_op jit(solution)/shard_map/ppermute | solution.py:63
  485.3 9.9 %collective-permute-done.48.moved_ref = bf16[256,768]{1,0:T(8,128)(2,1)} collective-permute-done((bf16[256,768]{1,0:T(8,128)(2,1)S(1)}, bf16[256,768]{1,0:T(8,128)(2,1)}, u32[]{:S(2)}, u32[]{:S(2)}) %collective-permute-start.48) | collective-permute-done | bytes 393248 | tf_op jit(solution)/shard_map/ppermute | solution.py:63
  500.7 5.2 collective-permute-start.38
  507.5 9.5 %collective-permute-done.49.moved_ref = bf16[512,768]{1,0:T(8,128)(2,1)S(1)} collective-permute-done((bf16[512,768]{1,0:T(8,128)(2,1)}, bf16[512,768]{1,0:T(8,128)(2,1)S(1)}, u32[]{:S(2)}, u32[]{:S(2)}) %collective-permute-start.49) | collective-permute-done | bytes 786464 | tf_op jit(solution)/shard_map/ppermute | solution.py:63
  518.0 6.7 %shard_map.127.refs_4_ = bf16[512,4,2304]{2,1,0:T(4,128)(2,1)} custom-call(s32[1]{0:T(128)} %bitcast.level_ref, bf16[512,768]{1,0:T(8,128)(2,1)S(1)} %copy-done.30, bf16[512,768]{1,0:T(8,128)(2,1)} %shard_map.110.refs_1_, bf16[512,768]{1,0:T(8,128)(2,1)S(1)} %pad_maximum_fusion.1.refs_2_, ...), custom_call_target="tpu_custom_call", output_to_operand_aliasing={{}: (5, {})} | custom-call | tf_op jit(solution)/shard_map/pallas_call | solution.py:177
  534.9 9.1 %collective-permute-done.50.moved_ref = bf16[256,768]{1,0:T(8,128)(2,1)} collective-permute-done((bf16[256,768]{1,0:T(8,128)(2,1)}, bf16[256,768]{1,0:T(8,128)(2,1)}, u32[]{:S(2)}, u32[]{:S(2)}) %collective-permute-start.50) | collective-permute-done | bytes 393248 | tf_op jit(solution)/shard_map/ppermute | solution.py:63
  545.2 6.6 %shard_map.128 = bf16[512,4,2304]{2,1,0:T(4,128)(2,1)} custom-call(s32[1]{0:T(128)} %bitcast.level_ref, bf16[512,768]{1,0:T(8,128)(2,1)S(1)} %get-tuple-element.152.refs_0_, bf16[512,768]{1,0:T(8,128)(2,1)} %shard_map.122.refs_1_, bf16[512,768]{1,0:T(8,128)(2,1)S(1)} %pad_maximum_fusion.refs_2_, ...), custom_call_target="tpu_custom_call", output_to_operand_aliasing={{}: (5, {})} | custom-call | tf_op jit(solution)/shard_map/pallas_call | solution.py:177
  (282 shorter events, 214.0 us)
Async XLA Ops:
  23.2 45.1 %collective-permute-start.12 = (bf16[512,768]{1,0:T(8,128)(2,1)S(1)}, bf16[512,768]{1,0:T(8,128)(2,1)S(1)}, u32[]{:S(2)}, u32[]{:S(2)}) collective-permute-start(bf16[512,768]{1,0:T(8,128)(2,1)S(1)} %get-tuple-element.102), channel_id=1, source_target_pairs={{0,1},{1,2},{2,3},{3,0},{4,5},{5,6},{6,7},{7,4},{8,9},{9,10},{10,1... | collective-permute-start | bytes 2359304 | tf_op jit(solution)/shard_map/ppermute | solution.py:63
  25.6 27.2 %collective-permute-start.6 = (bf16[128,2048]{1,0:T(8,128)(2,1)S(1)}, bf16[128,2048]{1,0:T(8,128)(2,1)}, u32[]{:S(2)}, u32[]{:S(2)}) collective-permute-start(bf16[128,2048]{1,0:T(8,128)(2,1)S(1)} %copy-done.21), channel_id=1, source_target_pairs={{0,1},{1,2},{2,3},{4,5},{5,6},{6,7},{8,9},{9,10},{10,11},{12,13},{... | collective-permute-start | bytes 1572872 | tf_op jit(solution)/shard_map/ppermute | solution.py:112
  30.1 29.6 %collective-permute-start.9 = (bf16[128,2048]{1,0:T(8,128)(2,1)S(1)}, bf16[128,2048]{1,0:T(8,128)(2,1)}, u32[]{:S(2)}, u32[]{:S(2)}) collective-permute-start(bf16[128,2048]{1,0:T(8,128)(2,1)S(1)} %copy-done.21), channel_id=1, source_target_pairs={{1,0},{2,1},{3,2},{5,4},{6,5},{7,6},{9,8},{10,9},{11,10},{13,12},{... | collective-permute-start | bytes 1572872 | tf_op jit(solution)/shard_map/ppermute | solution.py:112
  31.4 29.8 %collective-permute-start.2 = (bf16[128,2176]{1,0:T(8,128)(2,1)S(1)}, bf16[128,2176]{1,0:T(8,128)(2,1)S(1)}, u32[]{:S(2)}, u32[]{:S(2)}) collective-permute-start(bf16[128,2176]{1,0:T(8,128)(2,1)S(1)} %collective-permute-done.refs_1_.refs_8_), channel_id=1, source_target_pairs={{1,2},{2,3},{5,6},{6,7},{9,10},{10,11},{13,14},{14,15},{17,18},{18... | collective-permute-start | bytes 1671176 | tf_op jit(solution)/shard_map/ppermute | solution.py:112
  32.1 35.5 %collective-permute-start.4 = (bf16[128,2176]{1,0:T(8,128)(2,1)S(1)}, bf16[128,2176]{1,0:T(8,128)(2,1)S(1)}, u32[]{:S(2)}, u32[]{:S(2)}) collective-permute-start(bf16[128,2176]{1,0:T(8,128)(2,1)S(1)} %collective-permute-done.1.refs_4_.refs_11_), channel_id=1, source_target_pairs={{1,0},{2,1},{5,4},{6,5},{9,8},{10,9},{13,12},{14,13},{17,16},{18,1... | collective-permute-start | bytes 1671176 | tf_op jit(solution)/shard_map/ppermute | solution.py:112
  52.8 31.7 %collective-permute-start.14 = (bf16[512,768]{1,0:T(8,128)(2,1)}, bf16[512,768]{1,0:T(8,128)(2,1)}, u32[]{:S(2)}, u32[]{:S(2)}) collective-permute-start(bf16[512,768]{1,0:T(8,128)(2,1)} %get-tuple-element.104), channel_id=1, source_target_pairs={{0,3},{1,0},{2,1},{3,2},{4,7},{5,4},{6,5},{7,6},{8,11},{9,8},{10,9... | collective-permute-start | bytes 2359304 | tf_op jit(solution)/shard_map/ppermute | solution.py:63
  59.7 35.1 %collective-permute-start.7 = (bf16[128,2048]{1,0:T(8,128)(2,1)}, bf16[128,2048]{1,0:T(8,128)(2,1)}, u32[]{:S(2)}, u32[]{:S(2)}) collective-permute-start(bf16[128,2048]{1,0:T(8,128)(2,1)} %collective-permute-done.6.refs_8_), channel_id=1, source_target_pairs={{1,2},{2,3},{5,6},{6,7},{9,10},{10,11},{13,14},{14,15},{17,18},{18... | collective-permute-start | bytes 1572872 | tf_op jit(solution)/shard_map/ppermute | solution.py:112
  61.1 50.2 %collective-permute-start.10 = (bf16[128,2048]{1,0:T(8,128)(2,1)}, bf16[128,2048]{1,0:T(8,128)(2,1)}, u32[]{:S(2)}, u32[]{:S(2)}) collective-permute-start(bf16[128,2048]{1,0:T(8,128)(2,1)} %collective-permute-done.9.refs_11_), channel_id=1, source_target_pairs={{1,0},{2,1},{5,4},{6,5},{9,8},{10,9},{13,12},{14,13},{17,16},{18,1... | collective-permute-start | bytes 1572872 | tf_op jit(solution)/shard_map/ppermute | solution.py:112
  67.5 45.2 %collective-permute-start.3 = (bf16[128,2176]{1,0:T(8,128)(2,1)S(1)}, bf16[128,2176]{1,0:T(8,128)(2,1)S(1)}, u32[]{:S(2)}, u32[]{:S(2)}) collective-permute-start(bf16[128,2176]{1,0:T(8,128)(2,1)S(1)} %collective-permute-done.2.refs_2_.refs_9_), channel_id=1, source_target_pairs={{2,3},{6,7},{10,11},{14,15},{18,19},{22,23},{26,27},{30,31}} | collective-permute-start | bytes 1671176 | tf_op jit(solution)/shard_map/ppermute | solution.py:112
  69.1 46.7 %collective-permute-start.5 = (bf16[128,2176]{1,0:T(8,128)(2,1)S(1)}, bf16[128,2176]{1,0:T(8,128)(2,1)}, u32[]{:S(2)}, u32[]{:S(2)}) collective-permute-start(bf16[128,2176]{1,0:T(8,128)(2,1)S(1)} %collective-permute-done.4.refs_5_.refs_12_), channel_id=1, source_target_pairs={{1,0},{5,4},{9,8},{13,12},{17,16},{21,20},{25,24},{29,28}} | collective-permute-start | bytes 1671176 | tf_op jit(solution)/shard_map/ppermute | solution.py:112
  84.5 41.4 %collective-permute-start.13 = (bf16[256,768]{1,0:T(8,128)(2,1)}, bf16[256,768]{1,0:T(8,128)(2,1)}, u32[]{:S(2)}, u32[]{:S(2)}) collective-permute-start(bf16[256,768]{1,0:T(8,128)(2,1)} %get-tuple-element.103), channel_id=1, source_target_pairs={{0,2},{1,3},{2,0},{3,1},{4,6},{5,7},{6,4},{7,5},{8,10},{9,11},{10,... | collective-permute-start | bytes 1179656 | tf_op jit(solution)/shard_map/ppermute | solution.py:63
  94.8 37.5 %collective-permute-start.15 = (bf16[256,768]{1,0:T(8,128)(2,1)}, bf16[256,768]{1,0:T(8,128)(2,1)}, u32[]{:S(2)}, u32[]{:S(2)}) collective-permute-start(bf16[256,768]{1,0:T(8,128)(2,1)} %get-tuple-element.105), channel_id=1, source_target_pairs={{0,2},{1,3},{2,0},{3,1},{4,6},{5,7},{6,4},{7,5},{8,10},{9,11},{10,... | collective-permute-start | bytes 1179656 | tf_op jit(solution)/shard_map/ppermute | solution.py:63
  112.8 43.6 %collective-permute-start.11 = (bf16[128,2048]{1,0:T(8,128)(2,1)}, bf16[128,2048]{1,0:T(8,128)(2,1)}, u32[]{:S(2)}, u32[]{:S(2)}) collective-permute-start(bf16[128,2048]{1,0:T(8,128)(2,1)} %collective-permute-done.10.refs_12_), channel_id=1, source_target_pairs={{1,0},{5,4},{9,8},{13,12},{17,16},{21,20},{25,24},{29,28}} | collective-permute-start | bytes 1572872 | tf_op jit(solution)/shard_map/ppermute | solution.py:112
  121.1 53.7 %all-to-all-start = ((bf16[8,4,32,2048]{3,2,1,0:T(8,128)(2,1)}), bf16[8,4,32,2048]{3,2,1,0:T(8,128)(2,1)}, u32[]{:S(2)}, u32[]{:S(2)}) async-start(bf16[8,4,32,2048]{3,2,1,0:T(8,128)(2,1)} %shard_map.85), calls=%async_computation | async-start | bytes 8388608 | tf_op jit(solution)/shard_map/all_to_all | solution.py:520
  125.9 36.6 %collective-permute-start.16 = (bf16[512,768]{1,0:T(8,128)(2,1)}, bf16[512,768]{1,0:T(8,128)(2,1)S(1)}, u32[]{:S(2)}, u32[]{:S(2)}) collective-permute-start(bf16[512,768]{1,0:T(8,128)(2,1)} %get-tuple-element.106), channel_id=1, source_target_pairs={{0,1},{1,2},{2,3},{3,0},{4,5},{5,6},{6,7},{7,4},{8,9},{9,10},{10,1... | collective-permute-start | bytes 2359304 | tf_op jit(solution)/shard_map/ppermute | solution.py:63
  132.3 37.1 %collective-permute-start.18 = (bf16[512,768]{1,0:T(8,128)(2,1)}, bf16[512,768]{1,0:T(8,128)(2,1)S(1)}, u32[]{:S(2)}, u32[]{:S(2)}) collective-permute-start(bf16[512,768]{1,0:T(8,128)(2,1)} %get-tuple-element.108), channel_id=1, source_target_pairs={{0,3},{1,0},{2,1},{3,2},{4,7},{5,4},{6,5},{7,6},{8,11},{9,8},{10,9... | collective-permute-start | bytes 2359304 | tf_op jit(solution)/shard_map/ppermute | solution.py:63
  163.7 27.0 %collective-permute-start.17 = (bf16[256,768]{1,0:T(8,128)(2,1)S(1)}, bf16[256,768]{1,0:T(8,128)(2,1)S(1)}, u32[]{:S(2)}, u32[]{:S(2)}) collective-permute-start(bf16[256,768]{1,0:T(8,128)(2,1)S(1)} %copy-done.64), channel_id=1, source_target_pairs={{0,2},{1,3},{2,0},{3,1},{4,6},{5,7},{6,4},{7,5},{8,10},{9,11},{10,... | collective-permute-start | bytes 1179656 | tf_op jit(solution)/shard_map/ppermute | solution.py:63
  170.3 45.5 %collective-permute-start.19 = (bf16[256,768]{1,0:T(8,128)(2,1)S(1)}, bf16[256,768]{1,0:T(8,128)(2,1)S(1)}, u32[]{:S(2)}, u32[]{:S(2)}) collective-permute-start(bf16[256,768]{1,0:T(8,128)(2,1)S(1)} %copy-done.63), channel_id=1, source_target_pairs={{0,2},{1,3},{2,0},{3,1},{4,6},{5,7},{6,4},{7,5},{8,10},{9,11},{10,... | collective-permute-start | bytes 1179656 | tf_op jit(solution)/shard_map/ppermute | solution.py:63
  174.8 54.8 %all-to-all-start.1 = ((bf16[8,4,32,2048]{3,2,1,0:T(8,128)(2,1)}), bf16[8,4,32,2048]{3,2,1,0:T(8,128)(2,1)}, u32[]{:S(2)}, u32[]{:S(2)}) async-start(bf16[8,4,32,2048]{3,2,1,0:T(8,128)(2,1)} %shard_map.95), calls=%async_computation.1 | async-start | bytes 8388608 | tf_op jit(solution)/shard_map/all_to_all | solution.py:520
  216.6 41.6 %collective-permute-start.22 = (bf16[512,768]{1,0:T(8,128)(2,1)}, bf16[512,768]{1,0:T(8,128)(2,1)}, u32[]{:S(2)}, u32[]{:S(2)}) collective-permute-start(bf16[512,768]{1,0:T(8,128)(2,1)} %get-tuple-element.116), channel_id=1, source_target_pairs={{0,3},{1,0},{2,1},{3,2},{4,7},{5,4},{6,5},{7,6},{8,11},{9,8},{10,9... | collective-permute-start | bytes 2359304 | tf_op jit(solution)/shard_map/ppermute | solution.py:63
  229.6 44.7 %collective-permute-start.21 = (bf16[256,768]{1,0:T(8,128)(2,1)}, bf16[256,768]{1,0:T(8,128)(2,1)}, u32[]{:S(2)}, u32[]{:S(2)}) collective-permute-start(bf16[256,768]{1,0:T(8,128)(2,1)} %get-tuple-element.115), channel_id=1, source_target_pairs={{0,2},{1,3},{2,0},{3,1},{4,6},{5,7},{6,4},{7,5},{8,10},{9,11},{10,... | collective-permute-start | bytes 1179656 | tf_op jit(solution)/shard_map/ppermute | solution.py:63
  276.3 34.6 %collective-permute-start.25 = (bf16[512,768]{1,0:T(8,128)(2,1)}, bf16[512,768]{1,0:T(8,128)(2,1)}, u32[]{:S(2)}, u32[]{:S(2)}) collective-permute-start(bf16[512,768]{1,0:T(8,128)(2,1)} %shard_map.97), channel_id=1, source_target_pairs={{0,1},{1,2},{2,3},{3,0},{4,5},{5,6},{6,7},{7,4},{8,9},{9,10},{10,1... | collective-permute-start | bytes 2359304 | tf_op jit(solution)/shard_map/ppermute | solution.py:63
  294.1 37.9 %collective-permute-start.26 = (bf16[256,768]{1,0:T(8,128)(2,1)}, bf16[256,768]{1,0:T(8,128)(2,1)}, u32[]{:S(2)}, u32[]{:S(2)}) collective-permute-start(bf16[256,768]{1,0:T(8,128)(2,1)} %copy-done.54), channel_id=1, source_target_pairs={{0,2},{1,3},{2,0},{3,1},{4,6},{5,7},{6,4},{7,5},{8,10},{9,11},{10,... | collective-permute-start | bytes 1179656 | tf_op jit(solution)/shard_map/ppermute | solution.py:63
  324.1 53.7 %all-to-all-start.2 = ((bf16[8,4,32,2048]{3,2,1,0:T(8,128)(2,1)}), bf16[8,4,32,2048]{3,2,1,0:T(8,128)(2,1)}, u32[]{:S(2)}, u32[]{:S(2)}) async-start(bf16[8,4,32,2048]{3,2,1,0:T(8,128)(2,1)} %bitcast.15), calls=%async_computation.2 | async-start | bytes 8388608 | tf_op jit(solution)/shard_map/all_to_all | solution.py:520
  332.0 35.4 %collective-permute-start.27 = (bf16[512,768]{1,0:T(8,128)(2,1)}, bf16[512,768]{1,0:T(8,128)(2,1)}, u32[]{:S(2)}, u32[]{:S(2)}) collective-permute-start(bf16[512,768]{1,0:T(8,128)(2,1)} %get-tuple-element.127), channel_id=1, source_target_pairs={{0,3},{1,0},{2,1},{3,2},{4,7},{5,4},{6,5},{7,6},{8,11},{9,8},{10,9... | collective-permute-start | bytes 2359304 | tf_op jit(solution)/shard_map/ppermute | solution.py:63
  351.9 42.2 %collective-permute-start.35 = (bf16[512,768]{1,0:T(8,128)(2,1)}, bf16[512,768]{1,0:T(8,128)(2,1)}, u32[]{:S(2)}, u32[]{:S(2)}) collective-permute-start(bf16[512,768]{1,0:T(8,128)(2,1)} %get-tuple-element.141), channel_id=1, source_target_pairs={{0,1},{1,2},{2,3},{3,0},{4,5},{5,6},{6,7},{7,4},{8,9},{9,10},{10,1... | collective-permute-start | bytes 2359304 | tf_op jit(solution)/shard_map/ppermute | solution.py:63
  398.0 67.0 %all-to-all-start.3 = ((bf16[8,4,32,2048]{3,2,1,0:T(8,128)(2,1)}), bf16[8,4,32,2048]{3,2,1,0:T(8,128)(2,1)}, u32[]{:S(2)}, u32[]{:S(2)}) async-start(bf16[8,4,32,2048]{3,2,1,0:T(8,128)(2,1)} %bitcast.14), calls=%async_computation.3 | async-start | bytes 8388608 | tf_op jit(solution)/shard_map/all_to_all | solution.py:520
  420.9 26.1 %collective-permute-start.29 = (bf16[128,2048]{1,0:T(8,128)(2,1)}, bf16[128,2048]{1,0:T(8,128)(2,1)}, u32[]{:S(2)}, u32[]{:S(2)}) collective-permute-start(bf16[128,2048]{1,0:T(8,128)(2,1)} %get-tuple-element.176), channel_id=1, source_target_pairs={{0,1},{1,2},{4,5},{5,6},{8,9},{9,10},{12,13},{13,14},{16,17},{17,1... | collective-permute-start | bytes 1572872 | tf_op jit(solution)/shard_map/ppermute | solution.py:112
  485.3 31.7 %collective-permute-start.49 = (bf16[512,768]{1,0:T(8,128)(2,1)}, bf16[512,768]{1,0:T(8,128)(2,1)S(1)}, u32[]{:S(2)}, u32[]{:S(2)}) collective-permute-start(bf16[512,768]{1,0:T(8,128)(2,1)} %get-tuple-element.157), channel_id=1, source_target_pairs={{0,1},{1,2},{2,3},{3,0},{4,5},{5,6},{6,7},{7,4},{8,9},{9,10},{10,1... | collective-permute-start | bytes 2359304 | tf_op jit(solution)/shard_map/ppermute | solution.py:63
  500.7 25.6 %collective-permute-start.38 = (bf16[128,2048]{1,0:T(8,128)(2,1)}, bf16[128,2048]{1,0:T(8,128)(2,1)}, u32[]{:S(2)}, u32[]{:S(2)}) collective-permute-start(bf16[128,2048]{1,0:T(8,128)(2,1)} %get-tuple-element.174), channel_id=1, source_target_pairs={{0,1},{1,2},{4,5},{5,6},{8,9},{9,10},{12,13},{13,14},{16,17},{17,1... | collective-permute-start | bytes 1572872 | tf_op jit(solution)/shard_map/ppermute | solution.py:112
  505.9 26.2 %collective-permute-start.41 = (bf16[128,2048]{1,0:T(8,128)(2,1)}, bf16[128,2048]{1,0:T(8,128)(2,1)}, u32[]{:S(2)}, u32[]{:S(2)}) collective-permute-start(bf16[128,2048]{1,0:T(8,128)(2,1)} %get-tuple-element.175), channel_id=1, source_target_pairs={{2,1},{3,2},{6,5},{7,6},{10,9},{11,10},{14,13},{15,14},{18,17},{19... | collective-permute-start | bytes 1572872 | tf_op jit(solution)/shard_map/ppermute | solution.py:112
  517.9 26.1 %collective-permute-start.50 = (bf16[256,768]{1,0:T(8,128)(2,1)}, bf16[256,768]{1,0:T(8,128)(2,1)}, u32[]{:S(2)}, u32[]{:S(2)}) collective-permute-start(bf16[256,768]{1,0:T(8,128)(2,1)} %copy-done.57), channel_id=1, source_target_pairs={{0,2},{1,3},{2,0},{3,1},{4,6},{5,7},{6,4},{7,5},{8,10},{9,11},{10,... | collective-permute-start | bytes 1179656 | tf_op jit(solution)/shard_map/ppermute | solution.py:63
  (90 other events, 1329.5 us)

commit v4 on v3

--- a/solution.py
+++ b/solution.py
@@ -26,8 +26,8 @@
  18: ['back_out'],
  19: ['out_parts'],
  20: ['o1'],
- 21: ['o2', 'back_grad'],
- 22: ['o3', 'grad_parts', 'gate_grad']}
+ 21: ['o2'],
+ 22: ['o3', 'grad_parts', 'gate_grad', 'back_grad']}
 GATES = {'back_out': [12],
  'down': ['other_down_grads', 'middle_down_grad', 'own_down_grad'],
  'g1': ['t1'],

time: 560 us -> 557 us (level)
  waiting for transfers between devices: 200 us -> 185 us
  starting transfers between devices: 184 us -> 195 us
    ppermute x27, waiting for transfers between devices: 120 us -> 91.7 us  [shift(): return lax.ppermute(x, 'narrow', [(i, (i + k) % n) for i in range(n)])]
    ppermute x24, waiting for transfers between devices: 69.9 us -> 84 us  [hop(): return lax.ppermute(x, 'narrow', [(i, i + step) for i in sources])]
    ppermute x24, starting transfers between devices: 53.9 us -> 61.4 us  [hop(): return lax.ppermute(x, 'narrow', [(i, i + step) for i in sources])]
    unnamed x135 -> x131, local copies, waits for them, and re-layouts: 24.2 us -> 24.8 us
where the time goes in v4:
time: 557 us; the launch traced here: 553 us
  starting transfers between devices  195 us (35%)
  waiting for transfers between devices  185 us (33%)
  Pallas kernels  120 us (22%)
  local copies, waits for them, and re-layouts  31 us (6%)
  other arithmetic  20.9 us (4%)
    ppermute x27, starting transfers between devices, shift(): return lax.ppermute(x, 'narrow', [(i, (i + k) % n) for i in range(n)])  115 us
    ppermute x27, waiting for transfers between devices, shift(): return lax.ppermute(x, 'narrow', [(i, (i + k) % n) for i in range(n)])  91.7 us
    ppermute x24, waiting for transfers between devices, hop(): return lax.ppermute(x, 'narrow', [(i, i + step) for i in sources])  84 us
    ppermute x24, starting transfers between devices, hop(): return lax.ppermute(x, 'narrow', [(i, i + step) for i in sources])  61.4 us
    pallas_call x10, Pallas kernels, weight_grad(): pl.pallas_call(weight_grad_kernel, out_shape=[jax.ShapeDtypeStruct((width...  34.1 us
    unnamed x131, local copies, waits for them, and re-layouts  24.8 us
    pallas_call x3, Pallas kernels, join_shard(): pl.pallas_call(functools.partial(join_kernel, n), out_shape=jax.ShapeDtyp...  20.2 us
    all_to_all x4, starting transfers between devices, swap(): return lax.all_to_all(x, 'wide', split_axis=0, concat_axis=0, tiled=True)  18.4 us
  transfers between devices with their start and end apart: 55, of which 29 were waited for; matrix products, arithmetic and copies ran while one was open for 4% of the time, Pallas kernels for 22%

profile of v4, /device:TPU:0, one launch (start us, length us, event | category | flops | bytes accessed | tf_op | source)
XLA Modules:
  0.0 553.5 jit_solution(2817972108470597808)
XLA Ops:
  5.7 5.6 %collective-permute-start = (bf16[128,2176]{1,0:T(8,128)(2,1)S(1)}, bf16[128,2176]{1,0:T(8,128)(2,1)S(1)}, u32[]{:S(2)}, u32[]{:S(2)}) collective-permute-start(bf16[128,2176]{1,0:T(8,128)(2,1)S(1)} %concatenate.12.refs_0_.refs_7_), channel_id=1, source_target_pairs={{0,1},{1,2},{2,3},{4,5},{5,6},{6,7},{8,9},{9,10},{10,11},{12,13},{... | collective-permute-start | bytes 1671176 | tf_op jit(solution)/shard_map/ppermute | solution.py:112
  11.3 9.7 %shard_map.84 = (bf16[512,768]{1,0:T(8,128)(2,1)S(1)}, bf16[512,768]{1,0:T(8,128)(2,1)S(1)}, bf16[512,768]{1,0:T(8,128)(2,1)S(1)}, bf16[512,768]{1,0:T(8,128)(2,...) custom-call(s32[1]{0:T(128)} %bitcast.level_ref, ...), custom_call_target="tpu_custom_call" | custom-call | tf_op jit(solution)/shard_map/pallas_call | solution.py:150
  37.3 15.5 %collective-permute-done.6.refs_8_ = bf16[128,2048]{1,0:T(8,128)(2,1)} collective-permute-done((bf16[128,2048]{1,0:T(8,128)(2,1)S(1)}, bf16[128,2048]{1,0:T(8,128)(2,1)}, u32[]{:S(2)}, u32[]{:S(2)}) %collective-permute-start.6) | collective-permute-done | bytes 524320 | tf_op jit(solution)/shard_map/ppermute | solution.py:112
  52.8 6.9 %collective-permute-start.14 = (bf16[512,768]{1,0:T(8,128)(2,1)}, bf16[512,768]{1,0:T(8,128)(2,1)}, u32[]{:S(2)}, u32[]{:S(2)}) collective-permute-start(bf16[512,768]{1,0:T(8,128)(2,1)} %get-tuple-element.104), channel_id=1, source_target_pairs={{0,3},{1,0},{2,1},{3,2},{4,7},{5,4},{6,5},{7,6},{8,11},{9,8},{10,9... | collective-permute-start | bytes 2359304 | tf_op jit(solution)/shard_map/ppermute | solution.py:63
  70.4 14.1 %collective-permute-done.14.moved_ref = bf16[512,768]{1,0:T(8,128)(2,1)} collective-permute-done((bf16[512,768]{1,0:T(8,128)(2,1)}, bf16[512,768]{1,0:T(8,128)(2,1)}, u32[]{:S(2)}, u32[]{:S(2)}) %collective-permute-start.14) | collective-permute-done | bytes 786464 | tf_op jit(solution)/shard_map/ppermute | solution.py:63
  84.5 10.3 %collective-permute-start.13 = (bf16[256,768]{1,0:T(8,128)(2,1)}, bf16[256,768]{1,0:T(8,128)(2,1)}, u32[]{:S(2)}, u32[]{:S(2)}) collective-permute-start(bf16[256,768]{1,0:T(8,128)(2,1)} %get-tuple-element.103), channel_id=1, source_target_pairs={{0,2},{1,3},{2,0},{3,1},{4,6},{5,7},{6,4},{7,5},{8,10},{9,11},{10,... | collective-permute-start | bytes 1179656 | tf_op jit(solution)/shard_map/ppermute | solution.py:63
  94.8 16.5 %collective-permute-start.15 = (bf16[256,768]{1,0:T(8,128)(2,1)}, bf16[256,768]{1,0:T(8,128)(2,1)}, u32[]{:S(2)}, u32[]{:S(2)}) collective-permute-start(bf16[256,768]{1,0:T(8,128)(2,1)} %get-tuple-element.105), channel_id=1, source_target_pairs={{0,2},{1,3},{2,0},{3,1},{4,6},{5,7},{6,4},{7,5},{8,10},{9,11},{10,... | collective-permute-start | bytes 1179656 | tf_op jit(solution)/shard_map/ppermute | solution.py:63
  125.9 6.3 %collective-permute-start.16 = (bf16[512,768]{1,0:T(8,128)(2,1)}, bf16[512,768]{1,0:T(8,128)(2,1)S(1)}, u32[]{:S(2)}, u32[]{:S(2)}) collective-permute-start(bf16[512,768]{1,0:T(8,128)(2,1)} %get-tuple-element.106), channel_id=1, source_target_pairs={{0,1},{1,2},{2,3},{3,0},{4,5},{5,6},{6,7},{7,4},{8,9},{9,10},{10,1... | collective-permute-start | bytes 2359304 | tf_op jit(solution)/shard_map/ppermute | solution.py:63
  132.3 24.1 %collective-permute-done.11.refs_13_ = bf16[128,2048]{1,0:T(8,128)(2,1)} collective-permute-done((bf16[128,2048]{1,0:T(8,128)(2,1)}, bf16[128,2048]{1,0:T(8,128)(2,1)}, u32[]{:S(2)}, u32[]{:S(2)}) %collective-permute-start.11) | collective-permute-done | bytes 524320 | tf_op jit(solution)/shard_map/ppermute | solution.py:112
  156.4 6.1 %shard_map.95 = bf16[8,4,32,2048]{3,2,1,0:T(8,128)(2,1)} custom-call(s32[1]{0:T(128)} %bitcast.level_ref, bf16[128,2176]{1,0:T(8,128)(2,1)} %copy-done.4, bf16[128,2176]{1,0:T(8,128)(2,1)} %copy-done.7, bf16[128,2176]{1,0:T(8,128)(2,1)} %copy-done.9, bf16[128,2176]{1,0:T(8,128)(2,1)} %copy-done.12, bf16[128,2176]{1,0:T(8,128)(2,1)} %copy-done.6, ...), custom_call_target="tpu_custom_call" | custom-call | tf_op jit(solution)/shard_map/pallas_call | solution.py:260
  163.7 5.7 %collective-permute-done.18.moved_ref = bf16[512,768]{1,0:T(8,128)(2,1)S(1)} collective-permute-done((bf16[512,768]{1,0:T(8,128)(2,1)}, bf16[512,768]{1,0:T(8,128)(2,1)S(1)}, u32[]{:S(2)}, u32[]{:S(2)}) %collective-permute-start.18) | collective-permute-done | bytes 786464 | tf_op jit(solution)/shard_map/ppermute | solution.py:63
  179.3 11.4 %collective-permute-done.17.moved_ref = bf16[256,768]{1,0:T(8,128)(2,1)S(1)} collective-permute-done((bf16[256,768]{1,0:T(8,128)(2,1)S(1)}, bf16[256,768]{1,0:T(8,128)(2,1)S(1)}, u32[]{:S(2)}, u32[]{:S(2)}) %collective-permute-start.17) | collective-permute-done | bytes 393248 | tf_op jit(solution)/shard_map/ppermute | solution.py:63
  194.2 21.6 %collective-permute-done.19.moved_ref = bf16[256,768]{1,0:T(8,128)(2,1)S(1)} collective-permute-done((bf16[256,768]{1,0:T(8,128)(2,1)S(1)}, bf16[256,768]{1,0:T(8,128)(2,1)S(1)}, u32[]{:S(2)}, u32[]{:S(2)}) %collective-permute-start.19) | collective-permute-done | bytes 393248 | tf_op jit(solution)/shard_map/ppermute | solution.py:63
  218.4 11.2 %shard_map.94 = (bf16[1024,768]{1,0:T(8,128)(2,1)}, f32[1024,768]{1,0:T(8,128)}, f32[1024,768]{1,0:T(8,128)}) custom-call(bf16[1024,2048]{1,0:T(8,128)(2,1)} %bitcast.1.refs_0_.rows_ref, bf16[512,768]{1,0:T(8,128)(2,1)S(1)} %copy-done.17, bf16[512,768]{1,0:T(8,128)(2,1)S(1)} %copy-done.20, bf16[256,768]{1,0:T(8,128)(2,1)} %shard_map.87.refs_3_.refs_4_, ...), custom_call_target="tpu_custom_call" | custom-call | tf_op jit(solution)/shard_map/pallas_call | solution.py:399
  229.6 28.5 %collective-permute-start.21 = (bf16[256,768]{1,0:T(8,128)(2,1)}, bf16[256,768]{1,0:T(8,128)(2,1)}, u32[]{:S(2)}, u32[]{:S(2)}) collective-permute-start(bf16[256,768]{1,0:T(8,128)(2,1)} %get-tuple-element.115), channel_id=1, source_target_pairs={{0,2},{1,3},{2,0},{3,1},{4,6},{5,7},{6,4},{7,5},{8,10},{9,11},{10,... | collective-permute-start | bytes 1179656 | tf_op jit(solution)/shard_map/ppermute | solution.py:63
  280.0 11.3 %shard_map.105 = (bf16[1024,2048]{1,0:T(8,128)(2,1)}, bf16[1024,768]{1,0:T(8,128)(2,1)}, bf16[1024,768]{1,0:T(8,128)(2,1)}) custom-call(bf16[1024,768]{1,0:T(8,128)(2,1)} %get-tuple-element.111.refs_0_, bf16[1024,2048]{1,0:T(8,128)(2,1)} %bitcast.2.rows_ref.refs_1_, f32[1024,768]{1,0:T(8,128)} %get-tuple-element.112.refs_2_, ...), custom_call_target="tpu_custom_call" | custom-call | tf_op jit(solution)/shard_map/pallas_call | solution.py:431
  299.2 11.7 %collective-permute-done.25.moved_ref = bf16[512,768]{1,0:T(8,128)(2,1)} collective-permute-done((bf16[512,768]{1,0:T(8,128)(2,1)}, bf16[512,768]{1,0:T(8,128)(2,1)}, u32[]{:S(2)}, u32[]{:S(2)}) %collective-permute-start.25) | collective-permute-done | bytes 786464 | tf_op jit(solution)/shard_map/ppermute | solution.py:63
  332.0 8.4 %collective-permute-done.34.moved_ref = bf16[256,768]{1,0:T(8,128)(2,1)S(1)} collective-permute-done((bf16[256,768]{1,0:T(8,128)(2,1)}, bf16[256,768]{1,0:T(8,128)(2,1)S(1)}, u32[]{:S(2)}, u32[]{:S(2)}) %collective-permute-start.34) | collective-permute-done | bytes 393248 | tf_op jit(solution)/shard_map/ppermute | solution.py:63
  341.1 10.7 %shard_map.113 = bf16[1024,2048]{1,0:T(8,128)(2,1)} custom-call(bf16[1024,768]{1,0:T(8,128)(2,1)} %get-tuple-element.151.refs_0_, bf16[1024,768]{1,0:T(8,128)(2,1)} %get-tuple-element.124.refs_1_, bf16[512,768]{1,0:T(8,128)(2,1)S(1)} %copy-done.17, bf16[512,768]{1,0:T(8,128)(2,1)S(1)} %copy-done.20, bf16[256,768]{1,0:T(8,128)(2,1)} %shard_map.87.refs_3_.refs_4_, ...), custom_call_target="tpu_custom_call" | custom-call | tf_op jit(solution)/shard_map/pallas_call | solution.py:459
  351.9 13.6 %collective-permute-start.35 = (bf16[512,768]{1,0:T(8,128)(2,1)}, bf16[512,768]{1,0:T(8,128)(2,1)}, u32[]{:S(2)}, u32[]{:S(2)}) collective-permute-start(bf16[512,768]{1,0:T(8,128)(2,1)} %get-tuple-element.141), channel_id=1, source_target_pairs={{0,1},{1,2},{2,3},{3,0},{4,5},{5,6},{6,7},{7,4},{8,9},{9,10},{10,1... | collective-permute-start | bytes 2359304 | tf_op jit(solution)/shard_map/ppermute | solution.py:63
  378.9 6.5 %shard_map.111 = (bf16[128,2048]{1,0:T(8,128)(2,1)S(1)}, bf16[128,2048]{1,0:T(8,128)(2,1)S(1)}, bf16[128,2048]{1,0:T(8,128)(2,1)S(1)}, bf16[128,2048]{1,0:T(8,128)(2,1)S(1)}, f32[4,4,128]{2,1,0:T(4,128)S(1)}) custom-call(s32[1]{0:T(128)} %bitcast.level_ref, bf16[128,2176]{1,0:T(8,128)(2,1)} %copy-done.4, bf16[128,2176]{1,0:T(8,128)(2,1)} %copy-done.7, ...), custom_call_target="tpu_custom_call" | custom-call | tf_op jit(solution)/shard_map/pallas_call | solution.py:359
  409.0 9.4 %collective-permute-done.28 = bf16[128,2048]{1,0:T(8,128)(2,1)} collective-permute-done((bf16[128,2048]{1,0:T(8,128)(2,1)S(1)}, bf16[128,2048]{1,0:T(8,128)(2,1)}, u32[]{:S(2)}, u32[]{:S(2)}) %collective-permute-start.28) | collective-permute-done | bytes 524320 | tf_op jit(solution)/shard_map/ppermute | solution.py:112
  420.9 5.3 collective-permute-start.29
  434.2 6.7 %shard_map.126.refs_4_ = bf16[512,4,2304]{2,1,0:T(4,128)(2,1)} custom-call(s32[1]{0:T(128)} %bitcast.level_ref, bf16[512,768]{1,0:T(8,128)(2,1)S(1)} %copy-done.14, bf16[512,768]{1,0:T(8,128)(2,1)S(1)} %copy-done.34, bf16[512,768]{1,0:T(8,128)(2,1)S(1)} %copy-done.15, bf16[512,768]{1,0:T(8,128)(2,1)} %shard_map.107.refs_3_), custom_call_target="tpu_custom_call" | custom-call | tf_op jit(solution)/shard_map/pallas_call | solution.py:177
  440.9 6.1 %collective-permute-start.47 = (bf16[512,768]{1,0:T(8,128)(2,1)S(1)}, bf16[512,768]{1,0:T(8,128)(2,1)}, u32[]{:S(2)}, u32[]{:S(2)}) collective-permute-start(bf16[512,768]{1,0:T(8,128)(2,1)S(1)} %copy-done.53), channel_id=1, source_target_pairs={{0,3},{1,0},{2,1},{3,2},{4,7},{5,4},{6,5},{7,6},{8,11},{9,8},{10,9... | collective-permute-start | bytes 2359304 | tf_op jit(solution)/shard_map/ppermute | solution.py:63
  456.1 8.9 %collective-permute-done.47.moved_ref = bf16[512,768]{1,0:T(8,128)(2,1)} collective-permute-done((bf16[512,768]{1,0:T(8,128)(2,1)S(1)}, bf16[512,768]{1,0:T(8,128)(2,1)}, u32[]{:S(2)}, u32[]{:S(2)}) %collective-permute-start.47) | collective-permute-done | bytes 786464 | tf_op jit(solution)/shard_map/ppermute | solution.py:63
  465.0 11.3 %collective-permute-done.30 = bf16[128,2048]{1,0:T(8,128)(2,1)} collective-permute-done((bf16[128,2048]{1,0:T(8,128)(2,1)}, bf16[128,2048]{1,0:T(8,128)(2,1)}, u32[]{:S(2)}, u32[]{:S(2)}) %collective-permute-start.30) | collective-permute-done | bytes 524320 | tf_op jit(solution)/shard_map/ppermute | solution.py:112
  486.9 5.3 collective-permute-start.37
  494.2 6.7 %shard_map.127.refs_4_ = bf16[512,4,2304]{2,1,0:T(4,128)(2,1)} custom-call(s32[1]{0:T(128)} %bitcast.level_ref, bf16[512,768]{1,0:T(8,128)(2,1)S(1)} %copy-done.30, bf16[512,768]{1,0:T(8,128)(2,1)} %shard_map.110.refs_1_, bf16[512,768]{1,0:T(8,128)(2,1)S(1)} %pad_maximum_fusion.1.refs_2_, ...), custom_call_target="tpu_custom_call", output_to_operand_aliasing={{}: (5, {})} | custom-call | tf_op jit(solution)/shard_map/pallas_call | solution.py:177
  516.3 7.7 %collective-permute-done.38 = bf16[128,2048]{1,0:T(8,128)(2,1)} collective-permute-done((bf16[128,2048]{1,0:T(8,128)(2,1)S(1)}, bf16[128,2048]{1,0:T(8,128)(2,1)}, u32[]{:S(2)}, u32[]{:S(2)}) %collective-permute-start.38) | collective-permute-done | bytes 524320 | tf_op jit(solution)/shard_map/ppermute | solution.py:112
  525.4 10.9 %collective-permute-start.39 = (bf16[128,2048]{1,0:T(8,128)(2,1)S(1)}, bf16[128,2048]{1,0:T(8,128)(2,1)}, u32[]{:S(2)}, u32[]{:S(2)}) collective-permute-start(bf16[128,2048]{1,0:T(8,128)(2,1)S(1)} %add_convert_fusion.2), channel_id=1, source_target_pairs={{0,1},{1,2},{2,3},{4,5},{5,6},{6,7},{8,9},{9,10},{10,11},{12,13},{... | collective-permute-start | bytes 1572872 | tf_op jit(solution)/shard_map/ppermute | solution.py:112
  541.3 6.8 %shard_map.128 = bf16[512,4,2304]{2,1,0:T(4,128)(2,1)} custom-call(s32[1]{0:T(128)} %bitcast.level_ref, bf16[512,768]{1,0:T(8,128)(2,1)S(1)} %get-tuple-element.152.refs_0_, bf16[512,768]{1,0:T(8,128)(2,1)} %shard_map.122.refs_1_, bf16[512,768]{1,0:T(8,128)(2,1)S(1)} %pad_maximum_fusion.refs_2_, ...), custom_call_target="tpu_custom_call", output_to_operand_aliasing={{}: (5, {})} | custom-call | tf_op jit(solution)/shard_map/pallas_call | solution.py:177
  (278 shorter events, 211.4 us)
Async XLA Ops:
  23.2 45.1 %collective-permute-start.12 = (bf16[512,768]{1,0:T(8,128)(2,1)S(1)}, bf16[512,768]{1,0:T(8,128)(2,1)S(1)}, u32[]{:S(2)}, u32[]{:S(2)}) collective-permute-start(bf16[512,768]{1,0:T(8,128)(2,1)S(1)} %get-tuple-element.102), channel_id=1, source_target_pairs={{0,1},{1,2},{2,3},{3,0},{4,5},{5,6},{6,7},{7,4},{8,9},{9,10},{10,1... | collective-permute-start | bytes 2359304 | tf_op jit(solution)/shard_map/ppermute | solution.py:63
  25.6 27.2 %collective-permute-start.6 = (bf16[128,2048]{1,0:T(8,128)(2,1)S(1)}, bf16[128,2048]{1,0:T(8,128)(2,1)}, u32[]{:S(2)}, u32[]{:S(2)}) collective-permute-start(bf16[128,2048]{1,0:T(8,128)(2,1)S(1)} %copy-done.21), channel_id=1, source_target_pairs={{0,1},{1,2},{2,3},{4,5},{5,6},{6,7},{8,9},{9,10},{10,11},{12,13},{... | collective-permute-start | bytes 1572872 | tf_op jit(solution)/shard_map/ppermute | solution.py:112
  30.1 29.6 %collective-permute-start.9 = (bf16[128,2048]{1,0:T(8,128)(2,1)S(1)}, bf16[128,2048]{1,0:T(8,128)(2,1)}, u32[]{:S(2)}, u32[]{:S(2)}) collective-permute-start(bf16[128,2048]{1,0:T(8,128)(2,1)S(1)} %copy-done.21), channel_id=1, source_target_pairs={{1,0},{2,1},{3,2},{5,4},{6,5},{7,6},{9,8},{10,9},{11,10},{13,12},{... | collective-permute-start | bytes 1572872 | tf_op jit(solution)/shard_map/ppermute | solution.py:112
  31.3 29.8 %collective-permute-start.2 = (bf16[128,2176]{1,0:T(8,128)(2,1)S(1)}, bf16[128,2176]{1,0:T(8,128)(2,1)S(1)}, u32[]{:S(2)}, u32[]{:S(2)}) collective-permute-start(bf16[128,2176]{1,0:T(8,128)(2,1)S(1)} %collective-permute-done.refs_1_.refs_8_), channel_id=1, source_target_pairs={{1,2},{2,3},{5,6},{6,7},{9,10},{10,11},{13,14},{14,15},{17,18},{18... | collective-permute-start | bytes 1671176 | tf_op jit(solution)/shard_map/ppermute | solution.py:112
  32.0 35.5 %collective-permute-start.4 = (bf16[128,2176]{1,0:T(8,128)(2,1)S(1)}, bf16[128,2176]{1,0:T(8,128)(2,1)S(1)}, u32[]{:S(2)}, u32[]{:S(2)}) collective-permute-start(bf16[128,2176]{1,0:T(8,128)(2,1)S(1)} %collective-permute-done.1.refs_4_.refs_11_), channel_id=1, source_target_pairs={{1,0},{2,1},{5,4},{6,5},{9,8},{10,9},{13,12},{14,13},{17,16},{18,1... | collective-permute-start | bytes 1671176 | tf_op jit(solution)/shard_map/ppermute | solution.py:112
  52.8 31.7 %collective-permute-start.14 = (bf16[512,768]{1,0:T(8,128)(2,1)}, bf16[512,768]{1,0:T(8,128)(2,1)}, u32[]{:S(2)}, u32[]{:S(2)}) collective-permute-start(bf16[512,768]{1,0:T(8,128)(2,1)} %get-tuple-element.104), channel_id=1, source_target_pairs={{0,3},{1,0},{2,1},{3,2},{4,7},{5,4},{6,5},{7,6},{8,11},{9,8},{10,9... | collective-permute-start | bytes 2359304 | tf_op jit(solution)/shard_map/ppermute | solution.py:63
  59.7 35.1 %collective-permute-start.7 = (bf16[128,2048]{1,0:T(8,128)(2,1)}, bf16[128,2048]{1,0:T(8,128)(2,1)}, u32[]{:S(2)}, u32[]{:S(2)}) collective-permute-start(bf16[128,2048]{1,0:T(8,128)(2,1)} %collective-permute-done.6.refs_8_), channel_id=1, source_target_pairs={{1,2},{2,3},{5,6},{6,7},{9,10},{10,11},{13,14},{14,15},{17,18},{18... | collective-permute-start | bytes 1572872 | tf_op jit(solution)/shard_map/ppermute | solution.py:112
  61.1 50.2 %collective-permute-start.10 = (bf16[128,2048]{1,0:T(8,128)(2,1)}, bf16[128,2048]{1,0:T(8,128)(2,1)}, u32[]{:S(2)}, u32[]{:S(2)}) collective-permute-start(bf16[128,2048]{1,0:T(8,128)(2,1)} %collective-permute-done.9.refs_11_), channel_id=1, source_target_pairs={{1,0},{2,1},{5,4},{6,5},{9,8},{10,9},{13,12},{14,13},{17,16},{18,1... | collective-permute-start | bytes 1572872 | tf_op jit(solution)/shard_map/ppermute | solution.py:112
  67.5 45.2 %collective-permute-start.3 = (bf16[128,2176]{1,0:T(8,128)(2,1)S(1)}, bf16[128,2176]{1,0:T(8,128)(2,1)S(1)}, u32[]{:S(2)}, u32[]{:S(2)}) collective-permute-start(bf16[128,2176]{1,0:T(8,128)(2,1)S(1)} %collective-permute-done.2.refs_2_.refs_9_), channel_id=1, source_target_pairs={{2,3},{6,7},{10,11},{14,15},{18,19},{22,23},{26,27},{30,31}} | collective-permute-start | bytes 1671176 | tf_op jit(solution)/shard_map/ppermute | solution.py:112
  69.1 46.7 %collective-permute-start.5 = (bf16[128,2176]{1,0:T(8,128)(2,1)S(1)}, bf16[128,2176]{1,0:T(8,128)(2,1)}, u32[]{:S(2)}, u32[]{:S(2)}) collective-permute-start(bf16[128,2176]{1,0:T(8,128)(2,1)S(1)} %collective-permute-done.4.refs_5_.refs_12_), channel_id=1, source_target_pairs={{1,0},{5,4},{9,8},{13,12},{17,16},{21,20},{25,24},{29,28}} | collective-permute-start | bytes 1671176 | tf_op jit(solution)/shard_map/ppermute | solution.py:112
  84.5 41.4 %collective-permute-start.13 = (bf16[256,768]{1,0:T(8,128)(2,1)}, bf16[256,768]{1,0:T(8,128)(2,1)}, u32[]{:S(2)}, u32[]{:S(2)}) collective-permute-start(bf16[256,768]{1,0:T(8,128)(2,1)} %get-tuple-element.103), channel_id=1, source_target_pairs={{0,2},{1,3},{2,0},{3,1},{4,6},{5,7},{6,4},{7,5},{8,10},{9,11},{10,... | collective-permute-start | bytes 1179656 | tf_op jit(solution)/shard_map/ppermute | solution.py:63
  94.8 37.5 %collective-permute-start.15 = (bf16[256,768]{1,0:T(8,128)(2,1)}, bf16[256,768]{1,0:T(8,128)(2,1)}, u32[]{:S(2)}, u32[]{:S(2)}) collective-permute-start(bf16[256,768]{1,0:T(8,128)(2,1)} %get-tuple-element.105), channel_id=1, source_target_pairs={{0,2},{1,3},{2,0},{3,1},{4,6},{5,7},{6,4},{7,5},{8,10},{9,11},{10,... | collective-permute-start | bytes 1179656 | tf_op jit(solution)/shard_map/ppermute | solution.py:63
  112.7 43.6 %collective-permute-start.11 = (bf16[128,2048]{1,0:T(8,128)(2,1)}, bf16[128,2048]{1,0:T(8,128)(2,1)}, u32[]{:S(2)}, u32[]{:S(2)}) collective-permute-start(bf16[128,2048]{1,0:T(8,128)(2,1)} %collective-permute-done.10.refs_12_), channel_id=1, source_target_pairs={{1,0},{5,4},{9,8},{13,12},{17,16},{21,20},{25,24},{29,28}} | collective-permute-start | bytes 1572872 | tf_op jit(solution)/shard_map/ppermute | solution.py:112
  121.1 53.7 %all-to-all-start = ((bf16[8,4,32,2048]{3,2,1,0:T(8,128)(2,1)}), bf16[8,4,32,2048]{3,2,1,0:T(8,128)(2,1)}, u32[]{:S(2)}, u32[]{:S(2)}) async-start(bf16[8,4,32,2048]{3,2,1,0:T(8,128)(2,1)} %shard_map.85), calls=%async_computation | async-start | bytes 8388608 | tf_op jit(solution)/shard_map/all_to_all | solution.py:520
  125.9 36.6 %collective-permute-start.16 = (bf16[512,768]{1,0:T(8,128)(2,1)}, bf16[512,768]{1,0:T(8,128)(2,1)S(1)}, u32[]{:S(2)}, u32[]{:S(2)}) collective-permute-start(bf16[512,768]{1,0:T(8,128)(2,1)} %get-tuple-element.106), channel_id=1, source_target_pairs={{0,1},{1,2},{2,3},{3,0},{4,5},{5,6},{6,7},{7,4},{8,9},{9,10},{10,1... | collective-permute-start | bytes 2359304 | tf_op jit(solution)/shard_map/ppermute | solution.py:63
  132.3 37.1 %collective-permute-start.18 = (bf16[512,768]{1,0:T(8,128)(2,1)}, bf16[512,768]{1,0:T(8,128)(2,1)S(1)}, u32[]{:S(2)}, u32[]{:S(2)}) collective-permute-start(bf16[512,768]{1,0:T(8,128)(2,1)} %get-tuple-element.108), channel_id=1, source_target_pairs={{0,3},{1,0},{2,1},{3,2},{4,7},{5,4},{6,5},{7,6},{8,11},{9,8},{10,9... | collective-permute-start | bytes 2359304 | tf_op jit(solution)/shard_map/ppermute | solution.py:63
  163.7 27.0 %collective-permute-start.17 = (bf16[256,768]{1,0:T(8,128)(2,1)S(1)}, bf16[256,768]{1,0:T(8,128)(2,1)S(1)}, u32[]{:S(2)}, u32[]{:S(2)}) collective-permute-start(bf16[256,768]{1,0:T(8,128)(2,1)S(1)} %copy-done.62), channel_id=1, source_target_pairs={{0,2},{1,3},{2,0},{3,1},{4,6},{5,7},{6,4},{7,5},{8,10},{9,11},{10,... | collective-permute-start | bytes 1179656 | tf_op jit(solution)/shard_map/ppermute | solution.py:63
  170.3 45.5 %collective-permute-start.19 = (bf16[256,768]{1,0:T(8,128)(2,1)S(1)}, bf16[256,768]{1,0:T(8,128)(2,1)S(1)}, u32[]{:S(2)}, u32[]{:S(2)}) collective-permute-start(bf16[256,768]{1,0:T(8,128)(2,1)S(1)} %copy-done.61), channel_id=1, source_target_pairs={{0,2},{1,3},{2,0},{3,1},{4,6},{5,7},{6,4},{7,5},{8,10},{9,11},{10,... | collective-permute-start | bytes 1179656 | tf_op jit(solution)/shard_map/ppermute | solution.py:63
  174.8 54.8 %all-to-all-start.1 = ((bf16[8,4,32,2048]{3,2,1,0:T(8,128)(2,1)}), bf16[8,4,32,2048]{3,2,1,0:T(8,128)(2,1)}, u32[]{:S(2)}, u32[]{:S(2)}) async-start(bf16[8,4,32,2048]{3,2,1,0:T(8,128)(2,1)} %shard_map.95), calls=%async_computation.1 | async-start | bytes 8388608 | tf_op jit(solution)/shard_map/all_to_all | solution.py:520
  191.5 25.2 %collective-permute-start.20 = (bf16[512,768]{1,0:T(8,128)(2,1)}, bf16[512,768]{1,0:T(8,128)(2,1)S(1)}, u32[]{:S(2)}, u32[]{:S(2)}) collective-permute-start(bf16[512,768]{1,0:T(8,128)(2,1)} %get-tuple-element.114), channel_id=1, source_target_pairs={{0,1},{1,2},{2,3},{3,0},{4,5},{5,6},{6,7},{7,4},{8,9},{9,10},{10,1... | collective-permute-start | bytes 2359304 | tf_op jit(solution)/shard_map/ppermute | solution.py:63
  216.6 41.6 %collective-permute-start.22 = (bf16[512,768]{1,0:T(8,128)(2,1)}, bf16[512,768]{1,0:T(8,128)(2,1)}, u32[]{:S(2)}, u32[]{:S(2)}) collective-permute-start(bf16[512,768]{1,0:T(8,128)(2,1)} %get-tuple-element.116), channel_id=1, source_target_pairs={{0,3},{1,0},{2,1},{3,2},{4,7},{5,4},{6,5},{7,6},{8,11},{9,8},{10,9... | collective-permute-start | bytes 2359304 | tf_op jit(solution)/shard_map/ppermute | solution.py:63
  229.6 44.7 %collective-permute-start.21 = (bf16[256,768]{1,0:T(8,128)(2,1)}, bf16[256,768]{1,0:T(8,128)(2,1)}, u32[]{:S(2)}, u32[]{:S(2)}) collective-permute-start(bf16[256,768]{1,0:T(8,128)(2,1)} %get-tuple-element.115), channel_id=1, source_target_pairs={{0,2},{1,3},{2,0},{3,1},{4,6},{5,7},{6,4},{7,5},{8,10},{9,11},{10,... | collective-permute-start | bytes 1179656 | tf_op jit(solution)/shard_map/ppermute | solution.py:63
  276.3 34.6 %collective-permute-start.25 = (bf16[512,768]{1,0:T(8,128)(2,1)}, bf16[512,768]{1,0:T(8,128)(2,1)}, u32[]{:S(2)}, u32[]{:S(2)}) collective-permute-start(bf16[512,768]{1,0:T(8,128)(2,1)} %shard_map.97), channel_id=1, source_target_pairs={{0,1},{1,2},{2,3},{3,0},{4,5},{5,6},{6,7},{7,4},{8,9},{9,10},{10,1... | collective-permute-start | bytes 2359304 | tf_op jit(solution)/shard_map/ppermute | solution.py:63
  294.1 37.9 %collective-permute-start.26 = (bf16[256,768]{1,0:T(8,128)(2,1)}, bf16[256,768]{1,0:T(8,128)(2,1)}, u32[]{:S(2)}, u32[]{:S(2)}) collective-permute-start(bf16[256,768]{1,0:T(8,128)(2,1)} %copy-done.51), channel_id=1, source_target_pairs={{0,2},{1,3},{2,0},{3,1},{4,6},{5,7},{6,4},{7,5},{8,10},{9,11},{10,... | collective-permute-start | bytes 1179656 | tf_op jit(solution)/shard_map/ppermute | solution.py:63
  324.2 53.7 %all-to-all-start.2 = ((bf16[8,4,32,2048]{3,2,1,0:T(8,128)(2,1)}), bf16[8,4,32,2048]{3,2,1,0:T(8,128)(2,1)}, u32[]{:S(2)}, u32[]{:S(2)}) async-start(bf16[8,4,32,2048]{3,2,1,0:T(8,128)(2,1)} %bitcast.15), calls=%async_computation.2 | async-start | bytes 8388608 | tf_op jit(solution)/shard_map/all_to_all | solution.py:520
  332.0 35.4 %collective-permute-start.27 = (bf16[512,768]{1,0:T(8,128)(2,1)}, bf16[512,768]{1,0:T(8,128)(2,1)}, u32[]{:S(2)}, u32[]{:S(2)}) collective-permute-start(bf16[512,768]{1,0:T(8,128)(2,1)} %get-tuple-element.127), channel_id=1, source_target_pairs={{0,3},{1,0},{2,1},{3,2},{4,7},{5,4},{6,5},{7,6},{8,11},{9,8},{10,9... | collective-permute-start | bytes 2359304 | tf_op jit(solution)/shard_map/ppermute | solution.py:63
  351.9 42.3 %collective-permute-start.35 = (bf16[512,768]{1,0:T(8,128)(2,1)}, bf16[512,768]{1,0:T(8,128)(2,1)}, u32[]{:S(2)}, u32[]{:S(2)}) collective-permute-start(bf16[512,768]{1,0:T(8,128)(2,1)} %get-tuple-element.141), channel_id=1, source_target_pairs={{0,1},{1,2},{2,3},{3,0},{4,5},{5,6},{6,7},{7,4},{8,9},{9,10},{10,1... | collective-permute-start | bytes 2359304 | tf_op jit(solution)/shard_map/ppermute | solution.py:63
  398.1 80.7 %all-to-all-start.3 = ((bf16[8,4,32,2048]{3,2,1,0:T(8,128)(2,1)}), bf16[8,4,32,2048]{3,2,1,0:T(8,128)(2,1)}, u32[]{:S(2)}, u32[]{:S(2)}) async-start(bf16[8,4,32,2048]{3,2,1,0:T(8,128)(2,1)} %bitcast.14), calls=%async_computation.3 | async-start | bytes 8388608 | tf_op jit(solution)/shard_map/all_to_all | solution.py:520
  420.9 26.1 %collective-permute-start.29 = (bf16[128,2048]{1,0:T(8,128)(2,1)}, bf16[128,2048]{1,0:T(8,128)(2,1)}, u32[]{:S(2)}, u32[]{:S(2)}) collective-permute-start(bf16[128,2048]{1,0:T(8,128)(2,1)} %get-tuple-element.176), channel_id=1, source_target_pairs={{0,1},{1,2},{4,5},{5,6},{8,9},{9,10},{12,13},{13,14},{16,17},{17,1... | collective-permute-start | bytes 1572872 | tf_op jit(solution)/shard_map/ppermute | solution.py:112
  449.0 27.4 %collective-permute-start.30 = (bf16[128,2048]{1,0:T(8,128)(2,1)}, bf16[128,2048]{1,0:T(8,128)(2,1)}, u32[]{:S(2)}, u32[]{:S(2)}) collective-permute-start(bf16[128,2048]{1,0:T(8,128)(2,1)} %add_convert_fusion.5), channel_id=1, source_target_pairs={{0,1},{1,2},{2,3},{4,5},{5,6},{6,7},{8,9},{9,10},{10,11},{12,13},{... | collective-permute-start | bytes 1572872 | tf_op jit(solution)/shard_map/ppermute | solution.py:112
  453.4 40.1 %collective-permute-start.49 = (bf16[512,768]{1,0:T(8,128)(2,1)}, bf16[512,768]{1,0:T(8,128)(2,1)}, u32[]{:S(2)}, u32[]{:S(2)}) collective-permute-start(bf16[512,768]{1,0:T(8,128)(2,1)} %get-tuple-element.157), channel_id=1, source_target_pairs={{0,1},{1,2},{2,3},{3,0},{4,5},{5,6},{6,7},{7,4},{8,9},{9,10},{10,1... | collective-permute-start | bytes 2359304 | tf_op jit(solution)/shard_map/ppermute | solution.py:63
  512.8 27.3 %collective-permute-start.48 = (bf16[256,768]{1,0:T(8,128)(2,1)S(1)}, bf16[256,768]{1,0:T(8,128)(2,1)}, u32[]{:S(2)}, u32[]{:S(2)}) collective-permute-start(bf16[256,768]{1,0:T(8,128)(2,1)S(1)} %copy-done.55), channel_id=1, source_target_pairs={{0,2},{1,3},{2,0},{3,1},{4,6},{5,7},{6,4},{7,5},{8,10},{9,11},{10,... | collective-permute-start | bytes 1179656 | tf_op jit(solution)/shard_map/ppermute | solution.py:63
  (88 other events, 1298.7 us)
